TPU v7x, 32 devices: a whole 2x2x4 slice. The times are simulated.
32 devices in a mesh: freq: 4 (over z), tm: 2 (over x), bl: 4 (over y, core).
Axes of the slice: x: 2, y: 2, z: 4, core: 2. Of those that a mesh axis runs over, the one named last changes fastest.
Arguments:
- samples: int32 [1024, 128, 2048], P(('freq', 'bl'), 'tm'), may hold values from 0 to 15
- chan_index: int32 [8], replicated, may hold values from 0 to 1023, as said below
Outputs:
- visibilities: float32 [8, 4, 2, 512, 512], P(('freq', 'tm'), 'bl')
Inputs may be any that keep to these rules, and one draw needn't show every extreme that they name: `chan_index`: the entries are distinct.
All inputs are finite; a program needn't handle non-finite values.
Results may differ from a plain program's by a relative error of at most 0.0064.
Values may be sent and summed in bfloat16 or wider, within the bound.
No kernel may reach another device: no remote copies, remote signals or barrier semaphores. Data moves between devices by JAX's collectives and lax.ppermute only.
A program may use at most 192 MiB of HBM per device.

v0:
```python
import math

import jax
import jax.numpy as jnp
from jax import lax
from jax.sharding import PartitionSpec as P

TAPS = 4


def from_behind(block, axis, distance):
    devices = range(lax.axis_size(axis))
    route = [(i - distance, i) for i in devices if i - distance in devices]
    return lax.ppermute(block, axis, route)


def tap_table(frame):
    place = jnp.arange(TAPS * frame, dtype=jnp.float32) + 0.5
    shifted = (place - 2.0 * frame) / frame
    window = 0.5 - 0.5 * jnp.cos(place * (2.0 * math.pi / (TAPS * frame)))
    return (jnp.sinc(shifted) * window).reshape(TAPS, frame)


def dft_table(chan_index, frame):
    steps = jnp.arange(frame, dtype=jnp.int32)
    phase = chan_index[None, :] * steps[:, None] % frame
    angle = phase.astype(jnp.float32) * (2.0 * math.pi / frame)
    scale = 1.0 / math.sqrt(frame)
    both = jnp.stack([jnp.cos(angle) * scale, -jnp.sin(angle) * scale], axis=-1)
    return both.reshape(frame, -1).astype(jnp.bfloat16)


def apply_taps(padded, taps):
    count = padded.shape[1] - (TAPS - 1)
    total = taps[0][None, None, :] * padded[:, 0:count]
    for k in range(1, TAPS):
        total = total + taps[k][None, None, :] * padded[:, k : k + count]
    return total


def corner_turn(spectra_t, groups):
    return lax.all_to_all(
        spectra_t.reshape(groups, -1), ("freq", "tm"), split_axis=0, concat_axis=0, tiled=True
    )


def on_device(samples, chan_index):
    in_dev, fr_dev, frame = samples.shape
    chans = chan_index.shape[0]
    n_freq = lax.axis_size("freq")
    n_tm = lax.axis_size("tm")
    n_bl = lax.axis_size("bl")
    groups = n_freq * n_tm
    chan_dev = chans // groups
    taps = tap_table(frame)
    volts = (samples.astype(jnp.float32) - 7.5) * 0.25
    edge = jnp.zeros((in_dev, TAPS - 1, frame), jnp.float32)
    tail = jnp.concatenate([volts[:, fr_dev - (TAPS - 1) :], edge], axis=1)
    carried = apply_taps(tail, taps)
    received = from_behind(carried, "tm", 1)
    own = apply_taps(jnp.concatenate([edge, volts], axis=1), taps)
    filtered = jnp.concatenate([own[:, : TAPS - 1] + received, own[:, TAPS - 1 :]], axis=1)
    filtered = filtered.astype(jnp.bfloat16).reshape(in_dev * fr_dev, frame)
    table = dft_table(chan_index, frame)
    spectra_t = lax.dot_general(
        table, filtered, (((0,), (1,)), ((), ())), preferred_element_type=jnp.float32
    ).astype(jnp.bfloat16)
    moved = corner_turn(spectra_t, groups)
    moved = moved.reshape(n_freq, n_tm, chan_dev, 2, in_dev, fr_dev)
    moved = jnp.transpose(moved, (2, 3, 0, 4, 1, 5))
    mine = moved.reshape(chan_dev, 2, n_freq, in_dev, n_tm * fr_dev)
    gathered = lax.all_gather(mine[None], "bl", axis=0, tiled=True)
    gathered = jnp.transpose(gathered, (1, 2, 3, 0, 4, 5))
    spectra_all = gathered.reshape(chan_dev, 2, n_freq * n_bl * in_dev, n_tm * fr_dev)
    total_in = spectra_all.shape[2]
    frames_all = spectra_all.shape[3]
    half = total_in // 2
    tile = lax.axis_index("bl")
    row_start = tile // 2 * half
    col_start = tile % 2 * half
    rows = lax.dynamic_slice_in_dim(spectra_all, row_start, half, 2)
    cols = lax.dynamic_slice_in_dim(spectra_all, col_start, half, 2)
    right = jnp.concatenate([cols[:, 0], cols[:, 1]], axis=2)
    left_re = jnp.concatenate([rows[:, 0], rows[:, 1]], axis=2)
    left_im = jnp.concatenate([rows[:, 1], -rows[:, 0]], axis=2)
    left = jnp.stack([left_re, left_im], axis=1)
    product = jnp.einsum("cphf,cqf->cphq", left, right, preferred_element_type=jnp.float32)
    return (product / frames_all)[:, None]


def solution(mesh):
    placed = (P(("freq", "bl"), "tm", None), P())
    return jax.shard_map(
        on_device,
        mesh=mesh,
        in_specs=placed,
        out_specs=P(("freq", "tm"), "bl", None, None, None),
        check_vma=False,
    )
```

profile of v0, /device:TPU:0, one launch (start us, length us, event | category | flops | bytes accessed | tf_op | source)
XLA Modules:
  0.0 184.2 jit_solution(1708876556733184734)
XLA Ops:
  0.0 0.2 fusion.23
  0.2 28.6 %fusion.2 = f32[64,64,2048]{2,0,1:T(8,128)S(1)} fusion(s32[64,64,2048]{2,1,0:T(8,128)} %param.2), kind=kLoop, calls=%fused_computation.6 | loop fusion | flops 25165824 | bytes 67108864 | tf_op jit(solution)/shard_map/mul | solution.py:56
  28.8 0.0 copy-start
  28.8 11.1 %copy-done = f32[64,64,2048]{2,0,1:T(8,128)} copy-done((f32[64,64,2048]{2,0,1:T(8,128)}, f32[64,64,2048]{2,0,1:T(8,128)S(1)}, u32[]{:S(2)}) %copy-start) | copy-done | bytes 33554456
  39.9 0.1 slice.88
  40.0 0.3 fusion.6
  40.3 5.1 %collective-permute-start = (f32[64,3,2048]{2,0,1:T(8,128)S(1)}, f32[64,3,2048]{2,0,1:T(8,128)S(1)}, u32[]{:S(2)}, u32[]{:S(2)}) collective-permute-start(f32[64,3,2048]{2,0,1:T(8,128)S(1)} %fusion.6), channel_id=1, source_target_pairs={{0,4},{1,5},{2,6},{3,7},{8,12},{9,13},{10,14},{11,15},{16,20},{17,... | collective-permute-start | bytes 4718600 | tf_op jit(solution)/shard_map/ppermute | solution.py:14
  45.4 53.8 %multiply_add_fusion = f32[64,64,2048]{2,0,1:T(8,128)} fusion(f32[64,64,2048]{2,0,1:T(8,128)} %copy-done, s32[64,64,2048]{2,1,0:T(8,128)} %param.2, f32[2048]{0:T(1024)S(1)} %get-tuple-element.13, f32[2048]{0:T(1024)S(1)} %get-tuple-element.14, f32[2048]{0:T(1024)S(1)} %get-tuple-element.15, f32[2048]{0:T(1024)S(1)} %get-tuple-element.16), kind=kLoop, calls=%fused_computation.2 | loop fusion | flops 75497472 | bytes 100696064 | tf_op jit(solution)/shard_map/add | solution.py:37
  99.2 0.0 copy-start.1
  99.2 16.9 %slice.117 = bf16[64,61,2048]{2,0,1:T(8,128)(2,1)} slice(f32[64,64,2048]{2,0,1:T(8,128)} %multiply_add_fusion), slice={[0:64], [3:64], [0:2048]} | slice | bytes 31981568 | tf_op jit(solution)/shard_map/slice | solution.py:62
  116.1 0.0 copy-done.1
  116.1 0.3 multiply_convert_fusion.1
  116.5 0.1 copy.21
  116.6 0.0 collective-permute-done
  116.6 1.6 fusion.8
  118.2 8.0 %pad_maximum_fusion = bf16[64,64,2048]{2,0,1:T(8,128)(2,1)S(1)} fusion(bf16[64,61,2048]{2,0,1:T(8,128)(2,1)} %slice.117, bf16[64,3,2048]{2,0,1:T(8,128)(2,1)S(1)} %fusion.8), kind=kLoop, calls=%fused_computation.7 | loop fusion | flops 8388608 | bytes 33554432 | tf_op jit(solution)/shard_map/concatenate | solution.py:62
  126.2 21.9 %copy.23 = bf16[64,64,2048]{2,1,0:T(8,128)(2,1)} copy(bf16[64,64,2048]{2,0,1:T(8,128)(2,1)S(1)} %pad_maximum_fusion) | data formatting | bytes 33554432 | tf_op jit(solution)/shard_map/concatenate | solution.py:62
  148.1 10.2 %convolution_convert_fusion = bf16[16,4096]{1,0:T(8,128)(2,1)S(1)} fusion(bf16[2048,16]{0,1:T(8,128)(2,1)S(1)} %convert_element_type.47, bf16[4096,2048]{1,0:T(8,128)(2,1)} %bitcast.30), kind=kOutput, calls=%fused_computation.8 | convolution fusion | flops 268500992 | bytes 16973824 | tf_op jit(solution)/shard_map/dot_general | solution.py:65
  158.3 0.2 all_to_all.8
  158.6 0.5 broadcast.161
  159.1 1.4 reduce.1
  160.5 0.7 reshape.170
  161.2 4.9 %all-to-all-start = ((bf16[8,2,4096]{2,1,0:T(2,128)(2,1)}), bf16[8,2,4096]{2,1,0:T(2,128)(2,1)S(1)}, u32[]{:S(2)}, u32[]{:S(2)}) async-start(bf16[8,2,4096]{2,1,0:T(2,128)(2,1)} %reshape.170), calls=%async_computation | async-start | bytes 262144 | tf_op jit(solution)/shard_map/all_to_all | solution.py:42
  166.1 7.3 %all-to-all-done = bf16[8,2,4096]{2,1,0:T(2,128)(2,1)S(1)} async-done(((bf16[8,2,4096]{2,1,0:T(2,128)(2,1)}), bf16[8,2,4096]{2,1,0:T(2,128)(2,1)S(1)}, u32[]{:S(2)}, u32[]{:S(2)}) %all-to-all-start) | async-done | bytes 131104 | tf_op jit(solution)/shard_map/all_to_all | solution.py:42
  173.5 0.1 reshape.171
  173.6 0.8 reduce
  174.4 0.2 reshape.164
  174.6 0.3 copy.25
  174.9 0.1 broadcast_in_dim_reshape.3
  175.0 7.2 %all_gather.3 = bf16[4,1,2,4,64,128]{5,4,3,2,1,0:T(8,128)(2,1)S(1)} all-gather(bf16[1,1,2,4,64,128]{5,4,3,2,1,0:T(8,128)(2,1)S(1)} %broadcast_in_dim_reshape.3), channel_id=1, replica_groups=mesh['freq'=4,'tm'=2,'bl'=4] {'bl'}, dimensions={0}, use_global_device_ids=true | all-gather | bytes 655360 | tf_op jit(solution)/shard_map/all_gather | solution.py:72
  182.4 0.1 maximum_bitcast_fusion.2
  182.4 1.8 multiply_bitcast_fusion
  (6 shorter events, 0.2 us)
Async XLA Ops:
  28.8 11.1 %copy-start = (f32[64,64,2048]{2,0,1:T(8,128)}, f32[64,64,2048]{2,0,1:T(8,128)S(1)}, u32[]{:S(2)}) copy-start(f32[64,64,2048]{2,0,1:T(8,128)S(1)} %fusion.2) | copy-start | bytes 100663296
  40.3 76.3 %collective-permute-start = (f32[64,3,2048]{2,0,1:T(8,128)S(1)}, f32[64,3,2048]{2,0,1:T(8,128)S(1)}, u32[]{:S(2)}, u32[]{:S(2)}) collective-permute-start(f32[64,3,2048]{2,0,1:T(8,128)S(1)} %fusion.6), channel_id=1, source_target_pairs={{0,4},{1,5},{2,6},{3,7},{8,12},{9,13},{10,14},{11,15},{16,20},{17,... | collective-permute-start | bytes 4718600 | tf_op jit(solution)/shard_map/ppermute | solution.py:14
  99.2 16.9 %copy-start.1 = (s32[8]{0:T(128)S(1)}, s32[8]{0:T(128)}, u32[]{:S(2)}) copy-start(s32[8]{0:T(128)} %param.3) | copy-start | bytes 100
  161.2 12.2 %all-to-all-start = ((bf16[8,2,4096]{2,1,0:T(2,128)(2,1)}), bf16[8,2,4096]{2,1,0:T(2,128)(2,1)S(1)}, u32[]{:S(2)}, u32[]{:S(2)}) async-start(bf16[8,2,4096]{2,1,0:T(2,128)(2,1)} %reshape.170), calls=%async_computation | async-start | bytes 262144 | tf_op jit(solution)/shard_map/all_to_all | solution.py:42
where the time goes:
time: 185 us; the launch traced here: 184 us
  other arithmetic  95.1 us (51%)
  local copies, waits for them, and re-layouts  52.4 us (28%)
  matrix products  12 us (6%)
  starting transfers between devices  10 us (5%)
  waiting for transfers between devices  7.35 us (4%)
  blocking collectives  7.2 us (4%)
    add x2, other arithmetic, apply_taps(): total = total + taps[k][None, None, :] * padded[:, k:k + count]  54.1 us
    mul x1, other arithmetic, on_device(): volts = (samples.astype(jnp.float32) - 7.5) * 0.25  28.6 us
    concatenate x1, local copies, waits for them, and re-layouts, on_device(): jnp.concatenate([own[:, :TAPS - 1] + received, own[:, TAPS - 1:]], axis=1)  21.9 us
    slice x1, local copies, waits for them, and re-layouts, on_device(): own[:, TAPS - 1:]  16.9 us
    unnamed x6, local copies, waits for them, and re-layouts  11.9 us
    dot_general x1, matrix products, on_device(): lax.dot_general(table, filtered, (((0,), (1,)), ((), ())), preferred_elem...  10.2 us
    concatenate x1, other arithmetic, on_device(): jnp.concatenate([own[:, :TAPS - 1] + received, own[:, TAPS - 1:]], axis=1)  7.99 us
    all_to_all x1, waiting for transfers between devices, corner_turn(): lax.all_to_all(spectra_t.reshape(groups, -1), ('freq', 'tm'), split_axis=...  7.34 us
  transfers between devices with their start and end apart: 2, of which 1 were waited for; matrix products, arithmetic and copies ran while one was open for 39% of the time, Pallas kernels for 0%

commit v1 on v0

v1 whole, which is shorter than its diff:
```python
import functools
import math

import jax
import jax.numpy as jnp
from jax import lax
from jax.experimental import pallas as pl
from jax.experimental.pallas import tpu as pltpu
from jax.sharding import PartitionSpec as P

TAPS = 4
LANES = 128
GROUP = 4


def tap_table(frame):
    place = jnp.arange(TAPS * frame, dtype=jnp.float32) + 0.5
    shifted = (place - 2.0 * frame) / frame
    window = 0.5 - 0.5 * jnp.cos(place * (2.0 * math.pi / (TAPS * frame)))
    return (jnp.sinc(shifted) * window).reshape(TAPS, frame)


def weights(chan_index, frame):
    steps = jnp.arange(frame, dtype=jnp.int32)
    phase = chan_index[:, None] * steps[None, :] % frame
    angle = phase.astype(jnp.float32) * (2.0 * math.pi / frame)
    scale = 1.0 / math.sqrt(frame)
    table = jnp.stack([jnp.cos(angle) * scale, -jnp.sin(angle) * scale])
    table = table.astype(jnp.bfloat16).astype(jnp.float32)
    full = (tap_table(frame)[:, None, None, :] * 0.25 * table[None]).reshape(-1, frame)
    high = full.astype(jnp.bfloat16)
    low = (full - high.astype(jnp.float32)).astype(jnp.bfloat16)
    return jnp.concatenate([high, low], axis=0)


def channelize_kernel(chans, in_dev, fr_dev, w_ref, x_ref, o_ref, spec, carry):
    step = pl.program_id(0)
    frame = x_ref.shape[-1]

    @pl.when(step == 0)
    def _():
        carry[...] = jnp.zeros_like(carry)

    x = (x_ref[...].astype(jnp.float32) - 7.5).astype(jnp.bfloat16).reshape(-1, frame)
    both = lax.dot_general(
        w_ref[...], x, (((1,), (1,)), ((), ())), preferred_element_type=jnp.float32
    )
    half = both.shape[0] // 2
    both = both[:half] + both[half:]
    rows = 2 * chans
    lane = lax.broadcasted_iota(jnp.int32, (rows, LANES), 1)
    place = lane % fr_dev
    first = lax.broadcasted_iota(jnp.int32, (chans, LANES), 1) < fr_dev
    for pair in range(GROUP // 2):
        part = both[:, pair * LANES : (pair + 1) * LANES]
        own = part[(TAPS - 1) * rows :]
        over = jnp.zeros_like(own)
        for k in range(TAPS - 1):
            late = TAPS - 1 - k
            moved = pltpu.roll(part[k * rows : (k + 1) * rows], late, 1)
            own = own + jnp.where(place >= late, moved, 0.0)
            over = over + jnp.where(place < late, moved, 0.0)
        re, im = own[:chans], own[chans:]
        even = jnp.where(first, re, pltpu.roll(im, fr_dev, 1))
        odd = jnp.where(first, pltpu.roll(re, fr_dev, 1), im)
        i = step * GROUP + pair * 2
        spec[pl.ds(i, chans, stride=in_dev), :] = even
        spec[pl.ds(i + 1, chans, stride=in_dev), :] = odd
        shift = (step * (GROUP // 2) + pair) * TAPS
        from_even = jnp.where(lane >= fr_dev, over, 0.0)
        from_odd = jnp.where(lane < fr_dev, over, 0.0)
        carry[0] += pltpu.roll(from_even, (shift + fr_dev) % LANES, 1)
        carry[1] += pltpu.roll(from_odd, shift, 1)

    @pl.when(step == pl.num_programs(0) - 1)
    def _():
        extra = o_ref.shape[1] - in_dev - 4
        for c in range(chans):
            block = [spec[c * in_dev : (c + 1) * in_dev]]
            for p in range(2):
                for odd_one in range(2):
                    block.append(carry[odd_one, p * chans + c : p * chans + c + 1])
            if extra:
                block.append(jnp.zeros((extra, LANES), jnp.float32))
            o_ref[c] = jnp.concatenate(block, axis=0).astype(jnp.bfloat16)


def channelize(samples, table):
    in_dev, fr_dev, frame = samples.shape
    chans = table.shape[0] // (2 * TAPS * 2)
    rows = (in_dev + 4 + 15) // 16 * 16
    return pl.pallas_call(
        functools.partial(channelize_kernel, chans, in_dev, fr_dev),
        grid=(in_dev // GROUP,),
        in_specs=[
            pl.BlockSpec(table.shape, lambda i: (0, 0)),
            pl.BlockSpec((GROUP, fr_dev, frame), lambda i: (i, 0, 0)),
        ],
        out_specs=pl.BlockSpec((chans, rows, LANES), lambda i: (0, 0, 0)),
        out_shape=jax.ShapeDtypeStruct((chans, rows, LANES), jnp.bfloat16),
        scratch_shapes=[
            pltpu.VMEM((chans * in_dev, LANES), jnp.float32),
            pltpu.VMEM((2, 2 * chans, LANES), jnp.float32),
        ],
        compiler_params=pltpu.CompilerParams(vmem_limit_bytes=40 * 2**20),
        name="channelize",
    )(table, samples)


def carry_maps(in_dev, fr_dev):
    mine = lax.broadcasted_iota(jnp.int32, (in_dev, LANES), 0)
    lane = lax.broadcasted_iota(jnp.int32, (in_dev, LANES), 1)
    mask = (lane // TAPS == mine // 2)
    odd = mine % 2 == 1
    src = lax.broadcasted_iota(jnp.int32, (2 * LANES, LANES), 0)
    dst = lax.broadcasted_iota(jnp.int32, (2 * LANES, LANES), 1)
    place = (src // LANES) * fr_dev + src % TAPS
    spread = jnp.where((place == dst) & (src % TAPS < TAPS - 1), 1.0, 0.0).astype(jnp.bfloat16)
    return mask, odd, spread


def with_carry(block, carried, maps):
    mask, odd, spread = maps
    picked = []
    for p in range(2):
        row = jnp.where(odd, carried[2 * p + 1][None], carried[2 * p][None])
        picked.append(jnp.where(mask, row, 0.0).astype(jnp.bfloat16))
    moved = jnp.dot(
        jnp.concatenate(picked, axis=1), spread, preferred_element_type=jnp.float32
    )
    return (block.astype(jnp.float32) + moved).astype(jnp.bfloat16)


def correlate_kernel(n_freq, n_tm, in_dev, fr_dev, scale, where_ref, g_ref, o_ref, left, right):
    n_bl = g_ref.shape[0]
    step = pl.program_id(0)
    per_half = n_freq // 2 * n_bl

    @pl.when(step == 0)
    def _():
        maps = carry_maps(in_dev, fr_dev)
        for out, side in ((left, 0), (right, 1)):
            base = where_ref[side] * (n_freq // 2)
            for m in range(per_half):
                f, b = base + m // n_bl, m % n_bl
                for t in range(n_tm):
                    block = g_ref[b, f * n_tm + t, :in_dev, :]
                    if t:
                        carried = g_ref[b, f * n_tm + t - 1, in_dev : in_dev + 4, :]
                        block = with_carry(block, carried.astype(jnp.float32), maps)
                    out[m * in_dev : (m + 1) * in_dev, t * LANES : (t + 1) * LANES] = block

    rows = o_ref.shape[3]
    mine = left[pl.ds(pl.multiple_of(step * rows, rows), rows), :]
    lane = lax.broadcasted_iota(jnp.int32, (rows, LANES), 1)
    turned = []
    for t in range(n_tm):
        part = mine[:, t * LANES : (t + 1) * LANES].astype(jnp.float32)
        part = pltpu.roll(part, fr_dev, 1)
        turned.append(jnp.where(lane < fr_dev, part, -part).astype(jnp.bfloat16))
    dims = (((1,), (1,)), ((), ()))
    for p, a in enumerate((mine, jnp.concatenate(turned, axis=1))):
        o_ref[0, 0, p] = scale * lax.dot_general(
            a, right[...], dims, preferred_element_type=jnp.float32
        )


def correlate(gathered, where, n_freq, n_tm, in_dev, fr_dev):
    n_bl = gathered.shape[0]
    half = n_freq * n_bl * in_dev // 2
    rows = half // 4
    scale = 1.0 / (n_tm * fr_dev)
    return pl.pallas_call(
        functools.partial(correlate_kernel, n_freq, n_tm, in_dev, fr_dev, scale),
        grid_spec=pltpu.PrefetchScalarGridSpec(
            num_scalar_prefetch=1,
            grid=(half // rows,),
            in_specs=[pl.BlockSpec(gathered.shape, lambda i, w: (0, 0, 0, 0))],
            out_specs=pl.BlockSpec((1, 1, 2, rows, half), lambda i, w: (0, 0, 0, i, 0)),
            scratch_shapes=[pltpu.VMEM((half, n_tm * LANES), jnp.bfloat16)] * 2,
        ),
        out_shape=jax.ShapeDtypeStruct((1, 1, 2, half, half), jnp.float32),
        compiler_params=pltpu.CompilerParams(vmem_limit_bytes=40 * 2**20),
        name="correlate",
    )(where, gathered)


def correlate_plain(gathered, where, n_freq, n_tm, in_dev, fr_dev):
    n_bl = gathered.shape[0]
    half = n_freq * n_bl * in_dev // 2
    blocks = gathered.reshape(n_bl, n_freq, n_tm, -1, LANES)
    blocks = jnp.transpose(blocks, (1, 0, 2, 3, 4)).astype(jnp.float32)
    main = blocks[:, :, :, :in_dev].reshape(n_freq, n_bl, n_tm, in_dev, 2, fr_dev)
    over = blocks[:, :, :-1, in_dev : in_dev + 4, : in_dev // 2 * TAPS]
    over = over.reshape(n_freq, n_bl, n_tm - 1, 2, 2, in_dev // 2, TAPS)
    over = jnp.transpose(over, (0, 1, 2, 5, 4, 3, 6))
    over = over.reshape(n_freq, n_bl, n_tm - 1, in_dev, 2, TAPS)[..., : TAPS - 1]
    over = jnp.pad(over, [(0, 0)] * 2 + [(1, 0)] + [(0, 0)] * 2 + [(0, fr_dev - TAPS + 1)])
    whole = (main + over).astype(jnp.bfloat16)
    whole = jnp.transpose(whole, (4, 0, 1, 3, 2, 5)).reshape(2, 2 * half, n_tm * fr_dev)
    rows = lax.dynamic_slice_in_dim(whole, where[0] * half, half, 1)
    cols = lax.dynamic_slice_in_dim(whole, where[1] * half, half, 1)
    right = jnp.concatenate([cols[0], cols[1]], axis=1)
    left = jnp.stack(
        [jnp.concatenate([rows[0], rows[1]], 1), jnp.concatenate([rows[1], -rows[0]], 1)]
    )
    product = jnp.einsum("phf,qf->phq", left, right, preferred_element_type=jnp.float32)
    return (product / (n_tm * fr_dev))[None, None]


def on_device(samples, chan_index):
    in_dev, fr_dev, frame = samples.shape
    n_freq = lax.axis_size("freq")
    n_tm = lax.axis_size("tm")
    table = weights(chan_index, frame)
    spectra = channelize(samples, table)
    moved = lax.all_to_all(spectra, ("freq", "tm"), split_axis=0, concat_axis=0, tiled=True)
    gathered = lax.all_gather(moved, "bl", axis=0, tiled=False)
    tile = lax.axis_index("bl")
    where = jnp.stack([tile // 2, tile % 2]).astype(jnp.int32)
    form = correlate if in_dev % 16 == 0 else correlate_plain
    return form(gathered, where, n_freq, n_tm, in_dev, fr_dev)


def solution(mesh):
    placed = (P(("freq", "bl"), "tm", None), P())
    return jax.shard_map(
        on_device,
        mesh=mesh,
        in_specs=placed,
        out_specs=P(("freq", "tm"), "bl", None, None, None),
        check_vma=False,
    )
```

time: 185 us -> 48.4 us (0.26)
  other arithmetic: 95.1 us -> 1.55 us
  local copies, waits for them, and re-layouts: 52.4 us -> 0 us
  Pallas kernels: 0 us -> 23.8 us
  matrix products: 12 us -> 0 us
  starting transfers between devices: 10 us -> 7.25 us
    add x2 -> x0, other arithmetic: 54.1 us -> none  [apply_taps(): total = total + taps[k][None, None, :] * padded[:, k:k + count]]
    mul x3 -> x2, other arithmetic: 28.8 us -> 0.37 us  [weights(): tap_table(frame)[:, None, None, :] * 0.25 * table[None]]
    pallas_call x0 -> x2, Pallas kernels: none -> 23.8 us  [the longest x1 20.3 us: channelize(): pl.pallas_call(functools.partial(channelize_kernel, chans, in_dev, fr_dev...]
    concatenate x1 -> x0, local copies, waits for them, and re-layouts: 21.9 us -> none  [on_device(): jnp.concatenate([own[:, :TAPS - 1] + received, own[:, TAPS - 1:]], axis=1)]
    slice x2 -> x0, local copies, waits for them, and re-layouts: 17 us -> none  [the longest x1 16.9 us: on_device(): own[:, TAPS - 1:]]
    dot_general x2 -> x0, matrix products: 12 us -> none  [the longest x1 10.2 us: on_device(): lax.dot_general(table, filtered, (((0,), (1,)), ((), ())), preferred_elem...]
    unnamed x6 -> x0, local copies, waits for them, and re-layouts: 11.9 us -> none
    concatenate x1, other arithmetic: 7.99 us -> 0.04 us  [weights(): return jnp.concatenate([high, low], axis=0)]
  transfers between devices with their start and end apart: 2 -> 1, of which waited for: 1 -> 1; matrix products, arithmetic and copies ran while one was open for 39% -> 0% of each run, Pallas kernels for 0% -> 0%
where the time goes in v1:
time: 48.4 us; the launch traced here: 48 us
  Pallas kernels  23.8 us (49%)
  blocking collectives  7.9 us (16%)
  waiting for transfers between devices  7.49 us (15%)
  starting transfers between devices  7.25 us (15%)
  other arithmetic  1.55 us (3%)
    pallas_call x1, Pallas kernels, channelize(): pl.pallas_call(functools.partial(channelize_kernel, chans, in_dev, fr_dev...  20.3 us
    all_gather x1, blocking collectives, on_device(): gathered = lax.all_gather(moved, 'bl', axis=0, tiled=False)  7.9 us
    all_to_all x1, waiting for transfers between devices, on_device(): lax.all_to_all(spectra, ('freq', 'tm'), split_axis=0, concat_axis=0, tile...  7.49 us
    all_to_all x1, starting transfers between devices, on_device(): lax.all_to_all(spectra, ('freq', 'tm'), split_axis=0, concat_axis=0, tile...  7.25 us
    pallas_call x1, Pallas kernels, correlate(): pl.pallas_call(functools.partial(correlate_kernel, n_freq, n_tm, in_dev,...  3.43 us
    another operation x1, other arithmetic  1 us
  transfers between devices with their start and end apart: 1, of which 1 were waited for; matrix products, arithmetic and copies ran while one was open for 0% of the time, Pallas kernels for 0%

profile of v1, /device:TPU:0, one launch (start us, length us, event | category | flops | bytes accessed | tf_op | source)
XLA Modules:
  0.0 48.0 jit_solution(10750567297368814044)
XLA Ops:
  0.0 0.3 fusion.13
  0.3 1.0 %multiply_convert_fusion.1 = (bf16[1,8,2048]{2,1,0:T(8,128)(2,1)S(1)}, bf16[1,8,2048]{2,1,0:T(8,128)(2,1)S(1)}) fusion(s32[8]{0:T(128)} %param.3), kind=kLoop, calls=%fused_computation.13 | loop fusion | flops 311296 | bytes 65568 | tf_op jit(solution)/shard_map/convert
  1.5 20.3 %channelize.1 = bf16[8,80,128]{2,1,0:T(8,128)(2,1)} custom-call(bf16[128,2048]{1,0:T(8,128)(2,1)S(1)} %pad_maximum_fusion.w_ref, s32[64,64,2048]{2,1,0:T(8,128)} %x_ref.1), custom_call_target="tpu_custom_call" | custom-call | tf_op jit(solution)/shard_map/channelize/pallas_call | solution.py:92
  21.9 7.3 %all-to-all-start = ((bf16[8,80,128]{2,1,0:T(8,128)(2,1)}), bf16[8,80,128]{2,1,0:T(8,128)(2,1)S(1)}, u32[]{:S(2)}, u32[]{:S(2)}) async-start(bf16[8,80,128]{2,1,0:T(8,128)(2,1)} %channelize.1), calls=%async_computation | async-start | bytes 327680 | tf_op jit(solution)/shard_map/all_to_all | solution.py:217
  29.1 0.1 pad_add_fusion.where_ref
  29.2 7.5 %all-to-all-done = bf16[8,80,128]{2,1,0:T(8,128)(2,1)S(1)} async-done(((bf16[8,80,128]{2,1,0:T(8,128)(2,1)}), bf16[8,80,128]{2,1,0:T(8,128)(2,1)S(1)}, u32[]{:S(2)}, u32[]{:S(2)}) %all-to-all-start) | async-done | bytes 163872 | tf_op jit(solution)/shard_map/all_to_all | solution.py:217
  36.7 7.9 %all-gather = bf16[32,80,128]{2,1,0:T(8,128)(2,1)S(1)} all-gather(bf16[8,80,128]{2,1,0:T(8,128)(2,1)S(1)} %all-to-all-done), channel_id=2, replica_groups=mesh['freq'=4,'tm'=2,'bl'=4] {'bl'}, dimensions={0}, use_global_device_ids=true | all-gather | bytes 819200 | tf_op jit(solution)/shard_map/all_gather | solution.py:218
  44.6 3.4 %correlate.1 = f32[1,1,2,512,512]{4,3,2,1,0:T(8,128)} custom-call(s32[2]{0:T(128)S(1)} %pad_add_fusion.where_ref, bf16[4,8,80,128]{3,2,1,0:T(8,128)(2,1)S(1)} %bitcast.9), custom_call_target="tpu_custom_call" | custom-call | tf_op jit(solution)/shard_map/correlate/pallas_call | solution.py:173
  (4 shorter events, 0.1 us)
Async XLA Ops:
  21.9 14.8 %all-to-all-start = ((bf16[8,80,128]{2,1,0:T(8,128)(2,1)}), bf16[8,80,128]{2,1,0:T(8,128)(2,1)S(1)}, u32[]{:S(2)}, u32[]{:S(2)}) async-start(bf16[8,80,128]{2,1,0:T(8,128)(2,1)} %channelize.1), calls=%async_computation | async-start | bytes 327680 | tf_op jit(solution)/shard_map/all_to_all | solution.py:217

commit v2 on v0

v2 whole, which is shorter than its diff:
```python
import functools
import math

import jax
import jax.numpy as jnp
from jax import lax
from jax.experimental import pallas as pl
from jax.experimental.pallas import tpu as pltpu
from jax.sharding import PartitionSpec as P

TAPS = 4
LANES = 128
GROUP = 4
PARTS = 4


def bin_column(chan_ref, chans):
    row = lax.broadcasted_iota(jnp.int32, (chans, LANES), 0)
    out = jnp.zeros((chans, LANES), jnp.int32)
    for c in range(chans):
        out = jnp.where(row == c, chan_ref[c], out)
    return out[:, :1]


def build_weights(chan_ref, w_ref, chans):
    frame = w_ref.shape[1]
    half = w_ref.shape[0] // 2
    bins = bin_column(chan_ref, chans)
    steps = lax.broadcasted_iota(jnp.int32, (chans, frame), 1)
    angle = (bins * steps % frame).astype(jnp.float32) * (2.0 * math.pi / frame)
    scale = 1.0 / math.sqrt(frame)
    table = jnp.concatenate([jnp.cos(angle) * scale, -jnp.sin(angle) * scale], axis=0)
    table = table.astype(jnp.bfloat16).astype(jnp.float32) * 0.25
    tap = lax.broadcasted_iota(jnp.int32, (8, frame), 0) % TAPS
    place = lax.broadcasted_iota(jnp.int32, (8, frame), 1) + tap * frame
    place = place.astype(jnp.float32) + 0.5
    turn = math.pi * ((place - 2.0 * frame) / frame)
    window = 0.5 - 0.5 * jnp.cos(place * (2.0 * math.pi / (TAPS * frame)))
    taps = jnp.sin(turn) / turn * window
    rows = 2 * chans
    for k in range(TAPS):
        full = taps[k : k + 1] * table
        high = full.astype(jnp.bfloat16)
        low = (full - high.astype(jnp.float32)).astype(jnp.bfloat16)
        w_ref[k * rows : (k + 1) * rows] = high
        w_ref[half + k * rows : half + (k + 1) * rows] = low


def shift_and_add(chans, in_dev, fr_dev, pair, raw, spec, carry):
    rows = 2 * chans
    lane = lax.broadcasted_iota(jnp.int32, (rows, LANES), 1)
    place = lane % fr_dev
    first = lax.broadcasted_iota(jnp.int32, (chans, LANES), 1) < fr_dev
    span = slice(pair * LANES, (pair + 1) * LANES)
    own = raw[(TAPS - 1) * rows :, span]
    over = jnp.zeros_like(own)
    for k in range(TAPS - 1):
        late = TAPS - 1 - k
        moved = pltpu.roll(raw[k * rows : (k + 1) * rows, span], late, 1)
        own = own + jnp.where(place >= late, moved, 0.0)
        over = over + jnp.where(place < late, moved, 0.0)
    re, im = own[:chans], own[chans:]
    even = jnp.where(first, re, pltpu.roll(im, fr_dev, 1))
    odd = jnp.where(first, pltpu.roll(re, fr_dev, 1), im)
    spec[pl.ds(pair * 2, chans, stride=in_dev), :] = even
    spec[pl.ds(pair * 2 + 1, chans, stride=in_dev), :] = odd
    shift = pair * TAPS
    from_even = jnp.where(lane >= fr_dev, over, 0.0)
    from_odd = jnp.where(lane < fr_dev, over, 0.0)
    carry[0] += pltpu.roll(from_even, (shift + fr_dev) % LANES, 1)
    carry[1] += pltpu.roll(from_odd, shift, 1) if shift else from_odd


def channelize_kernel(chans, chan_ref, x_ref, o_ref, buf, w_ref, raw, spec, carry, sems):
    in_dev, fr_dev, frame = x_ref.shape
    count = in_dev // GROUP

    def fetch(g):
        span = pl.ds(g * GROUP, GROUP)
        return pltpu.make_async_copy(x_ref.at[span], buf.at[span], sems.at[g])

    for g in range(count):
        fetch(g).start()
    build_weights(chan_ref, w_ref, chans)
    carry[...] = jnp.zeros_like(carry)
    width = GROUP * fr_dev

    def multiply(g, _):
        fetch(g).wait()
        x = buf[pl.ds(g * GROUP, GROUP)].astype(jnp.float32) - 7.5
        x = x.astype(jnp.bfloat16).reshape(width, frame)
        both = lax.dot_general(
            w_ref[...], x, (((1,), (1,)), ((), ())), preferred_element_type=jnp.float32
        )
        half = both.shape[0] // 2
        at = pl.ds(pl.multiple_of(g * width, width), width)
        raw[:, at] = both[:half] + both[half:]
        return 0

    parts = min(PARTS, count)
    pairs = in_dev // 2 // parts
    for part in range(parts):
        lax.fori_loop(part * count // parts, (part + 1) * count // parts, multiply, 0)
        for pair in range(part * pairs, (part + 1) * pairs):
            shift_and_add(chans, in_dev, fr_dev, pair, raw, spec, carry)
    extra = o_ref.shape[1] - in_dev - 4
    for c in range(chans):
        block = [spec[c * in_dev : (c + 1) * in_dev]]
        for p in range(2):
            for odd in range(2):
                block.append(carry[odd, p * chans + c : p * chans + c + 1])
        if extra:
            block.append(jnp.zeros((extra, LANES), jnp.float32))
        o_ref[c] = jnp.concatenate(block, axis=0).astype(jnp.bfloat16)


def channelize(samples, chan_index):
    in_dev, fr_dev, frame = samples.shape
    chans = chan_index.shape[0]
    rows = (in_dev + 4 + 15) // 16 * 16
    products = TAPS * 2 * chans
    return pl.pallas_call(
        functools.partial(channelize_kernel, chans),
        in_specs=[
            pl.BlockSpec(memory_space=pltpu.SMEM),
            pl.BlockSpec(memory_space=pl.ANY),
        ],
        out_specs=pl.BlockSpec(memory_space=pltpu.VMEM),
        out_shape=jax.ShapeDtypeStruct((chans, rows, LANES), jnp.bfloat16),
        scratch_shapes=[
            pltpu.VMEM(samples.shape, jnp.int32),
            pltpu.VMEM((2 * products, frame), jnp.bfloat16),
            pltpu.VMEM((products, in_dev * fr_dev), jnp.float32),
            pltpu.VMEM((chans * in_dev, LANES), jnp.float32),
            pltpu.VMEM((2, 2 * chans, LANES), jnp.float32),
            pltpu.SemaphoreType.DMA((in_dev // GROUP,)),
        ],
        compiler_params=pltpu.CompilerParams(vmem_limit_bytes=48 * 2**20),
        name="channelize",
    )(chan_index, samples)


def place_carry(carried, in_dev, fr_dev):
    mine = lax.broadcasted_iota(jnp.int32, (in_dev, LANES), 0)
    lane = lax.broadcasted_iota(jnp.int32, (in_dev, LANES), 1)
    mask = lane // TAPS == mine // 2
    odd = mine % 2 == 1
    src = lax.broadcasted_iota(jnp.int32, (2 * LANES, LANES), 0)
    dst = lax.broadcasted_iota(jnp.int32, (2 * LANES, LANES), 1)
    place = (src // LANES) * fr_dev + src % TAPS
    spread = jnp.where((place == dst) & (src % TAPS < TAPS - 1), 1.0, 0.0).astype(jnp.bfloat16)
    picked = []
    for four in carried:
        both = []
        for p in range(2):
            row = jnp.where(odd, four[2 * p + 1][None], four[2 * p][None])
            both.append(jnp.where(mask, row, 0.0).astype(jnp.bfloat16))
        picked.append(jnp.concatenate(both, axis=1))
    return jnp.dot(
        jnp.concatenate(picked, axis=0), spread, preferred_element_type=jnp.float32
    )


def correlate_kernel(n_freq, n_tm, in_dev, fr_dev, where_ref, *refs):
    sources, (o_ref, left, right, result, sems) = refs[:4], refs[4:]
    n_bl = len(sources)
    me = where_ref[0]
    scale = 1.0 / (n_tm * fr_dev)
    order = [(f, k) for f in range(n_freq // 2) for k in range(n_bl)]
    for out, base in ((left, me // 2 * (n_freq // 2)), (right, me % 2 * (n_freq // 2))):
        for t in range(n_tm):
            blocks = [sources[k][(base + f) * n_tm + t, :in_dev, :] for f, k in order]
            if t:
                carried = [
                    sources[k][(base + f) * n_tm + t - 1, in_dev : in_dev + 4, :].astype(jnp.float32)
                    for f, k in order
                ]
                moved = place_carry(carried, in_dev, fr_dev)
                whole = jnp.concatenate(blocks, axis=0).astype(jnp.float32) + moved
                whole = whole.astype(jnp.bfloat16)
                blocks = [whole[m * in_dev : (m + 1) * in_dev] for m in range(len(order))]
            for (f, k), block in zip(order, blocks):
                at = pl.multiple_of((f * n_bl + (me ^ k)) * in_dev, in_dev)
                out[pl.ds(at, in_dev), t * LANES : (t + 1) * LANES] = block
    half = left.shape[0]
    rows = half // sems.shape[0]
    lane = lax.broadcasted_iota(jnp.int32, (rows, LANES), 1)
    dims = (((1,), (1,)), ((), ()))
    copies = []
    for m in range(sems.shape[0]):
        span = pl.ds(m * rows, rows)
        mine = left[m * rows : (m + 1) * rows, :]
        turned = []
        for t in range(n_tm):
            part = mine[:, t * LANES : (t + 1) * LANES].astype(jnp.float32)
            part = pltpu.roll(part, fr_dev, 1)
            turned.append(jnp.where(lane < fr_dev, part, -part).astype(jnp.bfloat16))
        for p, a in enumerate((mine, jnp.concatenate(turned, axis=1))):
            result[p, m * rows : (m + 1) * rows, :] = scale * lax.dot_general(
                a, right[...], dims, preferred_element_type=jnp.float32
            )
        copies.append(
            pltpu.make_async_copy(
                result.at[:, span], o_ref.at[0, 0, :, span], sems.at[m]
            )
        )
        copies[-1].start()
    for copy in copies:
        copy.wait()


def correlate(sources, me, n_freq, n_tm, in_dev, fr_dev):
    half = n_freq * len(sources) * in_dev // 2
    return pl.pallas_call(
        functools.partial(correlate_kernel, n_freq, n_tm, in_dev, fr_dev),
        in_specs=[pl.BlockSpec(memory_space=pltpu.SMEM)]
        + [pl.BlockSpec(memory_space=pltpu.VMEM)] * len(sources),
        out_specs=pl.BlockSpec(memory_space=pl.ANY),
        out_shape=jax.ShapeDtypeStruct((1, 1, 2, half, half), jnp.float32),
        scratch_shapes=[
            pltpu.VMEM((half, n_tm * LANES), jnp.bfloat16),
            pltpu.VMEM((half, n_tm * LANES), jnp.bfloat16),
            pltpu.VMEM((2, half, half), jnp.float32),
            pltpu.SemaphoreType.DMA((4,)),
        ],
        compiler_params=pltpu.CompilerParams(vmem_limit_bytes=16 * 2**20),
        name="correlate",
    )(me, *sources)


def correlate_plain(gathered, where, n_freq, n_tm, in_dev, fr_dev):
    n_bl = gathered.shape[0]
    half = n_freq * n_bl * in_dev // 2
    blocks = gathered.reshape(n_bl, n_freq, n_tm, -1, LANES)
    blocks = jnp.transpose(blocks, (1, 0, 2, 3, 4)).astype(jnp.float32)
    main = blocks[:, :, :, :in_dev].reshape(n_freq, n_bl, n_tm, in_dev, 2, fr_dev)
    over = blocks[:, :, :-1, in_dev : in_dev + 4, : in_dev // 2 * TAPS]
    over = over.reshape(n_freq, n_bl, n_tm - 1, 2, 2, in_dev // 2, TAPS)
    over = jnp.transpose(over, (0, 1, 2, 5, 4, 3, 6))
    over = over.reshape(n_freq, n_bl, n_tm - 1, in_dev, 2, TAPS)[..., : TAPS - 1]
    over = jnp.pad(over, [(0, 0)] * 2 + [(1, 0)] + [(0, 0)] * 2 + [(0, fr_dev - TAPS + 1)])
    whole = (main + over).astype(jnp.bfloat16)
    whole = jnp.transpose(whole, (4, 0, 1, 3, 2, 5)).reshape(2, 2 * half, n_tm * fr_dev)
    rows = lax.dynamic_slice_in_dim(whole, where[0] * half, half, 1)
    cols = lax.dynamic_slice_in_dim(whole, where[1] * half, half, 1)
    right = jnp.concatenate([cols[0], cols[1]], axis=1)
    left = jnp.stack(
        [jnp.concatenate([rows[0], rows[1]], 1), jnp.concatenate([rows[1], -rows[0]], 1)]
    )
    product = jnp.einsum("phf,qf->phq", left, right, preferred_element_type=jnp.float32)
    return (product / (n_tm * fr_dev))[None, None]


def swapped(block, axis, distance):
    count = lax.axis_size(axis)
    return lax.ppermute(block, axis, [(i, i ^ distance) for i in range(count)])


def on_device(samples, chan_index):
    in_dev, fr_dev, frame = samples.shape
    n_freq = lax.axis_size("freq")
    n_tm = lax.axis_size("tm")
    spectra = channelize(samples, chan_index)
    moved = lax.all_to_all(spectra, ("freq", "tm"), split_axis=0, concat_axis=0, tiled=True)
    tile = lax.axis_index("bl")
    if in_dev % 16 == 0:
        far = swapped(moved, "bl", 2)
        near = swapped(moved, "bl", 1)
        sources = (moved, near, far, swapped(far, "bl", 1))
        return correlate(sources, tile.reshape(1), n_freq, n_tm, in_dev, fr_dev)
    gathered = lax.all_gather(moved, "bl", axis=0, tiled=False)
    where = jnp.stack([tile // 2, tile % 2]).astype(jnp.int32)
    return correlate_plain(gathered, where, n_freq, n_tm, in_dev, fr_dev)


def solution(mesh):
    placed = (P(("freq", "bl"), "tm", None), P())
    return jax.shard_map(
        on_device,
        mesh=mesh,
        in_specs=placed,
        out_specs=P(("freq", "tm"), "bl", None, None, None),
        check_vma=False,
    )
```

time: 185 us -> 36.2 us (0.20)
  other arithmetic: 95.1 us -> 0 us
  local copies, waits for them, and re-layouts: 52.4 us -> 0.65 us
  Pallas kernels: 0 us -> 14 us
  matrix products: 12 us -> 0 us
  starting transfers between devices: 10 us -> 1.52 us
  blocking collectives: 7.2 us -> 14.6 us
  waiting for transfers between devices: 7.35 us -> 5.19 us
    add x2 -> x0, other arithmetic: 54.1 us -> none  [apply_taps(): total = total + taps[k][None, None, :] * padded[:, k:k + count]]
    mul x3 -> x0, other arithmetic: 28.8 us -> none  [the longest x1 28.6 us: on_device(): volts = (samples.astype(jnp.float32) - 7.5) * 0.25]
    concatenate x1 -> x0, local copies, waits for them, and re-layouts: 21.9 us -> none  [on_device(): jnp.concatenate([own[:, :TAPS - 1] + received, own[:, TAPS - 1:]], axis=1)]
    slice x2 -> x0, local copies, waits for them, and re-layouts: 17 us -> none  [the longest x1 16.9 us: on_device(): own[:, TAPS - 1:]]
    all_to_all x0 -> x1, blocking collectives: none -> 14.6 us  [on_device(): lax.all_to_all(spectra, ('freq', 'tm'), split_axis=0, concat_axis=0, tile...]
    pallas_call x0 -> x2, Pallas kernels: none -> 14 us  [the longest x1 12.1 us: channelize(): pl.pallas_call(functools.partial(channelize_kernel, chans), in_specs=[pl....]
    dot_general x2 -> x0, matrix products: 12 us -> none  [the longest x1 10.2 us: on_device(): lax.dot_general(table, filtered, (((0,), (1,)), ((), ())), preferred_elem...]
    unnamed x6 -> x2, local copies, waits for them, and re-layouts: 11.9 us -> 0.65 us
  transfers between devices with their start and end apart: 2 -> 3, of which waited for: 1 -> 2; matrix products, arithmetic and copies ran while one was open for 39% -> 0% of each run, Pallas kernels for 0% -> 0%
where the time goes in v2:
time: 36.2 us; the launch traced here: 36 us
  blocking collectives  14.6 us (40%)
  Pallas kernels  14 us (39%)
  waiting for transfers between devices  5.19 us (14%)
  starting transfers between devices  1.52 us (4%)
  local copies, waits for them, and re-layouts  0.65 us (2%)
    all_to_all x1, blocking collectives, on_device(): lax.all_to_all(spectra, ('freq', 'tm'), split_axis=0, concat_axis=0, tile...  14.6 us
    pallas_call x1, Pallas kernels, channelize(): pl.pallas_call(functools.partial(channelize_kernel, chans), in_specs=[pl....  12.1 us
    ppermute x3, waiting for transfers between devices, swapped(): return lax.ppermute(block, axis, [(i, i ^ distance) for i in range(count)])  5.19 us
    pallas_call x1, Pallas kernels, correlate(): pl.pallas_call(functools.partial(correlate_kernel, n_freq, n_tm, in_dev,...  1.99 us
    ppermute x3, starting transfers between devices, swapped(): return lax.ppermute(block, axis, [(i, i ^ distance) for i in range(count)])  1.52 us
  transfers between devices with their start and end apart: 3, of which 2 were waited for; matrix products, arithmetic and copies ran while one was open for 0% of the time, Pallas kernels for 0%

profile of v2, /device:TPU:0, one launch (start us, length us, event | category | flops | bytes accessed | tf_op | source)
XLA Modules:
  0.0 36.0 jit_solution(6649990830555314386)
XLA Ops:
  0.0 0.0 copy-start
  0.0 0.7 %copy-done = s32[8]{0:T(128)S(1)} copy-done((s32[8]{0:T(128)S(1)}, s32[8]{0:T(128)}, u32[]{:S(2)}) %copy-start) | copy-done | bytes 56
  0.7 12.1 %channelize.1 = bf16[8,80,128]{2,1,0:T(8,128)(2,1)S(1)} custom-call(s32[8]{0:T(128)S(1)} %copy-done, s32[64,64,2048]{2,1,0:T(8,128)} %x_ref.1), custom_call_target="tpu_custom_call" | custom-call | tf_op jit(solution)/shard_map/channelize/pallas_call | solution.py:122
  12.7 14.6 %all_to_all.5.refs_0_ = bf16[8,80,128]{2,1,0:T(8,128)(2,1)S(1)} all-to-all(bf16[8,80,128]{2,1,0:T(8,128)(2,1)S(1)} %channelize.1), channel_id=1, replica_groups=mesh['freq'=4,'tm'=2,'bl'=4] {'freq','tm'}, dimensions={0} | all-to-all | bytes 327680 | tf_op jit(solution)/shard_map/all_to_all | solution.py:264
  27.3 1.5 %collective-permute-start.1 = (bf16[8,80,128]{2,1,0:T(8,128)(2,1)S(1)}, bf16[8,80,128]{2,1,0:T(8,128)(2,1)S(1)}, u32[]{:S(2)}, u32[]{:S(2)}) collective-permute-start(bf16[8,80,128]{2,1,0:T(8,128)(2,1)S(1)} %all_to_all.5.refs_0_), channel_id=1, source_target_pairs={{0,2},{1,3},{2,0},{3,1},{4,6},{5,7},{6,4},{7,5},{8,10},{9,11},{10,... | collective-permute-start | bytes 491528 | tf_op jit(solution)/shard_map/ppermute | solution.py:256
  28.9 0.0 collective-permute-start
  28.9 3.8 %collective-permute-done.1.refs_2_ = bf16[8,80,128]{2,1,0:T(8,128)(2,1)S(1)} collective-permute-done((bf16[8,80,128]{2,1,0:T(8,128)(2,1)S(1)}, bf16[8,80,128]{2,1,0:T(8,128)(2,1)S(1)}, u32[]{:S(2)}, u32[]{:S(2)}) %collective-permute-start.1) | collective-permute-done | bytes 163872 | tf_op jit(solution)/shard_map/ppermute | solution.py:256
  32.7 0.0 collective-permute-start.2
  32.7 0.0 collective-permute-done.refs_1_
  32.7 1.4 %collective-permute-done.2.refs_3_ = bf16[8,80,128]{2,1,0:T(8,128)(2,1)S(1)} collective-permute-done((bf16[8,80,128]{2,1,0:T(8,128)(2,1)S(1)}, bf16[8,80,128]{2,1,0:T(8,128)(2,1)S(1)}, u32[]{:S(2)}, u32[]{:S(2)}) %collective-permute-start.2) | collective-permute-done | bytes 163872 | tf_op jit(solution)/shard_map/ppermute | solution.py:256
  34.1 2.0 %correlate.1 = f32[1,1,2,512,512]{4,3,2,1,0:T(8,128)} custom-call(s32[1]{0:T(128)} %bitcast.where_ref, bf16[8,80,128]{2,1,0:T(8,128)(2,1)S(1)} %all_to_all.5.refs_0_, bf16[8,80,128]{2,1,0:T(8,128)(2,1)S(1)} %collective-permute-done.refs_1_, bf16[8,80,128]{2,1,0:T(8,128)(2,1)S(1)} %collective-permute-done.1.refs_2_, ...), custom_call_target="tpu_custom_call" | custom-call | tf_op jit(solution)/shard_map/correlate/pallas_call | solution.py:214
Async XLA Ops:
  0.0 0.7 %copy-start = (s32[8]{0:T(128)S(1)}, s32[8]{0:T(128)}, u32[]{:S(2)}) copy-start(s32[8]{0:T(128)} %chan_ref.1) | copy-start | bytes 100
  27.3 5.3 %collective-permute-start.1 = (bf16[8,80,128]{2,1,0:T(8,128)(2,1)S(1)}, bf16[8,80,128]{2,1,0:T(8,128)(2,1)S(1)}, u32[]{:S(2)}, u32[]{:S(2)}) collective-permute-start(bf16[8,80,128]{2,1,0:T(8,128)(2,1)S(1)} %all_to_all.5.refs_0_), channel_id=1, source_target_pairs={{0,2},{1,3},{2,0},{3,1},{4,6},{5,7},{6,4},{7,5},{8,10},{9,11},{10,... | collective-permute-start | bytes 491528 | tf_op jit(solution)/shard_map/ppermute | solution.py:256
  28.9 3.8 %collective-permute-start = (bf16[8,80,128]{2,1,0:T(8,128)(2,1)S(1)}, bf16[8,80,128]{2,1,0:T(8,128)(2,1)S(1)}, u32[]{:S(2)}, u32[]{:S(2)}) collective-permute-start(bf16[8,80,128]{2,1,0:T(8,128)(2,1)S(1)} %all_to_all.5.refs_0_), channel_id=1, source_target_pairs={{0,1},{1,0},{2,3},{3,2},{4,5},{5,4},{6,7},{7,6},{8,9},{9,8},{10,11... | collective-permute-start | bytes 491528 | tf_op jit(solution)/shard_map/ppermute | solution.py:256
  32.7 1.4 %collective-permute-start.2 = (bf16[8,80,128]{2,1,0:T(8,128)(2,1)S(1)}, bf16[8,80,128]{2,1,0:T(8,128)(2,1)S(1)}, u32[]{:S(2)}, u32[]{:S(2)}) collective-permute-start(bf16[8,80,128]{2,1,0:T(8,128)(2,1)S(1)} %collective-permute-done.1.refs_2_), channel_id=1, source_target_pairs={{0,1},{1,0},{2,3},{3,2},{4,5},{5,4},{6,7},{7,6},{8,9},{9,8},{10,11... | collective-permute-start | bytes 491528 | tf_op jit(solution)/shard_map/ppermute | solution.py:256

commit v3 on v2

--- a/solution.py
+++ b/solution.py
@@ -11,7 +11,6 @@
 TAPS = 4
 LANES = 128
 GROUP = 4
-PARTS = 4
 
 
 def bin_column(chan_ref, chans):
@@ -71,73 +70,119 @@
     carry[1] += pltpu.roll(from_odd, shift, 1) if shift else from_odd
 
 
-def channelize_kernel(chans, chan_ref, x_ref, o_ref, buf, w_ref, raw, spec, carry, sems):
+def channelize_kernel(chans, relative, mesh_shape, me_ref, chan_hbm, x_ref, *refs):
+    outs, refs = refs[: -9], refs[-9:]
+    buf, w_ref, raw, spec, carry, edge, chan_ref, sems, chan_sem = refs
     in_dev, fr_dev, frame = x_ref.shape
-    count = in_dev // GROUP
-
-    def fetch(g):
-        span = pl.ds(g * GROUP, GROUP)
-        return pltpu.make_async_copy(x_ref.at[span], buf.at[span], sems.at[g])
-
-    for g in range(count):
-        fetch(g).start()
+    n_freq, n_tm, n_bl = mesh_shape
+    groups = [(i, GROUP) for i in range(0, in_dev - 2 * GROUP, GROUP)]
+    tail = len(groups) * GROUP
+    groups += [(i, 2) for i in range(tail, in_dev, 2)]
+
+    def fetch(first, count, sem):
+        span = pl.ds(first, count)
+        return pltpu.make_async_copy(x_ref.at[span], buf.at[span], sems.at[sem])
+
+    chan_copy = pltpu.make_async_copy(chan_hbm, chan_ref, chan_sem)
+    chan_copy.start()
+    for g, (first, count) in enumerate(groups):
+        fetch(first, count, g).start()
+    chan_copy.wait()
     build_weights(chan_ref, w_ref, chans)
     carry[...] = jnp.zeros_like(carry)
-    width = GROUP * fr_dev
-
-    def multiply(g, _):
-        fetch(g).wait()
-        x = buf[pl.ds(g * GROUP, GROUP)].astype(jnp.float32) - 7.5
-        x = x.astype(jnp.bfloat16).reshape(width, frame)
+
+    def multiply(first, count, sem):
+        fetch(first, count, sem).wait()
+        x = buf[pl.ds(first, count)].astype(jnp.float32) - 7.5
+        x = x.astype(jnp.bfloat16).reshape(count * fr_dev, frame)
         both = lax.dot_general(
             w_ref[...], x, (((1,), (1,)), ((), ())), preferred_element_type=jnp.float32
         )
         half = both.shape[0] // 2
-        at = pl.ds(pl.multiple_of(g * width, width), width)
-        raw[:, at] = both[:half] + both[half:]
+        at = first * fr_dev
+        if not isinstance(first, int):
+            at = pl.multiple_of(at, GROUP * fr_dev)
+        raw[:, pl.ds(at, count * fr_dev)] = both[:half] + both[half:]
+
+    def step(g, _):
+        multiply(g * GROUP, GROUP, g)
         return 0
 
-    parts = min(PARTS, count)
-    pairs = in_dev // 2 // parts
-    for part in range(parts):
-        lax.fori_loop(part * count // parts, (part + 1) * count // parts, multiply, 0)
-        for pair in range(part * pairs, (part + 1) * pairs):
+    def slot(m):
+        if not relative:
+            return m
+        freq, tm = me_ref[0] // (n_tm * n_bl), me_ref[0] // n_bl % n_tm
+        return (freq ^ (m // n_tm)) * n_tm + (tm ^ (m % n_tm))
+
+    def emit(first, count):
+        for m in range(chans):
+            at = slot(m) * in_dev + first
+            if relative:
+                at = pl.multiple_of(at, 8)
+            per = chans // len(outs)
+            block = spec[pl.ds(at, count), :].astype(jnp.bfloat16)
+            outs[m // per][m % per, first : first + count, :] = block
+
+    done = 0
+    while done < tail:
+        upto = min(done + 4 * GROUP, tail)
+        lax.fori_loop(done // GROUP, upto // GROUP, step, 0)
+        for pair in range(done // 2, upto // 2):
             shift_and_add(chans, in_dev, fr_dev, pair, raw, spec, carry)
-    extra = o_ref.shape[1] - in_dev - 4
-    for c in range(chans):
-        block = [spec[c * in_dev : (c + 1) * in_dev]]
-        for p in range(2):
-            for odd in range(2):
-                block.append(carry[odd, p * chans + c : p * chans + c + 1])
-        if extra:
-            block.append(jnp.zeros((extra, LANES), jnp.float32))
-        o_ref[c] = jnp.concatenate(block, axis=0).astype(jnp.bfloat16)
-
-
-def channelize(samples, chan_index):
+        done = upto
+    early = tail // 16 * 16
+    if early:
+        emit(0, early)
+    for g, (first, count) in enumerate(groups):
+        if first >= tail:
+            multiply(first, count, g)
+            shift_and_add(chans, in_dev, fr_dev, first // 2, raw, spec, carry)
+    emit(early, in_dev - early)
+    edge[...] = jnp.zeros_like(edge)
+    for p in range(2):
+        for odd in range(2):
+            rows = carry[odd, p * chans : (p + 1) * chans, :]
+            edge[pl.ds(2 * p + odd, chans, stride=8), :] = rows
+    for m in range(chans):
+        per = chans // len(outs)
+        at = slot(m) * 8
+        if relative:
+            at = pl.multiple_of(at, 8)
+        count = outs[0].shape[1] - in_dev
+        block = edge[pl.ds(at, count), :].astype(jnp.bfloat16)
+        outs[m // per][m % per, in_dev:, :] = block
+
+
+def channelize(samples, chan_index, me, relative, mesh_shape):
     in_dev, fr_dev, frame = samples.shape
     chans = chan_index.shape[0]
-    rows = (in_dev + 4 + 15) // 16 * 16
+    rows = (in_dev + 4 + 7) // 8 * 8
     products = TAPS * 2 * chans
+    parts = mesh_shape[0] if relative else 1
+    out = jax.ShapeDtypeStruct((chans // parts, rows, LANES), jnp.bfloat16)
     return pl.pallas_call(
-        functools.partial(channelize_kernel, chans),
+        functools.partial(channelize_kernel, chans, relative, mesh_shape),
         in_specs=[
             pl.BlockSpec(memory_space=pltpu.SMEM),
-            pl.BlockSpec(memory_space=pl.ANY),
+            pl.BlockSpec(memory_space=pltpu.HBM),
+            pl.BlockSpec(memory_space=pltpu.HBM),
         ],
-        out_specs=pl.BlockSpec(memory_space=pltpu.VMEM),
-        out_shape=jax.ShapeDtypeStruct((chans, rows, LANES), jnp.bfloat16),
+        out_specs=[pl.BlockSpec(memory_space=pltpu.VMEM)] * parts,
+        out_shape=[out] * parts,
         scratch_shapes=[
             pltpu.VMEM(samples.shape, jnp.int32),
             pltpu.VMEM((2 * products, frame), jnp.bfloat16),
             pltpu.VMEM((products, in_dev * fr_dev), jnp.float32),
             pltpu.VMEM((chans * in_dev, LANES), jnp.float32),
             pltpu.VMEM((2, 2 * chans, LANES), jnp.float32),
-            pltpu.SemaphoreType.DMA((in_dev // GROUP,)),
+            pltpu.VMEM((chans * 8, LANES), jnp.float32),
+            pltpu.SMEM((chans,), jnp.int32),
+            pltpu.SemaphoreType.DMA((in_dev // 2,)),
+            pltpu.SemaphoreType.DMA,
         ],
         compiler_params=pltpu.CompilerParams(vmem_limit_bytes=48 * 2**20),
         name="channelize",
-    )(chan_index, samples)
+    )(me, chan_index, samples)
 
 
 def place_carry(carried, in_dev, fr_dev):
@@ -161,27 +206,30 @@
     )
 
 
-def correlate_kernel(n_freq, n_tm, in_dev, fr_dev, where_ref, *refs):
-    sources, (o_ref, left, right, result, sems) = refs[:4], refs[4:]
-    n_bl = len(sources)
-    me = where_ref[0]
+def correlate_kernel(mesh_shape, in_dev, fr_dev, me_ref, *refs):
+    n_freq, n_tm, n_bl = mesh_shape
+    own_half, other_half = refs[:n_bl], refs[n_bl : 2 * n_bl]
+    o_ref, left, right, result, sems = refs[2 * n_bl :]
+    me = me_ref[0]
+    freq, tm, bl = me // (n_tm * n_bl), me // n_bl % n_tm, me % n_bl
     scale = 1.0 / (n_tm * fr_dev)
     order = [(f, k) for f in range(n_freq // 2) for k in range(n_bl)]
-    for out, base in ((left, me // 2 * (n_freq // 2)), (right, me % 2 * (n_freq // 2))):
-        for t in range(n_tm):
-            blocks = [sources[k][(base + f) * n_tm + t, :in_dev, :] for f, k in order]
-            if t:
-                carried = [
-                    sources[k][(base + f) * n_tm + t - 1, in_dev : in_dev + 4, :].astype(jnp.float32)
-                    for f, k in order
-                ]
-                moved = place_carry(carried, in_dev, fr_dev)
-                whole = jnp.concatenate(blocks, axis=0).astype(jnp.float32) + moved
-                whole = whole.astype(jnp.bfloat16)
-                blocks = [whole[m * in_dev : (m + 1) * in_dev] for m in range(len(order))]
-            for (f, k), block in zip(order, blocks):
-                at = pl.multiple_of((f * n_bl + (me ^ k)) * in_dev, in_dev)
-                out[pl.ds(at, in_dev), t * LANES : (t + 1) * LANES] = block
+    for out, base in ((left, bl // 2 * (n_freq // 2)), (right, bl % 2 * (n_freq // 2))):
+        early, late, carried = [], [], []
+        for f, k in order:
+            at = (base + f) ^ freq
+            mine, other = own_half[k], other_half[k]
+            body, over = slice(0, in_dev), slice(in_dev, in_dev + 4)
+            early.append(jnp.where(tm == 0, mine[at, body, :], other[at, body, :]))
+            late.append(jnp.where(tm == 0, other[at, body, :], mine[at, body, :]))
+            four = jnp.where(tm == 0, mine[at, over, :], other[at, over, :])
+            carried.append(four.astype(jnp.float32))
+        late = jnp.concatenate(late, axis=0).astype(jnp.float32)
+        late = (late + place_carry(carried, in_dev, fr_dev)).astype(jnp.bfloat16)
+        for m, (f, k) in enumerate(order):
+            at = pl.multiple_of((f * n_bl + (bl ^ k)) * in_dev, in_dev)
+            out[pl.ds(at, in_dev), :LANES] = early[m]
+            out[pl.ds(at, in_dev), LANES:] = late[m * in_dev : (m + 1) * in_dev]
     half = left.shape[0]
     rows = half // sems.shape[0]
     lane = lax.broadcasted_iota(jnp.int32, (rows, LANES), 1)
@@ -209,10 +257,11 @@
         copy.wait()
 
 
-def correlate(sources, me, n_freq, n_tm, in_dev, fr_dev):
-    half = n_freq * len(sources) * in_dev // 2
+def correlate(sources, me, mesh_shape, in_dev, fr_dev):
+    n_freq, n_tm, n_bl = mesh_shape
+    half = n_freq * n_bl * in_dev // 2
     return pl.pallas_call(
-        functools.partial(correlate_kernel, n_freq, n_tm, in_dev, fr_dev),
+        functools.partial(correlate_kernel, mesh_shape, in_dev, fr_dev),
         in_specs=[pl.BlockSpec(memory_space=pltpu.SMEM)]
         + [pl.BlockSpec(memory_space=pltpu.VMEM)] * len(sources),
         out_specs=pl.BlockSpec(memory_space=pl.ANY),
@@ -251,24 +300,42 @@
     return (product / (n_tm * fr_dev))[None, None]
 
 
-def swapped(block, axis, distance):
-    count = lax.axis_size(axis)
-    return lax.ppermute(block, axis, [(i, i ^ distance) for i in range(count)])
+def swapped(block, axes, distance):
+    count = math.prod(lax.axis_size(axis) for axis in axes)
+    return lax.ppermute(block, axes, [(i, i ^ distance) for i in range(count)])
+
+
+def exchange(parts, n_bl):
+    arrived = [parts[0]] + [None] * (len(parts) - 1)
+    for k in reversed(range(1, len(parts))):
+        arrived[k] = swapped(parts[k], ("freq",), k)
+    keep = jnp.stack([block[0] for block in arrived])
+    send = jnp.stack([block[1] for block in arrived])
+    across = ("tm", "bl")
+    corner = swapped(send, across, n_bl + 2)
+    beside = swapped(send, across, n_bl)
+    far = swapped(keep, across, 2)
+    own_half, other_half = [keep, None, far, None], [beside, None, corner, None]
+    for half in (own_half, other_half):
+        for k in (0, 2):
+            half[k + 1] = swapped(half[k], ("bl",), 1)
+    return own_half + other_half
 
 
 def on_device(samples, chan_index):
     in_dev, fr_dev, frame = samples.shape
-    n_freq = lax.axis_size("freq")
-    n_tm = lax.axis_size("tm")
-    spectra = channelize(samples, chan_index)
-    moved = lax.all_to_all(spectra, ("freq", "tm"), split_axis=0, concat_axis=0, tiled=True)
+    axes = ("freq", "tm", "bl")
+    mesh_shape = tuple(lax.axis_size(axis) for axis in axes)
+    n_freq, n_tm, n_bl = mesh_shape
+    me = lax.axis_index(axes).reshape(1)
+    relative = in_dev % 16 == 0 and n_freq <= 4 and n_tm == 2 and n_bl == 4
+    spectra = channelize(samples, chan_index, me, relative, mesh_shape)
+    if relative:
+        sources = exchange(spectra, n_bl)
+        return correlate(sources, me, mesh_shape, in_dev, fr_dev)
+    moved = lax.all_to_all(spectra[0], ("freq", "tm"), split_axis=0, concat_axis=0, tiled=True)
+    gathered = lax.all_gather(moved, "bl", axis=0, tiled=False)
     tile = lax.axis_index("bl")
-    if in_dev % 16 == 0:
-        far = swapped(moved, "bl", 2)
-        near = swapped(moved, "bl", 1)
-        sources = (moved, near, far, swapped(far, "bl", 1))
-        return correlate(sources, tile.reshape(1), n_freq, n_tm, in_dev, fr_dev)
-    gathered = lax.all_gather(moved, "bl", axis=0, tiled=False)
     where = jnp.stack([tile // 2, tile % 2]).astype(jnp.int32)
     return correlate_plain(gathered, where, n_freq, n_tm, in_dev, fr_dev)
 

time: 36.2 us -> 35.7 us (0.986)
  blocking collectives: 14.6 us -> 0 us
  starting transfers between devices: 1.52 us -> 9.31 us
  waiting for transfers between devices: 5.19 us -> 10.8 us
  Pallas kernels: 14 us -> 14.7 us
    all_to_all x1 -> x0, blocking collectives: 14.6 us -> none  [on_device(): lax.all_to_all(spectra, ('freq', 'tm'), split_axis=0, concat_axis=0, tile...]
    ppermute x3 -> x10, starting transfers between devices: 1.52 us -> 9.31 us  [swapped(): return lax.ppermute(block, axes, [(i, i ^ distance) for i in range(count)])]
    ppermute x3 -> x10, waiting for transfers between devices: 5.19 us -> 10.8 us  [swapped(): return lax.ppermute(block, axes, [(i, i ^ distance) for i in range(count)])]
    pallas_call x2, Pallas kernels: 14 us -> 14.7 us  [the longest x1 12.7 us: channelize(): pl.pallas_call(functools.partial(channelize_kernel, chans, relative, mesh...]
  transfers between devices with their start and end apart: 3 -> 10, of which waited for: 2 -> 7; matrix products, arithmetic and copies ran while one was open for 0% -> 0% of each run, Pallas kernels for 0% -> 0%
where the time goes in v3:
time: 35.7 us; the launch traced here: 35.5 us
  Pallas kernels  14.7 us (41%)
  waiting for transfers between devices  10.8 us (30%)
  starting transfers between devices  9.31 us (26%)
  local copies, waits for them, and re-layouts  0.67 us (2%)
    pallas_call x1, Pallas kernels, channelize(): pl.pallas_call(functools.partial(channelize_kernel, chans, relative, mesh...  12.7 us
    ppermute x10, waiting for transfers between devices, swapped(): return lax.ppermute(block, axes, [(i, i ^ distance) for i in range(count)])  10.8 us
    ppermute x10, starting transfers between devices, swapped(): return lax.ppermute(block, axes, [(i, i ^ distance) for i in range(count)])  9.31 us
    pallas_call x1, Pallas kernels, correlate(): pl.pallas_call(functools.partial(correlate_kernel, mesh_shape, in_dev, fr...  2.01 us
  transfers between devices with their start and end apart: 10, of which 7 were waited for; matrix products, arithmetic and copies ran while one was open for 0% of the time, Pallas kernels for 0%

profile of v3, /device:TPU:0, one launch (start us, length us, event | category | flops | bytes accessed | tf_op | source)
XLA Modules:
  0.0 35.5 jit_solution(17736348027850288903)
XLA Ops:
  0.0 0.0 copy-start
  0.0 0.7 %copy-done = s32[8]{0:T(128)S(1)} copy-done((s32[8]{0:T(128)S(1)}, s32[8]{0:T(128)}, u32[]{:S(2)}) %copy-start) | copy-done | bytes 56
  0.7 12.7 %channelize.1 = (bf16[2,72,128]{2,1,0:T(8,128)(2,1)S(1)}, bf16[2,72,128]{2,1,0:T(8,128)(2,1)S(1)}, bf16[2,72,128]{2,1,0:T(8,128)(2,1)S(1)}, bf16[2,72,128]{2,1,0:T(8,128)(2,1)S(1)}) custom-call(s32[1]{0:T(128)} %bitcast.me_ref, s32[8]{0:T(128)S(1)} %copy-done, s32[64,64,2048]{2,1,0:T(8,128)} %x_ref.1), custom_call_target="tpu_custom_call" | custom-call | tf_op jit(solution)/shard_map/channelize/pallas_call | solution.py:163
  13.4 3.1 %collective-permute-start = (bf16[2,72,128]{2,1,0:T(8,128)(2,1)S(1)}, bf16[2,72,128]{2,1,0:T(8,128)(2,1)S(1)}, u32[]{:S(2)}, u32[]{:S(2)}) collective-permute-start(bf16[2,72,128]{2,1,0:T(8,128)(2,1)S(1)} %get-tuple-element.10), channel_id=1, source_target_pairs={{0,8},{8,0},{16,24},{24,16},{1,9},{9,1},{17,25},{25,17},{2,10},{10... | collective-permute-start | bytes 110600 | tf_op jit(solution)/shard_map/ppermute | solution.py:305
  16.4 2.6 %collective-permute-start.1 = (bf16[2,72,128]{2,1,0:T(8,128)(2,1)S(1)}, bf16[2,72,128]{2,1,0:T(8,128)(2,1)S(1)}, u32[]{:S(2)}, u32[]{:S(2)}) collective-permute-start(bf16[2,72,128]{2,1,0:T(8,128)(2,1)S(1)} %get-tuple-element.11), channel_id=1, source_target_pairs={{0,16},{8,24},{16,0},{24,8},{1,17},{9,25},{17,1},{25,9},{2,18},{10... | collective-permute-start | bytes 110600 | tf_op jit(solution)/shard_map/ppermute | solution.py:305
  19.0 0.0 collective-permute-start.2
  19.0 0.0 collective-permute-done
  19.1 2.9 %collective-permute-done.1 = bf16[2,72,128]{2,1,0:T(8,128)(2,1)S(1)} collective-permute-done((bf16[2,72,128]{2,1,0:T(8,128)(2,1)S(1)}, bf16[2,72,128]{2,1,0:T(8,128)(2,1)S(1)}, u32[]{:S(2)}, u32[]{:S(2)}) %collective-permute-start.1) | collective-permute-done | bytes 36896 | tf_op jit(solution)/shard_map/ppermute | solution.py:305
  22.0 2.8 %collective-permute-done.2 = bf16[2,72,128]{2,1,0:T(8,128)(2,1)S(1)} collective-permute-done((bf16[2,72,128]{2,1,0:T(8,128)(2,1)S(1)}, bf16[2,72,128]{2,1,0:T(8,128)(2,1)S(1)}, u32[]{:S(2)}, u32[]{:S(2)}) %collective-permute-start.2) | collective-permute-done | bytes 36896 | tf_op jit(solution)/shard_map/ppermute | solution.py:305
  24.8 1.6 %collective-permute-start.4 = (bf16[4,72,128]{2,1,0:T(8,128)(2,1)S(1)}, bf16[4,72,128]{2,1,0:T(8,128)(2,1)S(1)}, u32[]{:S(2)}, u32[]{:S(2)}) collective-permute-start(bf16[4,72,128]{2,1,0:T(8,128)(2,1)S(1)} %pad_maximum_fusion.refs_0_), channel_id=1, source_target_pairs={{0,2},{1,3},{2,0},{3,1},{4,6},{5,7},{6,4},{7,5},{8,10},{9,11},{10,... | collective-permute-start | bytes 221192 | tf_op jit(solution)/shard_map/ppermute | solution.py:305
  26.4 1.5 %collective-permute-start.8 = (bf16[4,72,128]{2,1,0:T(8,128)(2,1)S(1)}, bf16[4,72,128]{2,1,0:T(8,128)(2,1)S(1)}, u32[]{:S(2)}, u32[]{:S(2)}) collective-permute-start(bf16[4,72,128]{2,1,0:T(8,128)(2,1)S(1)} %pad_maximum_fusion.1), channel_id=1, source_target_pairs={{0,6},{1,7},{2,4},{3,5},{4,2},{5,3},{6,0},{7,1},{8,14},{9,15},{10,... | collective-permute-start | bytes 221192 | tf_op jit(solution)/shard_map/ppermute | solution.py:305
  27.9 0.5 %collective-permute-start.6 = (bf16[4,72,128]{2,1,0:T(8,128)(2,1)S(1)}, bf16[4,72,128]{2,1,0:T(8,128)(2,1)S(1)}, u32[]{:S(2)}, u32[]{:S(2)}) collective-permute-start(bf16[4,72,128]{2,1,0:T(8,128)(2,1)S(1)} %pad_maximum_fusion.1), channel_id=1, source_target_pairs={{0,4},{1,5},{2,6},{3,7},{4,0},{5,1},{6,2},{7,3},{8,12},{9,13},{10,... | collective-permute-start | bytes 221192 | tf_op jit(solution)/shard_map/ppermute | solution.py:305
  28.4 0.0 collective-permute-start.3
  28.5 1.0 %collective-permute-done.4.refs_2_ = bf16[4,72,128]{2,1,0:T(8,128)(2,1)S(1)} collective-permute-done((bf16[4,72,128]{2,1,0:T(8,128)(2,1)S(1)}, bf16[4,72,128]{2,1,0:T(8,128)(2,1)S(1)}, u32[]{:S(2)}, u32[]{:S(2)}) %collective-permute-start.4) | collective-permute-done | bytes 73760 | tf_op jit(solution)/shard_map/ppermute | solution.py:305
  29.5 0.0 collective-permute-start.5
  29.5 2.2 %collective-permute-done.8.refs_6_ = bf16[4,72,128]{2,1,0:T(8,128)(2,1)S(1)} collective-permute-done((bf16[4,72,128]{2,1,0:T(8,128)(2,1)S(1)}, bf16[4,72,128]{2,1,0:T(8,128)(2,1)S(1)}, u32[]{:S(2)}, u32[]{:S(2)}) %collective-permute-start.8) | collective-permute-done | bytes 73760 | tf_op jit(solution)/shard_map/ppermute | solution.py:305
  31.7 0.0 collective-permute-start.9
  31.7 0.5 %collective-permute-done.6.refs_4_ = bf16[4,72,128]{2,1,0:T(8,128)(2,1)S(1)} collective-permute-done((bf16[4,72,128]{2,1,0:T(8,128)(2,1)S(1)}, bf16[4,72,128]{2,1,0:T(8,128)(2,1)S(1)}, u32[]{:S(2)}, u32[]{:S(2)}) %collective-permute-start.6) | collective-permute-done | bytes 73760 | tf_op jit(solution)/shard_map/ppermute | solution.py:305
  32.3 0.0 collective-permute-start.7
  32.3 0.0 collective-permute-done.3.refs_1_
  32.3 0.0 collective-permute-done.5.refs_3_
  32.3 0.7 %collective-permute-done.9.refs_7_ = bf16[4,72,128]{2,1,0:T(8,128)(2,1)S(1)} collective-permute-done((bf16[4,72,128]{2,1,0:T(8,128)(2,1)S(1)}, bf16[4,72,128]{2,1,0:T(8,128)(2,1)S(1)}, u32[]{:S(2)}, u32[]{:S(2)}) %collective-permute-start.9) | collective-permute-done | bytes 73760 | tf_op jit(solution)/shard_map/ppermute | solution.py:305
  33.0 0.5 %collective-permute-done.7.refs_5_ = bf16[4,72,128]{2,1,0:T(8,128)(2,1)S(1)} collective-permute-done((bf16[4,72,128]{2,1,0:T(8,128)(2,1)S(1)}, bf16[4,72,128]{2,1,0:T(8,128)(2,1)S(1)}, u32[]{:S(2)}, u32[]{:S(2)}) %collective-permute-start.7) | collective-permute-done | bytes 73760 | tf_op jit(solution)/shard_map/ppermute | solution.py:305
  33.5 2.0 %correlate.1 = f32[1,1,2,512,512]{4,3,2,1,0:T(8,128)} custom-call(s32[1]{0:T(128)} %bitcast.me_ref, bf16[4,72,128]{2,1,0:T(8,128)(2,1)S(1)} %pad_maximum_fusion.refs_0_, bf16[4,72,128]{2,1,0:T(8,128)(2,1)S(1)} %collective-permute-done.3.refs_1_, bf16[4,72,128]{2,1,0:T(8,128)(2,1)S(1)} %collective-permute-done.4.refs_2_, ...), custom_call_target="tpu_custom_call" | custom-call | tf_op jit(solution)/shard_map/correlate/pallas_call | solution.py:263
  (6 shorter events, 0.0 us)
Async XLA Ops:
  0.0 0.7 %copy-start = (s32[8]{0:T(128)S(1)}, s32[8]{0:T(128)}, u32[]{:S(2)}) copy-start(s32[8]{0:T(128)} %chan_hbm.1) | copy-start | bytes 100
  13.4 5.7 %collective-permute-start = (bf16[2,72,128]{2,1,0:T(8,128)(2,1)S(1)}, bf16[2,72,128]{2,1,0:T(8,128)(2,1)S(1)}, u32[]{:S(2)}, u32[]{:S(2)}) collective-permute-start(bf16[2,72,128]{2,1,0:T(8,128)(2,1)S(1)} %get-tuple-element.10), channel_id=1, source_target_pairs={{0,8},{8,0},{16,24},{24,16},{1,9},{9,1},{17,25},{25,17},{2,10},{10... | collective-permute-start | bytes 110600 | tf_op jit(solution)/shard_map/ppermute | solution.py:305
  16.4 5.5 %collective-permute-start.1 = (bf16[2,72,128]{2,1,0:T(8,128)(2,1)S(1)}, bf16[2,72,128]{2,1,0:T(8,128)(2,1)S(1)}, u32[]{:S(2)}, u32[]{:S(2)}) collective-permute-start(bf16[2,72,128]{2,1,0:T(8,128)(2,1)S(1)} %get-tuple-element.11), channel_id=1, source_target_pairs={{0,16},{8,24},{16,0},{24,8},{1,17},{9,25},{17,1},{25,9},{2,18},{10... | collective-permute-start | bytes 110600 | tf_op jit(solution)/shard_map/ppermute | solution.py:305
  19.0 5.8 %collective-permute-start.2 = (bf16[2,72,128]{2,1,0:T(8,128)(2,1)S(1)}, bf16[2,72,128]{2,1,0:T(8,128)(2,1)S(1)}, u32[]{:S(2)}, u32[]{:S(2)}) collective-permute-start(bf16[2,72,128]{2,1,0:T(8,128)(2,1)S(1)} %get-tuple-element.12), channel_id=1, source_target_pairs={{0,24},{8,16},{16,8},{24,0},{1,25},{9,17},{17,9},{25,1},{2,26},{10... | collective-permute-start | bytes 110600 | tf_op jit(solution)/shard_map/ppermute | solution.py:305
  24.8 4.7 %collective-permute-start.4 = (bf16[4,72,128]{2,1,0:T(8,128)(2,1)S(1)}, bf16[4,72,128]{2,1,0:T(8,128)(2,1)S(1)}, u32[]{:S(2)}, u32[]{:S(2)}) collective-permute-start(bf16[4,72,128]{2,1,0:T(8,128)(2,1)S(1)} %pad_maximum_fusion.refs_0_), channel_id=1, source_target_pairs={{0,2},{1,3},{2,0},{3,1},{4,6},{5,7},{6,4},{7,5},{8,10},{9,11},{10,... | collective-permute-start | bytes 221192 | tf_op jit(solution)/shard_map/ppermute | solution.py:305
  26.4 5.3 %collective-permute-start.8 = (bf16[4,72,128]{2,1,0:T(8,128)(2,1)S(1)}, bf16[4,72,128]{2,1,0:T(8,128)(2,1)S(1)}, u32[]{:S(2)}, u32[]{:S(2)}) collective-permute-start(bf16[4,72,128]{2,1,0:T(8,128)(2,1)S(1)} %pad_maximum_fusion.1), channel_id=1, source_target_pairs={{0,6},{1,7},{2,4},{3,5},{4,2},{5,3},{6,0},{7,1},{8,14},{9,15},{10,... | collective-permute-start | bytes 221192 | tf_op jit(solution)/shard_map/ppermute | solution.py:305
  27.9 4.4 %collective-permute-start.6 = (bf16[4,72,128]{2,1,0:T(8,128)(2,1)S(1)}, bf16[4,72,128]{2,1,0:T(8,128)(2,1)S(1)}, u32[]{:S(2)}, u32[]{:S(2)}) collective-permute-start(bf16[4,72,128]{2,1,0:T(8,128)(2,1)S(1)} %pad_maximum_fusion.1), channel_id=1, source_target_pairs={{0,4},{1,5},{2,6},{3,7},{4,0},{5,1},{6,2},{7,3},{8,12},{9,13},{10,... | collective-permute-start | bytes 221192 | tf_op jit(solution)/shard_map/ppermute | solution.py:305
  28.4 3.8 %collective-permute-start.3 = (bf16[4,72,128]{2,1,0:T(8,128)(2,1)S(1)}, bf16[4,72,128]{2,1,0:T(8,128)(2,1)S(1)}, u32[]{:S(2)}, u32[]{:S(2)}) collective-permute-start(bf16[4,72,128]{2,1,0:T(8,128)(2,1)S(1)} %pad_maximum_fusion.refs_0_), channel_id=1, source_target_pairs={{0,1},{1,0},{2,3},{3,2},{4,5},{5,4},{6,7},{7,6},{8,9},{9,8},{10,11... | collective-permute-start | bytes 221192 | tf_op jit(solution)/shard_map/ppermute | solution.py:305
  29.5 2.8 %collective-permute-start.5 = (bf16[4,72,128]{2,1,0:T(8,128)(2,1)S(1)}, bf16[4,72,128]{2,1,0:T(8,128)(2,1)S(1)}, u32[]{:S(2)}, u32[]{:S(2)}) collective-permute-start(bf16[4,72,128]{2,1,0:T(8,128)(2,1)S(1)} %collective-permute-done.4.refs_2_), channel_id=1, source_target_pairs={{0,1},{1,0},{2,3},{3,2},{4,5},{5,4},{6,7},{7,6},{8,9},{9,8},{10,11... | collective-permute-start | bytes 221192 | tf_op jit(solution)/shard_map/ppermute | solution.py:305
  31.7 1.3 %collective-permute-start.9 = (bf16[4,72,128]{2,1,0:T(8,128)(2,1)S(1)}, bf16[4,72,128]{2,1,0:T(8,128)(2,1)S(1)}, u32[]{:S(2)}, u32[]{:S(2)}) collective-permute-start(bf16[4,72,128]{2,1,0:T(8,128)(2,1)S(1)} %collective-permute-done.8.refs_6_), channel_id=1, source_target_pairs={{0,1},{1,0},{2,3},{3,2},{4,5},{5,4},{6,7},{7,6},{8,9},{9,8},{10,11... | collective-permute-start | bytes 221192 | tf_op jit(solution)/shard_map/ppermute | solution.py:305
  32.3 1.3 %collective-permute-start.7 = (bf16[4,72,128]{2,1,0:T(8,128)(2,1)S(1)}, bf16[4,72,128]{2,1,0:T(8,128)(2,1)S(1)}, u32[]{:S(2)}, u32[]{:S(2)}) collective-permute-start(bf16[4,72,128]{2,1,0:T(8,128)(2,1)S(1)} %collective-permute-done.6.refs_4_), channel_id=1, source_target_pairs={{0,1},{1,0},{2,3},{3,2},{4,5},{5,4},{6,7},{7,6},{8,9},{9,8},{10,11... | collective-permute-start | bytes 221192 | tf_op jit(solution)/shard_map/ppermute | solution.py:305

commit v4 on v3

--- a/solution.py
+++ b/solution.py
@@ -11,6 +11,9 @@
 TAPS = 4
 LANES = 128
 GROUP = 4
+BANK = 16
+PIECES = 3
+EIGHT = jnp.float8_e4m3fn
 
 
 def bin_column(chan_ref, chans):
@@ -21,28 +24,27 @@
     return out[:, :1]
 
 
-def build_weights(chan_ref, w_ref, chans):
-    frame = w_ref.shape[1]
-    half = w_ref.shape[0] // 2
+def build_weights(chan_ref, w_ref, chans, frame):
     bins = bin_column(chan_ref, chans)
     steps = lax.broadcasted_iota(jnp.int32, (chans, frame), 1)
     angle = (bins * steps % frame).astype(jnp.float32) * (2.0 * math.pi / frame)
     scale = 1.0 / math.sqrt(frame)
     table = jnp.concatenate([jnp.cos(angle) * scale, -jnp.sin(angle) * scale], axis=0)
-    table = table.astype(jnp.bfloat16).astype(jnp.float32) * 0.25
+    units = 2.0 ** math.floor(math.log2(256.0 * 4.0 / scale))
+    table = table.astype(jnp.bfloat16).astype(jnp.float32) * (0.25 * units)
     tap = lax.broadcasted_iota(jnp.int32, (8, frame), 0) % TAPS
     place = lax.broadcasted_iota(jnp.int32, (8, frame), 1) + tap * frame
     place = place.astype(jnp.float32) + 0.5
     turn = math.pi * ((place - 2.0 * frame) / frame)
     window = 0.5 - 0.5 * jnp.cos(place * (2.0 * math.pi / (TAPS * frame)))
     taps = jnp.sin(turn) / turn * window
-    rows = 2 * chans
-    for k in range(TAPS):
-        full = taps[k : k + 1] * table
-        high = full.astype(jnp.bfloat16)
-        low = (full - high.astype(jnp.float32)).astype(jnp.bfloat16)
-        w_ref[k * rows : (k + 1) * rows] = high
-        w_ref[half + k * rows : half + (k + 1) * rows] = low
+    left = jnp.concatenate([taps[k : k + 1] * table for k in range(TAPS)], axis=0)
+    count = left.shape[0]
+    for piece in range(PIECES):
+        part = left.astype(EIGHT)
+        w_ref[piece * count : (piece + 1) * count, :] = part
+        left = (left - part.astype(jnp.float32)) * 16.0
+    return units
 
 
 def shift_and_add(chans, in_dev, fr_dev, pair, raw, spec, carry):
@@ -63,11 +65,8 @@
     odd = jnp.where(first, pltpu.roll(re, fr_dev, 1), im)
     spec[pl.ds(pair * 2, chans, stride=in_dev), :] = even
     spec[pl.ds(pair * 2 + 1, chans, stride=in_dev), :] = odd
-    shift = pair * TAPS
-    from_even = jnp.where(lane >= fr_dev, over, 0.0)
-    from_odd = jnp.where(lane < fr_dev, over, 0.0)
-    carry[0] += pltpu.roll(from_even, (shift + fr_dev) % LANES, 1)
-    carry[1] += pltpu.roll(from_odd, shift, 1) if shift else from_odd
+    bank, shift = pair // BANK, pair % BANK * TAPS
+    carry[bank] += pltpu.roll(over, shift, 1) if shift else over
 
 
 def channelize_kernel(chans, relative, mesh_shape, me_ref, chan_hbm, x_ref, *refs):
@@ -75,9 +74,9 @@
     buf, w_ref, raw, spec, carry, edge, chan_ref, sems, chan_sem = refs
     in_dev, fr_dev, frame = x_ref.shape
     n_freq, n_tm, n_bl = mesh_shape
-    groups = [(i, GROUP) for i in range(0, in_dev - 2 * GROUP, GROUP)]
-    tail = len(groups) * GROUP
-    groups += [(i, 2) for i in range(tail, in_dev, 2)]
+    tail = (in_dev - 1) // GROUP * GROUP
+    groups = [(i, GROUP) for i in range(0, tail, GROUP)]
+    groups += [(i, 4) for i in range(tail, in_dev, 4)]
 
     def fetch(first, count, sem):
         span = pl.ds(first, count)
@@ -88,21 +87,24 @@
     for g, (first, count) in enumerate(groups):
         fetch(first, count, g).start()
     chan_copy.wait()
-    build_weights(chan_ref, w_ref, chans)
+    units = build_weights(chan_ref, w_ref, chans, frame)
     carry[...] = jnp.zeros_like(carry)
 
     def multiply(first, count, sem):
         fetch(first, count, sem).wait()
         x = buf[pl.ds(first, count)].astype(jnp.float32) - 7.5
-        x = x.astype(jnp.bfloat16).reshape(count * fr_dev, frame)
-        both = lax.dot_general(
+        x = x.astype(EIGHT).reshape(count * fr_dev, frame)
+        pieces = lax.dot_general(
             w_ref[...], x, (((1,), (1,)), ((), ())), preferred_element_type=jnp.float32
         )
-        half = both.shape[0] // 2
+        rows = pieces.shape[0] // PIECES
+        total = pieces[:rows] * (1.0 / units)
+        for piece in range(1, PIECES):
+            total += pieces[piece * rows : (piece + 1) * rows] * (0.0625**piece / units)
         at = first * fr_dev
         if not isinstance(first, int):
             at = pl.multiple_of(at, GROUP * fr_dev)
-        raw[:, pl.ds(at, count * fr_dev)] = both[:half] + both[half:]
+        raw[:, pl.ds(at, count * fr_dev)] = total
 
     def step(g, _):
         multiply(g * GROUP, GROUP, g)
@@ -136,13 +138,14 @@
     for g, (first, count) in enumerate(groups):
         if first >= tail:
             multiply(first, count, g)
-            shift_and_add(chans, in_dev, fr_dev, first // 2, raw, spec, carry)
+            for pair in range(first // 2, (first + count) // 2):
+                shift_and_add(chans, in_dev, fr_dev, pair, raw, spec, carry)
     emit(early, in_dev - early)
     edge[...] = jnp.zeros_like(edge)
     for p in range(2):
-        for odd in range(2):
-            rows = carry[odd, p * chans : (p + 1) * chans, :]
-            edge[pl.ds(2 * p + odd, chans, stride=8), :] = rows
+        for bank in range(2):
+            rows = carry[bank, p * chans : (p + 1) * chans, :]
+            edge[pl.ds(2 * p + bank, chans, stride=8), :] = rows
     for m in range(chans):
         per = chans // len(outs)
         at = slot(m) * 8
@@ -160,6 +163,7 @@
     products = TAPS * 2 * chans
     parts = mesh_shape[0] if relative else 1
     out = jax.ShapeDtypeStruct((chans // parts, rows, LANES), jnp.bfloat16)
+    chan_index = pltpu.with_memory_space_constraint(chan_index, pltpu.HBM)
     return pl.pallas_call(
         functools.partial(channelize_kernel, chans, relative, mesh_shape),
         in_specs=[
@@ -171,7 +175,7 @@
         out_shape=[out] * parts,
         scratch_shapes=[
             pltpu.VMEM(samples.shape, jnp.int32),
-            pltpu.VMEM((2 * products, frame), jnp.bfloat16),
+            pltpu.VMEM((PIECES * products, frame), EIGHT),
             pltpu.VMEM((products, in_dev * fr_dev), jnp.float32),
             pltpu.VMEM((chans * in_dev, LANES), jnp.float32),
             pltpu.VMEM((2, 2 * chans, LANES), jnp.float32),
@@ -188,8 +192,8 @@
 def place_carry(carried, in_dev, fr_dev):
     mine = lax.broadcasted_iota(jnp.int32, (in_dev, LANES), 0)
     lane = lax.broadcasted_iota(jnp.int32, (in_dev, LANES), 1)
-    mask = lane // TAPS == mine // 2
-    odd = mine % 2 == 1
+    mask = lane // TAPS == mine // 2 % BANK + (1 - mine % 2) * BANK
+    second = mine // 2 >= BANK
     src = lax.broadcasted_iota(jnp.int32, (2 * LANES, LANES), 0)
     dst = lax.broadcasted_iota(jnp.int32, (2 * LANES, LANES), 1)
     place = (src // LANES) * fr_dev + src % TAPS
@@ -198,7 +202,7 @@
     for four in carried:
         both = []
         for p in range(2):
-            row = jnp.where(odd, four[2 * p + 1][None], four[2 * p][None])
+            row = jnp.where(second, four[2 * p + 1][None], four[2 * p][None])
             both.append(jnp.where(mask, row, 0.0).astype(jnp.bfloat16))
         picked.append(jnp.concatenate(both, axis=1))
     return jnp.dot(
@@ -283,10 +287,10 @@
     blocks = gathered.reshape(n_bl, n_freq, n_tm, -1, LANES)
     blocks = jnp.transpose(blocks, (1, 0, 2, 3, 4)).astype(jnp.float32)
     main = blocks[:, :, :, :in_dev].reshape(n_freq, n_bl, n_tm, in_dev, 2, fr_dev)
-    over = blocks[:, :, :-1, in_dev : in_dev + 4, : in_dev // 2 * TAPS]
-    over = over.reshape(n_freq, n_bl, n_tm - 1, 2, 2, in_dev // 2, TAPS)
-    over = jnp.transpose(over, (0, 1, 2, 5, 4, 3, 6))
-    over = over.reshape(n_freq, n_bl, n_tm - 1, in_dev, 2, TAPS)[..., : TAPS - 1]
+    over = blocks[:, :, :-1, in_dev : in_dev + 4]
+    over = over.reshape(n_freq, n_bl, n_tm - 1, 2, 2, 2, BANK, TAPS)[:, :, :, :, :, ::-1]
+    over = jnp.transpose(over, (0, 1, 2, 4, 6, 5, 3, 7))
+    over = over.reshape(n_freq, n_bl, n_tm - 1, 4 * BANK, 2, TAPS)[:, :, :, :in_dev, :, : TAPS - 1]
     over = jnp.pad(over, [(0, 0)] * 2 + [(1, 0)] + [(0, 0)] * 2 + [(0, fr_dev - TAPS + 1)])
     whole = (main + over).astype(jnp.bfloat16)
     whole = jnp.transpose(whole, (4, 0, 1, 3, 2, 5)).reshape(2, 2 * half, n_tm * fr_dev)

time: 35.7 us -> 33.7 us (0.944)
  Pallas kernels: 14.7 us -> 13.4 us
  local copies, waits for them, and re-layouts: 0.67 us -> 0.02 us
    pallas_call x1, Pallas kernels: 12.7 us -> 11.4 us  [channelize(): pl.pallas_call(functools.partial(channelize_kernel, chans, relative, mesh...]
    unnamed x2 -> x0, local copies, waits for them, and re-layouts: 0.65 us -> none
where the time goes in v4:
time: 33.7 us; the launch traced here: 33.6 us
  Pallas kernels  13.4 us (40%)
  waiting for transfers between devices  10.8 us (32%)
  starting transfers between devices  9.31 us (28%)
    pallas_call x1, Pallas kernels, channelize(): pl.pallas_call(functools.partial(channelize_kernel, chans, relative, mesh...  11.4 us
    ppermute x10, waiting for transfers between devices, swapped(): return lax.ppermute(block, axes, [(i, i ^ distance) for i in range(count)])  10.8 us
    ppermute x10, starting transfers between devices, swapped(): return lax.ppermute(block, axes, [(i, i ^ distance) for i in range(count)])  9.31 us
    pallas_call x1, Pallas kernels, correlate(): pl.pallas_call(functools.partial(correlate_kernel, mesh_shape, in_dev, fr...  2 us
  transfers between devices with their start and end apart: 10, of which 7 were waited for; matrix products, arithmetic and copies ran while one was open for 0% of the time, Pallas kernels for 0%

profile of v4, /device:TPU:0, one launch (start us, length us, event | category | flops | bytes accessed | tf_op | source)
XLA Modules:
  0.0 33.6 jit_solution(2244877788451589826)
XLA Ops:
  0.0 11.4 %channelize.1 = (bf16[2,72,128]{2,1,0:T(8,128)(2,1)S(1)}, bf16[2,72,128]{2,1,0:T(8,128)(2,1)S(1)}, bf16[2,72,128]{2,1,0:T(8,128)(2,1)S(1)}, bf16[2,72,128]{2,1,0:T(8,128)(2,1)S(1)}) custom-call(s32[1]{0:T(128)} %bitcast.me_ref, s32[8]{0:T(128)} %chan_hbm.1, s32[64,64,2048]{2,1,0:T(8,128)} %x_ref.1), custom_call_target="tpu_custom_call" | custom-call | tf_op jit(solution)/shard_map/channelize/pallas_call | solution.py:167
  11.4 3.1 %collective-permute-start = (bf16[2,72,128]{2,1,0:T(8,128)(2,1)S(1)}, bf16[2,72,128]{2,1,0:T(8,128)(2,1)S(1)}, u32[]{:S(2)}, u32[]{:S(2)}) collective-permute-start(bf16[2,72,128]{2,1,0:T(8,128)(2,1)S(1)} %get-tuple-element.10), channel_id=1, source_target_pairs={{0,8},{8,0},{16,24},{24,16},{1,9},{9,1},{17,25},{25,17},{2,10},{10... | collective-permute-start | bytes 110600 | tf_op jit(solution)/shard_map/ppermute | solution.py:309
  14.5 2.6 %collective-permute-start.1 = (bf16[2,72,128]{2,1,0:T(8,128)(2,1)S(1)}, bf16[2,72,128]{2,1,0:T(8,128)(2,1)S(1)}, u32[]{:S(2)}, u32[]{:S(2)}) collective-permute-start(bf16[2,72,128]{2,1,0:T(8,128)(2,1)S(1)} %get-tuple-element.11), channel_id=1, source_target_pairs={{0,16},{8,24},{16,0},{24,8},{1,17},{9,25},{17,1},{25,9},{2,18},{10... | collective-permute-start | bytes 110600 | tf_op jit(solution)/shard_map/ppermute | solution.py:309
  17.1 0.0 collective-permute-start.2
  17.1 0.0 collective-permute-done
  17.1 2.9 %collective-permute-done.1 = bf16[2,72,128]{2,1,0:T(8,128)(2,1)S(1)} collective-permute-done((bf16[2,72,128]{2,1,0:T(8,128)(2,1)S(1)}, bf16[2,72,128]{2,1,0:T(8,128)(2,1)S(1)}, u32[]{:S(2)}, u32[]{:S(2)}) %collective-permute-start.1) | collective-permute-done | bytes 36896 | tf_op jit(solution)/shard_map/ppermute | solution.py:309
  20.0 2.8 %collective-permute-done.2 = bf16[2,72,128]{2,1,0:T(8,128)(2,1)S(1)} collective-permute-done((bf16[2,72,128]{2,1,0:T(8,128)(2,1)S(1)}, bf16[2,72,128]{2,1,0:T(8,128)(2,1)S(1)}, u32[]{:S(2)}, u32[]{:S(2)}) %collective-permute-start.2) | collective-permute-done | bytes 36896 | tf_op jit(solution)/shard_map/ppermute | solution.py:309
  22.9 1.6 %collective-permute-start.4 = (bf16[4,72,128]{2,1,0:T(8,128)(2,1)S(1)}, bf16[4,72,128]{2,1,0:T(8,128)(2,1)S(1)}, u32[]{:S(2)}, u32[]{:S(2)}) collective-permute-start(bf16[4,72,128]{2,1,0:T(8,128)(2,1)S(1)} %pad_maximum_fusion.refs_0_), channel_id=1, source_target_pairs={{0,2},{1,3},{2,0},{3,1},{4,6},{5,7},{6,4},{7,5},{8,10},{9,11},{10,... | collective-permute-start | bytes 221192 | tf_op jit(solution)/shard_map/ppermute | solution.py:309
  24.5 1.5 %collective-permute-start.8 = (bf16[4,72,128]{2,1,0:T(8,128)(2,1)S(1)}, bf16[4,72,128]{2,1,0:T(8,128)(2,1)S(1)}, u32[]{:S(2)}, u32[]{:S(2)}) collective-permute-start(bf16[4,72,128]{2,1,0:T(8,128)(2,1)S(1)} %pad_maximum_fusion.1), channel_id=1, source_target_pairs={{0,6},{1,7},{2,4},{3,5},{4,2},{5,3},{6,0},{7,1},{8,14},{9,15},{10,... | collective-permute-start | bytes 221192 | tf_op jit(solution)/shard_map/ppermute | solution.py:309
  26.0 0.5 %collective-permute-start.6 = (bf16[4,72,128]{2,1,0:T(8,128)(2,1)S(1)}, bf16[4,72,128]{2,1,0:T(8,128)(2,1)S(1)}, u32[]{:S(2)}, u32[]{:S(2)}) collective-permute-start(bf16[4,72,128]{2,1,0:T(8,128)(2,1)S(1)} %pad_maximum_fusion.1), channel_id=1, source_target_pairs={{0,4},{1,5},{2,6},{3,7},{4,0},{5,1},{6,2},{7,3},{8,12},{9,13},{10,... | collective-permute-start | bytes 221192 | tf_op jit(solution)/shard_map/ppermute | solution.py:309
  26.5 0.0 collective-permute-start.3
  26.5 1.1 %collective-permute-done.4.refs_2_ = bf16[4,72,128]{2,1,0:T(8,128)(2,1)S(1)} collective-permute-done((bf16[4,72,128]{2,1,0:T(8,128)(2,1)S(1)}, bf16[4,72,128]{2,1,0:T(8,128)(2,1)S(1)}, u32[]{:S(2)}, u32[]{:S(2)}) %collective-permute-start.4) | collective-permute-done | bytes 73760 | tf_op jit(solution)/shard_map/ppermute | solution.py:309
  27.6 0.0 collective-permute-start.5
  27.6 2.2 %collective-permute-done.8.refs_6_ = bf16[4,72,128]{2,1,0:T(8,128)(2,1)S(1)} collective-permute-done((bf16[4,72,128]{2,1,0:T(8,128)(2,1)S(1)}, bf16[4,72,128]{2,1,0:T(8,128)(2,1)S(1)}, u32[]{:S(2)}, u32[]{:S(2)}) %collective-permute-start.8) | collective-permute-done | bytes 73760 | tf_op jit(solution)/shard_map/ppermute | solution.py:309
  29.8 0.0 collective-permute-start.9
  29.8 0.5 %collective-permute-done.6.refs_4_ = bf16[4,72,128]{2,1,0:T(8,128)(2,1)S(1)} collective-permute-done((bf16[4,72,128]{2,1,0:T(8,128)(2,1)S(1)}, bf16[4,72,128]{2,1,0:T(8,128)(2,1)S(1)}, u32[]{:S(2)}, u32[]{:S(2)}) %collective-permute-start.6) | collective-permute-done | bytes 73760 | tf_op jit(solution)/shard_map/ppermute | solution.py:309
  30.3 0.0 collective-permute-start.7
  30.3 0.0 collective-permute-done.3.refs_1_
  30.3 0.0 collective-permute-done.5.refs_3_
  30.3 0.7 %collective-permute-done.9.refs_7_ = bf16[4,72,128]{2,1,0:T(8,128)(2,1)S(1)} collective-permute-done((bf16[4,72,128]{2,1,0:T(8,128)(2,1)S(1)}, bf16[4,72,128]{2,1,0:T(8,128)(2,1)S(1)}, u32[]{:S(2)}, u32[]{:S(2)}) %collective-permute-start.9) | collective-permute-done | bytes 73760 | tf_op jit(solution)/shard_map/ppermute | solution.py:309
  31.1 0.5 %collective-permute-done.7.refs_5_ = bf16[4,72,128]{2,1,0:T(8,128)(2,1)S(1)} collective-permute-done((bf16[4,72,128]{2,1,0:T(8,128)(2,1)S(1)}, bf16[4,72,128]{2,1,0:T(8,128)(2,1)S(1)}, u32[]{:S(2)}, u32[]{:S(2)}) %collective-permute-start.7) | collective-permute-done | bytes 73760 | tf_op jit(solution)/shard_map/ppermute | solution.py:309
  31.6 2.0 %correlate.1 = f32[1,1,2,512,512]{4,3,2,1,0:T(8,128)} custom-call(s32[1]{0:T(128)} %bitcast.me_ref, bf16[4,72,128]{2,1,0:T(8,128)(2,1)S(1)} %pad_maximum_fusion.refs_0_, bf16[4,72,128]{2,1,0:T(8,128)(2,1)S(1)} %collective-permute-done.3.refs_1_, bf16[4,72,128]{2,1,0:T(8,128)(2,1)S(1)} %collective-permute-done.4.refs_2_, ...), custom_call_target="tpu_custom_call" | custom-call | tf_op jit(solution)/shard_map/correlate/pallas_call | solution.py:267
  (6 shorter events, 0.0 us)
Async XLA Ops:
  11.4 5.7 %collective-permute-start = (bf16[2,72,128]{2,1,0:T(8,128)(2,1)S(1)}, bf16[2,72,128]{2,1,0:T(8,128)(2,1)S(1)}, u32[]{:S(2)}, u32[]{:S(2)}) collective-permute-start(bf16[2,72,128]{2,1,0:T(8,128)(2,1)S(1)} %get-tuple-element.10), channel_id=1, source_target_pairs={{0,8},{8,0},{16,24},{24,16},{1,9},{9,1},{17,25},{25,17},{2,10},{10... | collective-permute-start | bytes 110600 | tf_op jit(solution)/shard_map/ppermute | solution.py:309
  14.5 5.5 %collective-permute-start.1 = (bf16[2,72,128]{2,1,0:T(8,128)(2,1)S(1)}, bf16[2,72,128]{2,1,0:T(8,128)(2,1)S(1)}, u32[]{:S(2)}, u32[]{:S(2)}) collective-permute-start(bf16[2,72,128]{2,1,0:T(8,128)(2,1)S(1)} %get-tuple-element.11), channel_id=1, source_target_pairs={{0,16},{8,24},{16,0},{24,8},{1,17},{9,25},{17,1},{25,9},{2,18},{10... | collective-permute-start | bytes 110600 | tf_op jit(solution)/shard_map/ppermute | solution.py:309
  17.1 5.8 %collective-permute-start.2 = (bf16[2,72,128]{2,1,0:T(8,128)(2,1)S(1)}, bf16[2,72,128]{2,1,0:T(8,128)(2,1)S(1)}, u32[]{:S(2)}, u32[]{:S(2)}) collective-permute-start(bf16[2,72,128]{2,1,0:T(8,128)(2,1)S(1)} %get-tuple-element.12), channel_id=1, source_target_pairs={{0,24},{8,16},{16,8},{24,0},{1,25},{9,17},{17,9},{25,1},{2,26},{10... | collective-permute-start | bytes 110600 | tf_op jit(solution)/shard_map/ppermute | solution.py:309
  22.9 4.7 %collective-permute-start.4 = (bf16[4,72,128]{2,1,0:T(8,128)(2,1)S(1)}, bf16[4,72,128]{2,1,0:T(8,128)(2,1)S(1)}, u32[]{:S(2)}, u32[]{:S(2)}) collective-permute-start(bf16[4,72,128]{2,1,0:T(8,128)(2,1)S(1)} %pad_maximum_fusion.refs_0_), channel_id=1, source_target_pairs={{0,2},{1,3},{2,0},{3,1},{4,6},{5,7},{6,4},{7,5},{8,10},{9,11},{10,... | collective-permute-start | bytes 221192 | tf_op jit(solution)/shard_map/ppermute | solution.py:309
  24.5 5.3 %collective-permute-start.8 = (bf16[4,72,128]{2,1,0:T(8,128)(2,1)S(1)}, bf16[4,72,128]{2,1,0:T(8,128)(2,1)S(1)}, u32[]{:S(2)}, u32[]{:S(2)}) collective-permute-start(bf16[4,72,128]{2,1,0:T(8,128)(2,1)S(1)} %pad_maximum_fusion.1), channel_id=1, source_target_pairs={{0,6},{1,7},{2,4},{3,5},{4,2},{5,3},{6,0},{7,1},{8,14},{9,15},{10,... | collective-permute-start | bytes 221192 | tf_op jit(solution)/shard_map/ppermute | solution.py:309
  26.0 4.4 %collective-permute-start.6 = (bf16[4,72,128]{2,1,0:T(8,128)(2,1)S(1)}, bf16[4,72,128]{2,1,0:T(8,128)(2,1)S(1)}, u32[]{:S(2)}, u32[]{:S(2)}) collective-permute-start(bf16[4,72,128]{2,1,0:T(8,128)(2,1)S(1)} %pad_maximum_fusion.1), channel_id=1, source_target_pairs={{0,4},{1,5},{2,6},{3,7},{4,0},{5,1},{6,2},{7,3},{8,12},{9,13},{10,... | collective-permute-start | bytes 221192 | tf_op jit(solution)/shard_map/ppermute | solution.py:309
  26.5 3.8 %collective-permute-start.3 = (bf16[4,72,128]{2,1,0:T(8,128)(2,1)S(1)}, bf16[4,72,128]{2,1,0:T(8,128)(2,1)S(1)}, u32[]{:S(2)}, u32[]{:S(2)}) collective-permute-start(bf16[4,72,128]{2,1,0:T(8,128)(2,1)S(1)} %pad_maximum_fusion.refs_0_), channel_id=1, source_target_pairs={{0,1},{1,0},{2,3},{3,2},{4,5},{5,4},{6,7},{7,6},{8,9},{9,8},{10,11... | collective-permute-start | bytes 221192 | tf_op jit(solution)/shard_map/ppermute | solution.py:309
  27.6 2.8 %collective-permute-start.5 = (bf16[4,72,128]{2,1,0:T(8,128)(2,1)S(1)}, bf16[4,72,128]{2,1,0:T(8,128)(2,1)S(1)}, u32[]{:S(2)}, u32[]{:S(2)}) collective-permute-start(bf16[4,72,128]{2,1,0:T(8,128)(2,1)S(1)} %collective-permute-done.4.refs_2_), channel_id=1, source_target_pairs={{0,1},{1,0},{2,3},{3,2},{4,5},{5,4},{6,7},{7,6},{8,9},{9,8},{10,11... | collective-permute-start | bytes 221192 | tf_op jit(solution)/shard_map/ppermute | solution.py:309
  29.8 1.3 %collective-permute-start.9 = (bf16[4,72,128]{2,1,0:T(8,128)(2,1)S(1)}, bf16[4,72,128]{2,1,0:T(8,128)(2,1)S(1)}, u32[]{:S(2)}, u32[]{:S(2)}) collective-permute-start(bf16[4,72,128]{2,1,0:T(8,128)(2,1)S(1)} %collective-permute-done.8.refs_6_), channel_id=1, source_target_pairs={{0,1},{1,0},{2,3},{3,2},{4,5},{5,4},{6,7},{7,6},{8,9},{9,8},{10,11... | collective-permute-start | bytes 221192 | tf_op jit(solution)/shard_map/ppermute | solution.py:309
  30.3 1.3 %collective-permute-start.7 = (bf16[4,72,128]{2,1,0:T(8,128)(2,1)S(1)}, bf16[4,72,128]{2,1,0:T(8,128)(2,1)S(1)}, u32[]{:S(2)}, u32[]{:S(2)}) collective-permute-start(bf16[4,72,128]{2,1,0:T(8,128)(2,1)S(1)} %collective-permute-done.6.refs_4_), channel_id=1, source_target_pairs={{0,1},{1,0},{2,3},{3,2},{4,5},{5,4},{6,7},{7,6},{8,9},{9,8},{10,11... | collective-permute-start | bytes 221192 | tf_op jit(solution)/shard_map/ppermute | solution.py:309

commit v5 on v4

--- a/solution.py
+++ b/solution.py
@@ -12,8 +12,9 @@
 LANES = 128
 GROUP = 4
 BANK = 16
-PIECES = 3
-EIGHT = jnp.float8_e4m3fn
+PIECES = 2
+NARROW = jnp.bfloat16
+ORDER = (0, 2, 3, 1)
 
 
 def bin_column(chan_ref, chans):
@@ -30,8 +31,7 @@
     angle = (bins * steps % frame).astype(jnp.float32) * (2.0 * math.pi / frame)
     scale = 1.0 / math.sqrt(frame)
     table = jnp.concatenate([jnp.cos(angle) * scale, -jnp.sin(angle) * scale], axis=0)
-    units = 2.0 ** math.floor(math.log2(256.0 * 4.0 / scale))
-    table = table.astype(jnp.bfloat16).astype(jnp.float32) * (0.25 * units)
+    table = table.astype(jnp.bfloat16).astype(jnp.float32) * 0.25
     tap = lax.broadcasted_iota(jnp.int32, (8, frame), 0) % TAPS
     place = lax.broadcasted_iota(jnp.int32, (8, frame), 1) + tap * frame
     place = place.astype(jnp.float32) + 0.5
@@ -41,10 +41,9 @@
     left = jnp.concatenate([taps[k : k + 1] * table for k in range(TAPS)], axis=0)
     count = left.shape[0]
     for piece in range(PIECES):
-        part = left.astype(EIGHT)
+        part = left.astype(NARROW)
         w_ref[piece * count : (piece + 1) * count, :] = part
-        left = (left - part.astype(jnp.float32)) * 16.0
-    return units
+        left = left - part.astype(jnp.float32)
 
 
 def shift_and_add(chans, in_dev, fr_dev, pair, raw, spec, carry):
@@ -87,20 +86,20 @@
     for g, (first, count) in enumerate(groups):
         fetch(first, count, g).start()
     chan_copy.wait()
-    units = build_weights(chan_ref, w_ref, chans, frame)
+    build_weights(chan_ref, w_ref, chans, frame)
     carry[...] = jnp.zeros_like(carry)
 
     def multiply(first, count, sem):
         fetch(first, count, sem).wait()
         x = buf[pl.ds(first, count)].astype(jnp.float32) - 7.5
-        x = x.astype(EIGHT).reshape(count * fr_dev, frame)
+        x = x.astype(NARROW).reshape(count * fr_dev, frame)
         pieces = lax.dot_general(
             w_ref[...], x, (((1,), (1,)), ((), ())), preferred_element_type=jnp.float32
         )
         rows = pieces.shape[0] // PIECES
-        total = pieces[:rows] * (1.0 / units)
+        total = pieces[:rows]
         for piece in range(1, PIECES):
-            total += pieces[piece * rows : (piece + 1) * rows] * (0.0625**piece / units)
+            total += pieces[piece * rows : (piece + 1) * rows]
         at = first * fr_dev
         if not isinstance(first, int):
             at = pl.multiple_of(at, GROUP * fr_dev)
@@ -175,7 +174,7 @@
         out_shape=[out] * parts,
         scratch_shapes=[
             pltpu.VMEM(samples.shape, jnp.int32),
-            pltpu.VMEM((PIECES * products, frame), EIGHT),
+            pltpu.VMEM((PIECES * products, frame), NARROW),
             pltpu.VMEM((products, in_dev * fr_dev), jnp.float32),
             pltpu.VMEM((chans * in_dev, LANES), jnp.float32),
             pltpu.VMEM((2, 2 * chans, LANES), jnp.float32),
@@ -210,6 +209,13 @@
     )
 
 
+def place_of(turn):
+    at = jnp.int32(0)
+    for place, k in enumerate(ORDER):
+        at = jnp.where(turn == k, place, at)
+    return at
+
+
 def correlate_kernel(mesh_shape, in_dev, fr_dev, me_ref, *refs):
     n_freq, n_tm, n_bl = mesh_shape
     own_half, other_half = refs[:n_bl], refs[n_bl : 2 * n_bl]
@@ -221,7 +227,7 @@
     for out, base in ((left, bl // 2 * (n_freq // 2)), (right, bl % 2 * (n_freq // 2))):
         early, late, carried = [], [], []
         for f, k in order:
-            at = (base + f) ^ freq
+            at = place_of((base + f) ^ freq)
             mine, other = own_half[k], other_half[k]
             body, over = slice(0, in_dev), slice(in_dev, in_dev + 4)
             early.append(jnp.where(tm == 0, mine[at, body, :], other[at, body, :]))
@@ -313,8 +319,8 @@
     arrived = [parts[0]] + [None] * (len(parts) - 1)
     for k in reversed(range(1, len(parts))):
         arrived[k] = swapped(parts[k], ("freq",), k)
-    keep = jnp.stack([block[0] for block in arrived])
-    send = jnp.stack([block[1] for block in arrived])
+    keep = jnp.stack([arrived[k][0] for k in ORDER])
+    send = jnp.stack([arrived[k][1] for k in ORDER])
     across = ("tm", "bl")
     corner = swapped(send, across, n_bl + 2)
     beside = swapped(send, across, n_bl)

time: 33.7 us -> 32.4 us (0.961)
  waiting for transfers between devices: 10.8 us -> 9.23 us
    ppermute x10, waiting for transfers between devices: 10.8 us -> 9.23 us  [swapped(): return lax.ppermute(block, axes, [(i, i ^ distance) for i in range(count)])]
where the time goes in v5:
time: 32.4 us; the launch traced here: 32.3 us
  Pallas kernels  13.7 us (42%)
  starting transfers between devices  9.31 us (29%)
  waiting for transfers between devices  9.23 us (28%)
    pallas_call x1, Pallas kernels, channelize(): pl.pallas_call(functools.partial(channelize_kernel, chans, relative, mesh...  11.7 us
    ppermute x10, starting transfers between devices, swapped(): return lax.ppermute(block, axes, [(i, i ^ distance) for i in range(count)])  9.31 us
    ppermute x10, waiting for transfers between devices, swapped(): return lax.ppermute(block, axes, [(i, i ^ distance) for i in range(count)])  9.23 us
    pallas_call x1, Pallas kernels, correlate(): pl.pallas_call(functools.partial(correlate_kernel, mesh_shape, in_dev, fr...  1.99 us
  transfers between devices with their start and end apart: 10, of which 7 were waited for; matrix products, arithmetic and copies ran while one was open for 0% of the time, Pallas kernels for 0%

profile of v5, /device:TPU:0, one launch (start us, length us, event | category | flops | bytes accessed | tf_op | source)
XLA Modules:
  0.0 32.3 jit_solution(11402848149670745869)
XLA Ops:
  0.0 11.7 %channelize.1 = (bf16[2,72,128]{2,1,0:T(8,128)(2,1)S(1)}, bf16[2,72,128]{2,1,0:T(8,128)(2,1)S(1)}, bf16[2,72,128]{2,1,0:T(8,128)(2,1)S(1)}, bf16[2,72,128]{2,1,0:T(8,128)(2,1)S(1)}) custom-call(s32[1]{0:T(128)} %bitcast.me_ref, s32[8]{0:T(128)} %chan_hbm.1, s32[64,64,2048]{2,1,0:T(8,128)} %x_ref.1), custom_call_target="tpu_custom_call" | custom-call | tf_op jit(solution)/shard_map/channelize/pallas_call | solution.py:166
  11.7 4.1 %collective-permute-start = (bf16[2,72,128]{2,1,0:T(8,128)(2,1)S(1)}, bf16[2,72,128]{2,1,0:T(8,128)(2,1)S(1)}, u32[]{:S(2)}, u32[]{:S(2)}) collective-permute-start(bf16[2,72,128]{2,1,0:T(8,128)(2,1)S(1)} %get-tuple-element.10), channel_id=1, source_target_pairs={{0,16},{8,24},{16,0},{24,8},{1,17},{9,25},{17,1},{25,9},{2,18},{10... | collective-permute-start | bytes 110600 | tf_op jit(solution)/shard_map/ppermute | solution.py:315
  15.8 1.3 %collective-permute-start.1 = (bf16[2,72,128]{2,1,0:T(8,128)(2,1)S(1)}, bf16[2,72,128]{2,1,0:T(8,128)(2,1)S(1)}, u32[]{:S(2)}, u32[]{:S(2)}) collective-permute-start(bf16[2,72,128]{2,1,0:T(8,128)(2,1)S(1)} %get-tuple-element.11), channel_id=1, source_target_pairs={{0,24},{8,16},{16,8},{24,0},{1,25},{9,17},{17,9},{25,1},{2,26},{10... | collective-permute-start | bytes 110600 | tf_op jit(solution)/shard_map/ppermute | solution.py:315
  17.1 0.2 collective-permute-start.2
  17.4 0.8 %collective-permute-done = bf16[2,72,128]{2,1,0:T(8,128)(2,1)S(1)} collective-permute-done((bf16[2,72,128]{2,1,0:T(8,128)(2,1)S(1)}, bf16[2,72,128]{2,1,0:T(8,128)(2,1)S(1)}, u32[]{:S(2)}, u32[]{:S(2)}) %collective-permute-start) | collective-permute-done | bytes 36896 | tf_op jit(solution)/shard_map/ppermute | solution.py:315
  18.1 3.4 %collective-permute-done.1 = bf16[2,72,128]{2,1,0:T(8,128)(2,1)S(1)} collective-permute-done((bf16[2,72,128]{2,1,0:T(8,128)(2,1)S(1)}, bf16[2,72,128]{2,1,0:T(8,128)(2,1)S(1)}, u32[]{:S(2)}, u32[]{:S(2)}) %collective-permute-start.1) | collective-permute-done | bytes 36896 | tf_op jit(solution)/shard_map/ppermute | solution.py:315
  21.6 0.0 collective-permute-done.2
  21.6 1.6 %collective-permute-start.4 = (bf16[4,72,128]{2,1,0:T(8,128)(2,1)S(1)}, bf16[4,72,128]{2,1,0:T(8,128)(2,1)S(1)}, u32[]{:S(2)}, u32[]{:S(2)}) collective-permute-start(bf16[4,72,128]{2,1,0:T(8,128)(2,1)S(1)} %pad_maximum_fusion.refs_0_), channel_id=1, source_target_pairs={{0,2},{1,3},{2,0},{3,1},{4,6},{5,7},{6,4},{7,5},{8,10},{9,11},{10,... | collective-permute-start | bytes 221192 | tf_op jit(solution)/shard_map/ppermute | solution.py:315
  23.2 1.5 %collective-permute-start.8 = (bf16[4,72,128]{2,1,0:T(8,128)(2,1)S(1)}, bf16[4,72,128]{2,1,0:T(8,128)(2,1)S(1)}, u32[]{:S(2)}, u32[]{:S(2)}) collective-permute-start(bf16[4,72,128]{2,1,0:T(8,128)(2,1)S(1)} %pad_maximum_fusion.1), channel_id=1, source_target_pairs={{0,6},{1,7},{2,4},{3,5},{4,2},{5,3},{6,0},{7,1},{8,14},{9,15},{10,... | collective-permute-start | bytes 221192 | tf_op jit(solution)/shard_map/ppermute | solution.py:315
  24.7 0.5 %collective-permute-start.6 = (bf16[4,72,128]{2,1,0:T(8,128)(2,1)S(1)}, bf16[4,72,128]{2,1,0:T(8,128)(2,1)S(1)}, u32[]{:S(2)}, u32[]{:S(2)}) collective-permute-start(bf16[4,72,128]{2,1,0:T(8,128)(2,1)S(1)} %pad_maximum_fusion.1), channel_id=1, source_target_pairs={{0,4},{1,5},{2,6},{3,7},{4,0},{5,1},{6,2},{7,3},{8,12},{9,13},{10,... | collective-permute-start | bytes 221192 | tf_op jit(solution)/shard_map/ppermute | solution.py:315
  25.2 0.0 collective-permute-start.3
  25.2 1.2 %collective-permute-done.4.refs_2_ = bf16[4,72,128]{2,1,0:T(8,128)(2,1)S(1)} collective-permute-done((bf16[4,72,128]{2,1,0:T(8,128)(2,1)S(1)}, bf16[4,72,128]{2,1,0:T(8,128)(2,1)S(1)}, u32[]{:S(2)}, u32[]{:S(2)}) %collective-permute-start.4) | collective-permute-done | bytes 73760 | tf_op jit(solution)/shard_map/ppermute | solution.py:315
  26.4 0.0 collective-permute-start.5
  26.4 2.1 %collective-permute-done.8.refs_6_ = bf16[4,72,128]{2,1,0:T(8,128)(2,1)S(1)} collective-permute-done((bf16[4,72,128]{2,1,0:T(8,128)(2,1)S(1)}, bf16[4,72,128]{2,1,0:T(8,128)(2,1)S(1)}, u32[]{:S(2)}, u32[]{:S(2)}) %collective-permute-start.8) | collective-permute-done | bytes 73760 | tf_op jit(solution)/shard_map/ppermute | solution.py:315
  28.5 0.0 collective-permute-start.9
  28.5 0.5 %collective-permute-done.6.refs_4_ = bf16[4,72,128]{2,1,0:T(8,128)(2,1)S(1)} collective-permute-done((bf16[4,72,128]{2,1,0:T(8,128)(2,1)S(1)}, bf16[4,72,128]{2,1,0:T(8,128)(2,1)S(1)}, u32[]{:S(2)}, u32[]{:S(2)}) %collective-permute-start.6) | collective-permute-done | bytes 73760 | tf_op jit(solution)/shard_map/ppermute | solution.py:315
  29.0 0.0 collective-permute-start.7
  29.0 0.0 collective-permute-done.3.refs_1_
  29.0 0.0 collective-permute-done.5.refs_3_
  29.0 0.7 %collective-permute-done.9.refs_7_ = bf16[4,72,128]{2,1,0:T(8,128)(2,1)S(1)} collective-permute-done((bf16[4,72,128]{2,1,0:T(8,128)(2,1)S(1)}, bf16[4,72,128]{2,1,0:T(8,128)(2,1)S(1)}, u32[]{:S(2)}, u32[]{:S(2)}) %collective-permute-start.9) | collective-permute-done | bytes 73760 | tf_op jit(solution)/shard_map/ppermute | solution.py:315
  29.8 0.5 %collective-permute-done.7.refs_5_ = bf16[4,72,128]{2,1,0:T(8,128)(2,1)S(1)} collective-permute-done((bf16[4,72,128]{2,1,0:T(8,128)(2,1)S(1)}, bf16[4,72,128]{2,1,0:T(8,128)(2,1)S(1)}, u32[]{:S(2)}, u32[]{:S(2)}) %collective-permute-start.7) | collective-permute-done | bytes 73760 | tf_op jit(solution)/shard_map/ppermute | solution.py:315
  30.3 2.0 %correlate.1 = f32[1,1,2,512,512]{4,3,2,1,0:T(8,128)} custom-call(s32[1]{0:T(128)} %bitcast.me_ref, bf16[4,72,128]{2,1,0:T(8,128)(2,1)S(1)} %pad_maximum_fusion.refs_0_, bf16[4,72,128]{2,1,0:T(8,128)(2,1)S(1)} %collective-permute-done.3.refs_1_, bf16[4,72,128]{2,1,0:T(8,128)(2,1)S(1)} %collective-permute-done.4.refs_2_, ...), custom_call_target="tpu_custom_call" | custom-call | tf_op jit(solution)/shard_map/correlate/pallas_call | solution.py:273
  (6 shorter events, 0.0 us)
Async XLA Ops:
  11.7 6.4 %collective-permute-start = (bf16[2,72,128]{2,1,0:T(8,128)(2,1)S(1)}, bf16[2,72,128]{2,1,0:T(8,128)(2,1)S(1)}, u32[]{:S(2)}, u32[]{:S(2)}) collective-permute-start(bf16[2,72,128]{2,1,0:T(8,128)(2,1)S(1)} %get-tuple-element.10), channel_id=1, source_target_pairs={{0,16},{8,24},{16,0},{24,8},{1,17},{9,25},{17,1},{25,9},{2,18},{10... | collective-permute-start | bytes 110600 | tf_op jit(solution)/shard_map/ppermute | solution.py:315
  15.8 5.8 %collective-permute-start.1 = (bf16[2,72,128]{2,1,0:T(8,128)(2,1)S(1)}, bf16[2,72,128]{2,1,0:T(8,128)(2,1)S(1)}, u32[]{:S(2)}, u32[]{:S(2)}) collective-permute-start(bf16[2,72,128]{2,1,0:T(8,128)(2,1)S(1)} %get-tuple-element.11), channel_id=1, source_target_pairs={{0,24},{8,16},{16,8},{24,0},{1,25},{9,17},{17,9},{25,1},{2,26},{10... | collective-permute-start | bytes 110600 | tf_op jit(solution)/shard_map/ppermute | solution.py:315
  17.1 4.4 %collective-permute-start.2 = (bf16[2,72,128]{2,1,0:T(8,128)(2,1)S(1)}, bf16[2,72,128]{2,1,0:T(8,128)(2,1)S(1)}, u32[]{:S(2)}, u32[]{:S(2)}) collective-permute-start(bf16[2,72,128]{2,1,0:T(8,128)(2,1)S(1)} %get-tuple-element.12), channel_id=1, source_target_pairs={{0,8},{8,0},{16,24},{24,16},{1,9},{9,1},{17,25},{25,17},{2,10},{10... | collective-permute-start | bytes 110600 | tf_op jit(solution)/shard_map/ppermute | solution.py:315
  21.6 4.9 %collective-permute-start.4 = (bf16[4,72,128]{2,1,0:T(8,128)(2,1)S(1)}, bf16[4,72,128]{2,1,0:T(8,128)(2,1)S(1)}, u32[]{:S(2)}, u32[]{:S(2)}) collective-permute-start(bf16[4,72,128]{2,1,0:T(8,128)(2,1)S(1)} %pad_maximum_fusion.refs_0_), channel_id=1, source_target_pairs={{0,2},{1,3},{2,0},{3,1},{4,6},{5,7},{6,4},{7,5},{8,10},{9,11},{10,... | collective-permute-start | bytes 221192 | tf_op jit(solution)/shard_map/ppermute | solution.py:315
  23.2 5.3 %collective-permute-start.8 = (bf16[4,72,128]{2,1,0:T(8,128)(2,1)S(1)}, bf16[4,72,128]{2,1,0:T(8,128)(2,1)S(1)}, u32[]{:S(2)}, u32[]{:S(2)}) collective-permute-start(bf16[4,72,128]{2,1,0:T(8,128)(2,1)S(1)} %pad_maximum_fusion.1), channel_id=1, source_target_pairs={{0,6},{1,7},{2,4},{3,5},{4,2},{5,3},{6,0},{7,1},{8,14},{9,15},{10,... | collective-permute-start | bytes 221192 | tf_op jit(solution)/shard_map/ppermute | solution.py:315
  24.7 4.4 %collective-permute-start.6 = (bf16[4,72,128]{2,1,0:T(8,128)(2,1)S(1)}, bf16[4,72,128]{2,1,0:T(8,128)(2,1)S(1)}, u32[]{:S(2)}, u32[]{:S(2)}) collective-permute-start(bf16[4,72,128]{2,1,0:T(8,128)(2,1)S(1)} %pad_maximum_fusion.1), channel_id=1, source_target_pairs={{0,4},{1,5},{2,6},{3,7},{4,0},{5,1},{6,2},{7,3},{8,12},{9,13},{10,... | collective-permute-start | bytes 221192 | tf_op jit(solution)/shard_map/ppermute | solution.py:315
  25.2 3.8 %collective-permute-start.3 = (bf16[4,72,128]{2,1,0:T(8,128)(2,1)S(1)}, bf16[4,72,128]{2,1,0:T(8,128)(2,1)S(1)}, u32[]{:S(2)}, u32[]{:S(2)}) collective-permute-start(bf16[4,72,128]{2,1,0:T(8,128)(2,1)S(1)} %pad_maximum_fusion.refs_0_), channel_id=1, source_target_pairs={{0,1},{1,0},{2,3},{3,2},{4,5},{5,4},{6,7},{7,6},{8,9},{9,8},{10,11... | collective-permute-start | bytes 221192 | tf_op jit(solution)/shard_map/ppermute | solution.py:315
  26.4 2.6 %collective-permute-start.5 = (bf16[4,72,128]{2,1,0:T(8,128)(2,1)S(1)}, bf16[4,72,128]{2,1,0:T(8,128)(2,1)S(1)}, u32[]{:S(2)}, u32[]{:S(2)}) collective-permute-start(bf16[4,72,128]{2,1,0:T(8,128)(2,1)S(1)} %collective-permute-done.4.refs_2_), channel_id=1, source_target_pairs={{0,1},{1,0},{2,3},{3,2},{4,5},{5,4},{6,7},{7,6},{8,9},{9,8},{10,11... | collective-permute-start | bytes 221192 | tf_op jit(solution)/shard_map/ppermute | solution.py:315
  28.5 1.3 %collective-permute-start.9 = (bf16[4,72,128]{2,1,0:T(8,128)(2,1)S(1)}, bf16[4,72,128]{2,1,0:T(8,128)(2,1)S(1)}, u32[]{:S(2)}, u32[]{:S(2)}) collective-permute-start(bf16[4,72,128]{2,1,0:T(8,128)(2,1)S(1)} %collective-permute-done.8.refs_6_), channel_id=1, source_target_pairs={{0,1},{1,0},{2,3},{3,2},{4,5},{5,4},{6,7},{7,6},{8,9},{9,8},{10,11... | collective-permute-start | bytes 221192 | tf_op jit(solution)/shard_map/ppermute | solution.py:315
  29.0 1.3 %collective-permute-start.7 = (bf16[4,72,128]{2,1,0:T(8,128)(2,1)S(1)}, bf16[4,72,128]{2,1,0:T(8,128)(2,1)S(1)}, u32[]{:S(2)}, u32[]{:S(2)}) collective-permute-start(bf16[4,72,128]{2,1,0:T(8,128)(2,1)S(1)} %collective-permute-done.6.refs_4_), channel_id=1, source_target_pairs={{0,1},{1,0},{2,3},{3,2},{4,5},{5,4},{6,7},{7,6},{8,9},{9,8},{10,11... | collective-permute-start | bytes 221192 | tf_op jit(solution)/shard_map/ppermute | solution.py:315

commit v6 on v5

--- a/solution.py
+++ b/solution.py
@@ -14,7 +14,7 @@
 BANK = 16
 PIECES = 2
 NARROW = jnp.bfloat16
-ORDER = (0, 2, 3, 1)
+ORDER = (0, 1, 2, 3)
 
 
 def bin_column(chan_ref, chans):
@@ -46,17 +46,16 @@
         left = left - part.astype(jnp.float32)
 
 
-def shift_and_add(chans, in_dev, fr_dev, pair, raw, spec, carry):
+def shift_and_add(chans, in_dev, fr_dev, pair, part, spec, carry, keep):
     rows = 2 * chans
     lane = lax.broadcasted_iota(jnp.int32, (rows, LANES), 1)
     place = lane % fr_dev
     first = lax.broadcasted_iota(jnp.int32, (chans, LANES), 1) < fr_dev
-    span = slice(pair * LANES, (pair + 1) * LANES)
-    own = raw[(TAPS - 1) * rows :, span]
+    own = part[(TAPS - 1) * rows :]
     over = jnp.zeros_like(own)
     for k in range(TAPS - 1):
         late = TAPS - 1 - k
-        moved = pltpu.roll(raw[k * rows : (k + 1) * rows, span], late, 1)
+        moved = pltpu.roll(part[k * rows : (k + 1) * rows], late, 1)
         own = own + jnp.where(place >= late, moved, 0.0)
         over = over + jnp.where(place < late, moved, 0.0)
     re, im = own[:chans], own[chans:]
@@ -64,35 +63,31 @@
     odd = jnp.where(first, pltpu.roll(re, fr_dev, 1), im)
     spec[pl.ds(pair * 2, chans, stride=in_dev), :] = even
     spec[pl.ds(pair * 2 + 1, chans, stride=in_dev), :] = odd
-    bank, shift = pair // BANK, pair % BANK * TAPS
-    carry[bank] += pltpu.roll(over, shift, 1) if shift else over
-
-
-def channelize_kernel(chans, relative, mesh_shape, me_ref, chan_hbm, x_ref, *refs):
+    over = jnp.where(keep, pltpu.roll(over, pair % BANK * TAPS, 1), 0.0)
+    carry[pair // BANK] += over
+
+
+def channelize_kernel(chans, relative, mesh_shape, chan_hbm, x_ref, *refs):
     outs, refs = refs[: -9], refs[-9:]
     buf, w_ref, raw, spec, carry, edge, chan_ref, sems, chan_sem = refs
     in_dev, fr_dev, frame = x_ref.shape
     n_freq, n_tm, n_bl = mesh_shape
-    tail = (in_dev - 1) // GROUP * GROUP
-    groups = [(i, GROUP) for i in range(0, tail, GROUP)]
-    groups += [(i, 4) for i in range(tail, in_dev, 4)]
-
     def fetch(first, count, sem):
         span = pl.ds(first, count)
         return pltpu.make_async_copy(x_ref.at[span], buf.at[span], sems.at[sem])
 
     chan_copy = pltpu.make_async_copy(chan_hbm, chan_ref, chan_sem)
     chan_copy.start()
-    for g, (first, count) in enumerate(groups):
-        fetch(first, count, g).start()
+    for g in range(in_dev // GROUP):
+        fetch(g * GROUP, GROUP, g).start()
     chan_copy.wait()
     build_weights(chan_ref, w_ref, chans, frame)
     carry[...] = jnp.zeros_like(carry)
 
-    def multiply(first, count, sem):
-        fetch(first, count, sem).wait()
-        x = buf[pl.ds(first, count)].astype(jnp.float32) - 7.5
-        x = x.astype(NARROW).reshape(count * fr_dev, frame)
+    def multiply(g):
+        fetch(g * GROUP, GROUP, g).wait()
+        x = buf[pl.ds(g * GROUP, GROUP)].astype(jnp.float32) - 7.5
+        x = x.astype(NARROW).reshape(GROUP * fr_dev, frame)
         pieces = lax.dot_general(
             w_ref[...], x, (((1,), (1,)), ((), ())), preferred_element_type=jnp.float32
         )
@@ -100,20 +95,25 @@
         total = pieces[:rows]
         for piece in range(1, PIECES):
             total += pieces[piece * rows : (piece + 1) * rows]
-        at = first * fr_dev
-        if not isinstance(first, int):
-            at = pl.multiple_of(at, GROUP * fr_dev)
-        raw[:, pl.ds(at, count * fr_dev)] = total
+        return total
+
+    def finish(g, keep):
+        for i in range(GROUP // 2):
+            part = raw[g % 2, :, i * LANES : (i + 1) * LANES]
+            pair = g * (GROUP // 2) + i
+            shift_and_add(chans, in_dev, fr_dev, pair, part, spec, carry, keep)
 
     def step(g, _):
-        multiply(g * GROUP, GROUP, g)
+        total = multiply(g)
+        finish(jnp.maximum(g - 1, 0), g > 0)
+        raw[g % 2] = total
         return 0
 
     def slot(m):
         if not relative:
             return m
-        freq, tm = me_ref[0] // (n_tm * n_bl), me_ref[0] // n_bl % n_tm
-        return (freq ^ (m // n_tm)) * n_tm + (tm ^ (m % n_tm))
+        freq, tm = lax.axis_index("freq"), lax.axis_index("tm")
+        return label((label(freq) + m // n_tm) % n_freq) * n_tm + (tm ^ (m % n_tm))
 
     def emit(first, count):
         for m in range(chans):
@@ -124,22 +124,10 @@
             block = spec[pl.ds(at, count), :].astype(jnp.bfloat16)
             outs[m // per][m % per, first : first + count, :] = block
 
-    done = 0
-    while done < tail:
-        upto = min(done + 4 * GROUP, tail)
-        lax.fori_loop(done // GROUP, upto // GROUP, step, 0)
-        for pair in range(done // 2, upto // 2):
-            shift_and_add(chans, in_dev, fr_dev, pair, raw, spec, carry)
-        done = upto
-    early = tail // 16 * 16
-    if early:
-        emit(0, early)
-    for g, (first, count) in enumerate(groups):
-        if first >= tail:
-            multiply(first, count, g)
-            for pair in range(first // 2, (first + count) // 2):
-                shift_and_add(chans, in_dev, fr_dev, pair, raw, spec, carry)
-    emit(early, in_dev - early)
+    count = in_dev // GROUP
+    lax.fori_loop(0, count, step, 0)
+    finish(count - 1, True)
+    emit(0, in_dev)
     edge[...] = jnp.zeros_like(edge)
     for p in range(2):
         for bank in range(2):
@@ -166,7 +154,6 @@
     return pl.pallas_call(
         functools.partial(channelize_kernel, chans, relative, mesh_shape),
         in_specs=[
-            pl.BlockSpec(memory_space=pltpu.SMEM),
             pl.BlockSpec(memory_space=pltpu.HBM),
             pl.BlockSpec(memory_space=pltpu.HBM),
         ],
@@ -175,7 +162,7 @@
         scratch_shapes=[
             pltpu.VMEM(samples.shape, jnp.int32),
             pltpu.VMEM((PIECES * products, frame), NARROW),
-            pltpu.VMEM((products, in_dev * fr_dev), jnp.float32),
+            pltpu.VMEM((2, products, GROUP * fr_dev), jnp.float32),
             pltpu.VMEM((chans * in_dev, LANES), jnp.float32),
             pltpu.VMEM((2, 2 * chans, LANES), jnp.float32),
             pltpu.VMEM((chans * 8, LANES), jnp.float32),
@@ -185,7 +172,7 @@
         ],
         compiler_params=pltpu.CompilerParams(vmem_limit_bytes=48 * 2**20),
         name="channelize",
-    )(me, chan_index, samples)
+    )(chan_index, samples)
 
 
 def place_carry(carried, in_dev, fr_dev):
@@ -209,6 +196,10 @@
     )
 
 
+def label(z):
+    return z ^ (z // 2)
+
+
 def place_of(turn):
     at = jnp.int32(0)
     for place, k in enumerate(ORDER):
@@ -216,18 +207,17 @@
     return at
 
 
-def correlate_kernel(mesh_shape, in_dev, fr_dev, me_ref, *refs):
+def correlate_kernel(mesh_shape, in_dev, fr_dev, *refs):
     n_freq, n_tm, n_bl = mesh_shape
     own_half, other_half = refs[:n_bl], refs[n_bl : 2 * n_bl]
     o_ref, left, right, result, sems = refs[2 * n_bl :]
-    me = me_ref[0]
-    freq, tm, bl = me // (n_tm * n_bl), me // n_bl % n_tm, me % n_bl
+    freq, tm, bl = (lax.axis_index(axis) for axis in ("freq", "tm", "bl"))
     scale = 1.0 / (n_tm * fr_dev)
     order = [(f, k) for f in range(n_freq // 2) for k in range(n_bl)]
     for out, base in ((left, bl // 2 * (n_freq // 2)), (right, bl % 2 * (n_freq // 2))):
         early, late, carried = [], [], []
         for f, k in order:
-            at = place_of((base + f) ^ freq)
+            at = place_of((label(freq) - label(base + f) + n_freq) % n_freq)
             mine, other = own_half[k], other_half[k]
             body, over = slice(0, in_dev), slice(in_dev, in_dev + 4)
             early.append(jnp.where(tm == 0, mine[at, body, :], other[at, body, :]))
@@ -241,11 +231,12 @@
             out[pl.ds(at, in_dev), :LANES] = early[m]
             out[pl.ds(at, in_dev), LANES:] = late[m * in_dev : (m + 1) * in_dev]
     half = left.shape[0]
-    rows = half // sems.shape[0]
+    count = sems.shape[0] // 2
+    rows = half // count
     lane = lax.broadcasted_iota(jnp.int32, (rows, LANES), 1)
     dims = (((1,), (1,)), ((), ()))
     copies = []
-    for m in range(sems.shape[0]):
+    for m in range(count):
         span = pl.ds(m * rows, rows)
         mine = left[m * rows : (m + 1) * rows, :]
         turned = []
@@ -257,12 +248,10 @@
             result[p, m * rows : (m + 1) * rows, :] = scale * lax.dot_general(
                 a, right[...], dims, preferred_element_type=jnp.float32
             )
-        copies.append(
-            pltpu.make_async_copy(
-                result.at[:, span], o_ref.at[0, 0, :, span], sems.at[m]
+            copies.append(
+                pltpu.make_async_copy(result.at[p, span], o_ref.at[0, 0, p, span], sems.at[2 * m + p])
             )
-        )
-        copies[-1].start()
+            copies[-1].start()
     for copy in copies:
         copy.wait()
 
@@ -272,8 +261,7 @@
     half = n_freq * n_bl * in_dev // 2
     return pl.pallas_call(
         functools.partial(correlate_kernel, mesh_shape, in_dev, fr_dev),
-        in_specs=[pl.BlockSpec(memory_space=pltpu.SMEM)]
-        + [pl.BlockSpec(memory_space=pltpu.VMEM)] * len(sources),
+        in_specs=[pl.BlockSpec(memory_space=pltpu.VMEM)] * len(sources),
         out_specs=pl.BlockSpec(memory_space=pl.ANY),
         out_shape=jax.ShapeDtypeStruct((1, 1, 2, half, half), jnp.float32),
         scratch_shapes=[
@@ -284,7 +272,7 @@
         ],
         compiler_params=pltpu.CompilerParams(vmem_limit_bytes=16 * 2**20),
         name="correlate",
-    )(me, *sources)
+    )(*sources)
 
 
 def correlate_plain(gathered, where, n_freq, n_tm, in_dev, fr_dev):
@@ -318,7 +306,7 @@
 def exchange(parts, n_bl):
     arrived = [parts[0]] + [None] * (len(parts) - 1)
     for k in reversed(range(1, len(parts))):
-        arrived[k] = swapped(parts[k], ("freq",), k)
+        arrived[k] = lax.ppermute(parts[k], "freq", [(label(i), label((i + k) % len(parts))) for i in range(len(parts))])
     keep = jnp.stack([arrived[k][0] for k in ORDER])
     send = jnp.stack([arrived[k][1] for k in ORDER])
     across = ("tm", "bl")

time: 32.4 us -> 32 us (0.988)
  waiting for transfers between devices: 9.23 us -> 7.43 us
  starting transfers between devices: 9.31 us -> 10.8 us
    ppermute x0 -> x3, starting transfers between devices: none -> 7.13 us  [exchange(): lax.ppermute(parts[k], 'freq', [(label(i), label((i + k) % len(parts))) f...]
    ppermute x10 -> x7, starting transfers between devices: 9.31 us -> 3.63 us  [swapped(): return lax.ppermute(block, axes, [(i, i ^ distance) for i in range(count)])]
    ppermute x10 -> x7, waiting for transfers between devices: 9.23 us -> 5.07 us  [swapped(): return lax.ppermute(block, axes, [(i, i ^ distance) for i in range(count)])]
    ppermute x0 -> x3, waiting for transfers between devices: none -> 2.36 us  [exchange(): lax.ppermute(parts[k], 'freq', [(label(i), label((i + k) % len(parts))) f...]
where the time goes in v6:
time: 32 us; the launch traced here: 31.8 us
  Pallas kernels  13.6 us (42%)
  starting transfers between devices  10.8 us (34%)
  waiting for transfers between devices  7.43 us (23%)
    pallas_call x1, Pallas kernels, channelize(): pl.pallas_call(functools.partial(channelize_kernel, chans, relative, mesh...  11.6 us
    ppermute x3, starting transfers between devices, exchange(): lax.ppermute(parts[k], 'freq', [(label(i), label((i + k) % len(parts))) f...  7.13 us
    ppermute x7, waiting for transfers between devices, swapped(): return lax.ppermute(block, axes, [(i, i ^ distance) for i in range(count)])  5.07 us
    ppermute x7, starting transfers between devices, swapped(): return lax.ppermute(block, axes, [(i, i ^ distance) for i in range(count)])  3.63 us
    ppermute x3, waiting for transfers between devices, exchange(): lax.ppermute(parts[k], 'freq', [(label(i), label((i + k) % len(parts))) f...  2.36 us
    pallas_call x1, Pallas kernels, correlate(): pl.pallas_call(functools.partial(correlate_kernel, mesh_shape, in_dev, fr...  1.96 us
  transfers between devices with their start and end apart: 10, of which 7 were waited for; matrix products, arithmetic and copies ran while one was open for 0% of the time, Pallas kernels for 0%

profile of v6, /device:TPU:0, one launch (start us, length us, event | category | flops | bytes accessed | tf_op | source)
XLA Modules:
  0.0 31.8 jit_solution(17856030818025503622)
XLA Ops:
  0.0 11.6 %channelize.1 = (bf16[2,72,128]{2,1,0:T(8,128)(2,1)S(1)}, bf16[2,72,128]{2,1,0:T(8,128)(2,1)S(1)}, bf16[2,72,128]{2,1,0:T(8,128)(2,1)S(1)}, bf16[2,72,128]{2,1,0:T(8,128)(2,1)S(1)}) custom-call(s32[8]{0:T(128)} %chan_hbm.1, s32[64,64,2048]{2,1,0:T(8,128)} %x_ref.1), custom_call_target="tpu_custom_call" | custom-call | tf_op jit(solution)/shard_map/channelize/pallas_call | solution.py:154
  11.6 3.1 %collective-permute-start = (bf16[2,72,128]{2,1,0:T(8,128)(2,1)S(1)}, bf16[2,72,128]{2,1,0:T(8,128)(2,1)S(1)}, u32[]{:S(2)}, u32[]{:S(2)}) collective-permute-start(bf16[2,72,128]{2,1,0:T(8,128)(2,1)S(1)} %get-tuple-element.10), channel_id=1, source_target_pairs={{0,8},{8,24},{24,16},{16,0},{1,9},{9,25},{25,17},{17,1},{2,10},{10... | collective-permute-start | bytes 110600 | tf_op jit(solution)/shard_map/ppermute | solution.py:309
  14.7 2.5 %collective-permute-start.1 = (bf16[2,72,128]{2,1,0:T(8,128)(2,1)S(1)}, bf16[2,72,128]{2,1,0:T(8,128)(2,1)S(1)}, u32[]{:S(2)}, u32[]{:S(2)}) collective-permute-start(bf16[2,72,128]{2,1,0:T(8,128)(2,1)S(1)} %get-tuple-element.11), channel_id=1, source_target_pairs={{0,24},{8,16},{24,0},{16,8},{1,25},{9,17},{25,1},{17,9},{2,26},{10... | collective-permute-start | bytes 110600 | tf_op jit(solution)/shard_map/ppermute | solution.py:309
  17.1 1.6 %collective-permute-start.2 = (bf16[2,72,128]{2,1,0:T(8,128)(2,1)S(1)}, bf16[2,72,128]{2,1,0:T(8,128)(2,1)S(1)}, u32[]{:S(2)}, u32[]{:S(2)}) collective-permute-start(bf16[2,72,128]{2,1,0:T(8,128)(2,1)S(1)} %get-tuple-element.12), channel_id=1, source_target_pairs={{0,16},{8,0},{24,8},{16,24},{1,17},{9,1},{25,9},{17,25},{2,18},{10... | collective-permute-start | bytes 110600 | tf_op jit(solution)/shard_map/ppermute | solution.py:309
  18.7 0.0 collective-permute-done
  18.7 1.8 %collective-permute-done.1 = bf16[2,72,128]{2,1,0:T(8,128)(2,1)S(1)} collective-permute-done((bf16[2,72,128]{2,1,0:T(8,128)(2,1)S(1)}, bf16[2,72,128]{2,1,0:T(8,128)(2,1)S(1)}, u32[]{:S(2)}, u32[]{:S(2)}) %collective-permute-start.1) | collective-permute-done | bytes 36896 | tf_op jit(solution)/shard_map/ppermute | solution.py:309
  20.6 0.5 %collective-permute-done.2 = bf16[2,72,128]{2,1,0:T(8,128)(2,1)S(1)} collective-permute-done((bf16[2,72,128]{2,1,0:T(8,128)(2,1)S(1)}, bf16[2,72,128]{2,1,0:T(8,128)(2,1)S(1)}, u32[]{:S(2)}, u32[]{:S(2)}) %collective-permute-start.2) | collective-permute-done | bytes 36896 | tf_op jit(solution)/shard_map/ppermute | solution.py:309
  21.1 1.6 %collective-permute-start.4 = (bf16[4,72,128]{2,1,0:T(8,128)(2,1)S(1)}, bf16[4,72,128]{2,1,0:T(8,128)(2,1)S(1)}, u32[]{:S(2)}, u32[]{:S(2)}) collective-permute-start(bf16[4,72,128]{2,1,0:T(8,128)(2,1)S(1)} %pad_maximum_fusion.refs_0_), channel_id=1, source_target_pairs={{0,2},{1,3},{2,0},{3,1},{4,6},{5,7},{6,4},{7,5},{8,10},{9,11},{10,... | collective-permute-start | bytes 221192 | tf_op jit(solution)/shard_map/ppermute | solution.py:303
  22.7 1.5 %collective-permute-start.8 = (bf16[4,72,128]{2,1,0:T(8,128)(2,1)S(1)}, bf16[4,72,128]{2,1,0:T(8,128)(2,1)S(1)}, u32[]{:S(2)}, u32[]{:S(2)}) collective-permute-start(bf16[4,72,128]{2,1,0:T(8,128)(2,1)S(1)} %pad_maximum_fusion.1), channel_id=1, source_target_pairs={{0,6},{1,7},{2,4},{3,5},{4,2},{5,3},{6,0},{7,1},{8,14},{9,15},{10,... | collective-permute-start | bytes 221192 | tf_op jit(solution)/shard_map/ppermute | solution.py:303
  24.2 0.5 %collective-permute-start.6 = (bf16[4,72,128]{2,1,0:T(8,128)(2,1)S(1)}, bf16[4,72,128]{2,1,0:T(8,128)(2,1)S(1)}, u32[]{:S(2)}, u32[]{:S(2)}) collective-permute-start(bf16[4,72,128]{2,1,0:T(8,128)(2,1)S(1)} %pad_maximum_fusion.1), channel_id=1, source_target_pairs={{0,4},{1,5},{2,6},{3,7},{4,0},{5,1},{6,2},{7,3},{8,12},{9,13},{10,... | collective-permute-start | bytes 221192 | tf_op jit(solution)/shard_map/ppermute | solution.py:303
  24.8 0.0 collective-permute-start.3
  24.8 1.1 %collective-permute-done.4.refs_2_ = bf16[4,72,128]{2,1,0:T(8,128)(2,1)S(1)} collective-permute-done((bf16[4,72,128]{2,1,0:T(8,128)(2,1)S(1)}, bf16[4,72,128]{2,1,0:T(8,128)(2,1)S(1)}, u32[]{:S(2)}, u32[]{:S(2)}) %collective-permute-start.4) | collective-permute-done | bytes 73760 | tf_op jit(solution)/shard_map/ppermute | solution.py:303
  25.9 0.0 collective-permute-start.5
  25.9 2.2 %collective-permute-done.8.refs_6_ = bf16[4,72,128]{2,1,0:T(8,128)(2,1)S(1)} collective-permute-done((bf16[4,72,128]{2,1,0:T(8,128)(2,1)S(1)}, bf16[4,72,128]{2,1,0:T(8,128)(2,1)S(1)}, u32[]{:S(2)}, u32[]{:S(2)}) %collective-permute-start.8) | collective-permute-done | bytes 73760 | tf_op jit(solution)/shard_map/ppermute | solution.py:303
  28.1 0.0 collective-permute-start.9
  28.1 0.5 %collective-permute-done.6.refs_4_ = bf16[4,72,128]{2,1,0:T(8,128)(2,1)S(1)} collective-permute-done((bf16[4,72,128]{2,1,0:T(8,128)(2,1)S(1)}, bf16[4,72,128]{2,1,0:T(8,128)(2,1)S(1)}, u32[]{:S(2)}, u32[]{:S(2)}) %collective-permute-start.6) | collective-permute-done | bytes 73760 | tf_op jit(solution)/shard_map/ppermute | solution.py:303
  28.6 0.0 collective-permute-start.7
  28.6 0.0 collective-permute-done.3.refs_1_
  28.6 0.0 collective-permute-done.5.refs_3_
  28.6 0.7 %collective-permute-done.9.refs_7_ = bf16[4,72,128]{2,1,0:T(8,128)(2,1)S(1)} collective-permute-done((bf16[4,72,128]{2,1,0:T(8,128)(2,1)S(1)}, bf16[4,72,128]{2,1,0:T(8,128)(2,1)S(1)}, u32[]{:S(2)}, u32[]{:S(2)}) %collective-permute-start.9) | collective-permute-done | bytes 73760 | tf_op jit(solution)/shard_map/ppermute | solution.py:303
  29.3 0.5 %collective-permute-done.7.refs_5_ = bf16[4,72,128]{2,1,0:T(8,128)(2,1)S(1)} collective-permute-done((bf16[4,72,128]{2,1,0:T(8,128)(2,1)S(1)}, bf16[4,72,128]{2,1,0:T(8,128)(2,1)S(1)}, u32[]{:S(2)}, u32[]{:S(2)}) %collective-permute-start.7) | collective-permute-done | bytes 73760 | tf_op jit(solution)/shard_map/ppermute | solution.py:303
  29.9 2.0 %correlate.1 = f32[1,1,2,512,512]{4,3,2,1,0:T(8,128)} custom-call(bf16[4,72,128]{2,1,0:T(8,128)(2,1)S(1)} %pad_maximum_fusion.refs_0_, bf16[4,72,128]{2,1,0:T(8,128)(2,1)S(1)} %collective-permute-done.3.refs_1_, bf16[4,72,128]{2,1,0:T(8,128)(2,1)S(1)} %collective-permute-done.4.refs_2_, bf16[4,72,128]{2,1,0:T(8,128)(2,1)S(1)} %collective-permute-done.5.refs_3_, ...), custom_call_target="tpu_custom_call" | custom-call | tf_op jit(solution)/shard_map/correlate/pallas_call | solution.py:262
  (6 shorter events, 0.0 us)
Async XLA Ops:
  11.6 7.1 %collective-permute-start = (bf16[2,72,128]{2,1,0:T(8,128)(2,1)S(1)}, bf16[2,72,128]{2,1,0:T(8,128)(2,1)S(1)}, u32[]{:S(2)}, u32[]{:S(2)}) collective-permute-start(bf16[2,72,128]{2,1,0:T(8,128)(2,1)S(1)} %get-tuple-element.10), channel_id=1, source_target_pairs={{0,8},{8,24},{24,16},{16,0},{1,9},{9,25},{25,17},{17,1},{2,10},{10... | collective-permute-start | bytes 110600 | tf_op jit(solution)/shard_map/ppermute | solution.py:309
  14.7 5.9 %collective-permute-start.1 = (bf16[2,72,128]{2,1,0:T(8,128)(2,1)S(1)}, bf16[2,72,128]{2,1,0:T(8,128)(2,1)S(1)}, u32[]{:S(2)}, u32[]{:S(2)}) collective-permute-start(bf16[2,72,128]{2,1,0:T(8,128)(2,1)S(1)} %get-tuple-element.11), channel_id=1, source_target_pairs={{0,24},{8,16},{24,0},{16,8},{1,25},{9,17},{25,1},{17,9},{2,26},{10... | collective-permute-start | bytes 110600 | tf_op jit(solution)/shard_map/ppermute | solution.py:309
  17.1 4.0 %collective-permute-start.2 = (bf16[2,72,128]{2,1,0:T(8,128)(2,1)S(1)}, bf16[2,72,128]{2,1,0:T(8,128)(2,1)S(1)}, u32[]{:S(2)}, u32[]{:S(2)}) collective-permute-start(bf16[2,72,128]{2,1,0:T(8,128)(2,1)S(1)} %get-tuple-element.12), channel_id=1, source_target_pairs={{0,16},{8,0},{24,8},{16,24},{1,17},{9,1},{25,9},{17,25},{2,18},{10... | collective-permute-start | bytes 110600 | tf_op jit(solution)/shard_map/ppermute | solution.py:309
  21.1 4.7 %collective-permute-start.4 = (bf16[4,72,128]{2,1,0:T(8,128)(2,1)S(1)}, bf16[4,72,128]{2,1,0:T(8,128)(2,1)S(1)}, u32[]{:S(2)}, u32[]{:S(2)}) collective-permute-start(bf16[4,72,128]{2,1,0:T(8,128)(2,1)S(1)} %pad_maximum_fusion.refs_0_), channel_id=1, source_target_pairs={{0,2},{1,3},{2,0},{3,1},{4,6},{5,7},{6,4},{7,5},{8,10},{9,11},{10,... | collective-permute-start | bytes 221192 | tf_op jit(solution)/shard_map/ppermute | solution.py:303
  22.7 5.3 %collective-permute-start.8 = (bf16[4,72,128]{2,1,0:T(8,128)(2,1)S(1)}, bf16[4,72,128]{2,1,0:T(8,128)(2,1)S(1)}, u32[]{:S(2)}, u32[]{:S(2)}) collective-permute-start(bf16[4,72,128]{2,1,0:T(8,128)(2,1)S(1)} %pad_maximum_fusion.1), channel_id=1, source_target_pairs={{0,6},{1,7},{2,4},{3,5},{4,2},{5,3},{6,0},{7,1},{8,14},{9,15},{10,... | collective-permute-start | bytes 221192 | tf_op jit(solution)/shard_map/ppermute | solution.py:303
  24.2 4.4 %collective-permute-start.6 = (bf16[4,72,128]{2,1,0:T(8,128)(2,1)S(1)}, bf16[4,72,128]{2,1,0:T(8,128)(2,1)S(1)}, u32[]{:S(2)}, u32[]{:S(2)}) collective-permute-start(bf16[4,72,128]{2,1,0:T(8,128)(2,1)S(1)} %pad_maximum_fusion.1), channel_id=1, source_target_pairs={{0,4},{1,5},{2,6},{3,7},{4,0},{5,1},{6,2},{7,3},{8,12},{9,13},{10,... | collective-permute-start | bytes 221192 | tf_op jit(solution)/shard_map/ppermute | solution.py:303
  24.8 3.8 %collective-permute-start.3 = (bf16[4,72,128]{2,1,0:T(8,128)(2,1)S(1)}, bf16[4,72,128]{2,1,0:T(8,128)(2,1)S(1)}, u32[]{:S(2)}, u32[]{:S(2)}) collective-permute-start(bf16[4,72,128]{2,1,0:T(8,128)(2,1)S(1)} %pad_maximum_fusion.refs_0_), channel_id=1, source_target_pairs={{0,1},{1,0},{2,3},{3,2},{4,5},{5,4},{6,7},{7,6},{8,9},{9,8},{10,11... | collective-permute-start | bytes 221192 | tf_op jit(solution)/shard_map/ppermute | solution.py:303
  25.9 2.7 %collective-permute-start.5 = (bf16[4,72,128]{2,1,0:T(8,128)(2,1)S(1)}, bf16[4,72,128]{2,1,0:T(8,128)(2,1)S(1)}, u32[]{:S(2)}, u32[]{:S(2)}) collective-permute-start(bf16[4,72,128]{2,1,0:T(8,128)(2,1)S(1)} %collective-permute-done.4.refs_2_), channel_id=1, source_target_pairs={{0,1},{1,0},{2,3},{3,2},{4,5},{5,4},{6,7},{7,6},{8,9},{9,8},{10,11... | collective-permute-start | bytes 221192 | tf_op jit(solution)/shard_map/ppermute | solution.py:303
  28.1 1.3 %collective-permute-start.9 = (bf16[4,72,128]{2,1,0:T(8,128)(2,1)S(1)}, bf16[4,72,128]{2,1,0:T(8,128)(2,1)S(1)}, u32[]{:S(2)}, u32[]{:S(2)}) collective-permute-start(bf16[4,72,128]{2,1,0:T(8,128)(2,1)S(1)} %collective-permute-done.8.refs_6_), channel_id=1, source_target_pairs={{0,1},{1,0},{2,3},{3,2},{4,5},{5,4},{6,7},{7,6},{8,9},{9,8},{10,11... | collective-permute-start | bytes 221192 | tf_op jit(solution)/shard_map/ppermute | solution.py:303
  28.6 1.3 %collective-permute-start.7 = (bf16[4,72,128]{2,1,0:T(8,128)(2,1)S(1)}, bf16[4,72,128]{2,1,0:T(8,128)(2,1)S(1)}, u32[]{:S(2)}, u32[]{:S(2)}) collective-permute-start(bf16[4,72,128]{2,1,0:T(8,128)(2,1)S(1)} %collective-permute-done.6.refs_4_), channel_id=1, source_target_pairs={{0,1},{1,0},{2,3},{3,2},{4,5},{5,4},{6,7},{7,6},{8,9},{9,8},{10,11... | collective-permute-start | bytes 221192 | tf_op jit(solution)/shard_map/ppermute | solution.py:303

commit v7 on v6

--- a/solution.py
+++ b/solution.py
@@ -163,9 +163,9 @@
             pltpu.VMEM(samples.shape, jnp.int32),
             pltpu.VMEM((PIECES * products, frame), NARROW),
             pltpu.VMEM((2, products, GROUP * fr_dev), jnp.float32),
-            pltpu.VMEM((chans * in_dev, LANES), jnp.float32),
+            pltpu.VMEM(((chans + 1) * in_dev, LANES), jnp.float32),
             pltpu.VMEM((2, 2 * chans, LANES), jnp.float32),
-            pltpu.VMEM((chans * 8, LANES), jnp.float32),
+            pltpu.VMEM(((chans + 1) * 8, LANES), jnp.float32),
             pltpu.SMEM((chans,), jnp.int32),
             pltpu.SemaphoreType.DMA((in_dev // 2,)),
             pltpu.SemaphoreType.DMA,
@@ -197,7 +197,7 @@
 
 
 def label(z):
-    return z ^ (z // 2)
+    return z + 0
 
 
 def place_of(turn):
@@ -215,10 +215,11 @@
     scale = 1.0 / (n_tm * fr_dev)
     order = [(f, k) for f in range(n_freq // 2) for k in range(n_bl)]
     for out, base in ((left, bl // 2 * (n_freq // 2)), (right, bl % 2 * (n_freq // 2))):
-        early, late, carried = [], [], []
+        early, late, carried, core = [], [], [], []
         for f, k in order:
             at = place_of((label(freq) - label(base + f) + n_freq) % n_freq)
             mine, other = own_half[k], other_half[k]
+            core.append(jnp.where(at == 0, 0, 1))
             body, over = slice(0, in_dev), slice(in_dev, in_dev + 4)
             early.append(jnp.where(tm == 0, mine[at, body, :], other[at, body, :]))
             late.append(jnp.where(tm == 0, other[at, body, :], mine[at, body, :]))
@@ -227,7 +228,7 @@
         late = jnp.concatenate(late, axis=0).astype(jnp.float32)
         late = (late + place_carry(carried, in_dev, fr_dev)).astype(jnp.bfloat16)
         for m, (f, k) in enumerate(order):
-            at = pl.multiple_of((f * n_bl + (bl ^ k)) * in_dev, in_dev)
+            at = pl.multiple_of((f * n_bl + (bl ^ k ^ core[m])) * in_dev, in_dev)
             out[pl.ds(at, in_dev), :LANES] = early[m]
             out[pl.ds(at, in_dev), LANES:] = late[m * in_dev : (m + 1) * in_dev]
     half = left.shape[0]
@@ -303,20 +304,24 @@
     return lax.ppermute(block, axes, [(i, i ^ distance) for i in range(count)])
 
 
-def exchange(parts, n_bl):
+def exchange(parts, n_tm, n_bl):
+    across, plane = ("tm", "bl"), n_tm * n_bl
     arrived = [parts[0]] + [None] * (len(parts) - 1)
     for k in reversed(range(1, len(parts))):
-        arrived[k] = lax.ppermute(parts[k], "freq", [(label(i), label((i + k) % len(parts))) for i in range(len(parts))])
+        route = []
+        for z in range(len(parts)):
+            for i in range(plane):
+                to = label((label(z) + k) % len(parts))
+                route.append((z * plane + i, to * plane + (i ^ 1)))
+        arrived[k] = lax.ppermute(parts[k], ("freq",) + across, route)
     keep = jnp.stack([arrived[k][0] for k in ORDER])
     send = jnp.stack([arrived[k][1] for k in ORDER])
-    across = ("tm", "bl")
-    corner = swapped(send, across, n_bl + 2)
-    beside = swapped(send, across, n_bl)
-    far = swapped(keep, across, 2)
-    own_half, other_half = [keep, None, far, None], [beside, None, corner, None]
-    for half in (own_half, other_half):
-        for k in (0, 2):
-            half[k + 1] = swapped(half[k], ("bl",), 1)
+    corner = swapped(send, across, n_bl + 3)
+    beside = swapped(send, across, n_bl + 1)
+    far = swapped(keep, across, 3)
+    turn = lambda block: swapped(block, ("bl",), 1)
+    own_half = [keep, turn(keep), turn(far), far]
+    other_half = [turn(beside), beside, turn(corner), corner]
     return own_half + other_half
 
 
@@ -329,7 +334,7 @@
     relative = in_dev % 16 == 0 and n_freq <= 4 and n_tm == 2 and n_bl == 4
     spectra = channelize(samples, chan_index, me, relative, mesh_shape)
     if relative:
-        sources = exchange(spectra, n_bl)
+        sources = exchange(spectra, n_tm, n_bl)
         return correlate(sources, me, mesh_shape, in_dev, fr_dev)
     moved = lax.all_to_all(spectra[0], ("freq", "tm"), split_axis=0, concat_axis=0, tiled=True)
     gathered = lax.all_gather(moved, "bl", axis=0, tiled=False)

time: 32 us -> 31.5 us (0.984)
  starting transfers between devices: 10.8 us -> 10.2 us
    ppermute x3, starting transfers between devices: 7.13 us -> 6.17 us  [exchange(): arrived[k] = lax.ppermute(parts[k], ('freq',) + across, route)]
    ppermute x3, waiting for transfers between devices: 2.36 us -> 3.03 us  [exchange(): arrived[k] = lax.ppermute(parts[k], ('freq',) + across, route)]
    ppermute x7, waiting for transfers between devices: 5.07 us -> 4.57 us  [swapped(): return lax.ppermute(block, axes, [(i, i ^ distance) for i in range(count)])]
    ppermute x7, starting transfers between devices: 3.63 us -> 4.04 us  [swapped(): return lax.ppermute(block, axes, [(i, i ^ distance) for i in range(count)])]
where the time goes in v7:
time: 31.5 us; the launch traced here: 31.4 us
  Pallas kernels  13.5 us (43%)
  starting transfers between devices  10.2 us (32%)
  waiting for transfers between devices  7.6 us (24%)
    pallas_call x1, Pallas kernels, channelize(): pl.pallas_call(functools.partial(channelize_kernel, chans, relative, mesh...  11.6 us
    ppermute x3, starting transfers between devices, exchange(): arrived[k] = lax.ppermute(parts[k], ('freq',) + across, route)  6.17 us
    ppermute x7, waiting for transfers between devices, swapped(): return lax.ppermute(block, axes, [(i, i ^ distance) for i in range(count)])  4.57 us
    ppermute x7, starting transfers between devices, swapped(): return lax.ppermute(block, axes, [(i, i ^ distance) for i in range(count)])  4.04 us
    ppermute x3, waiting for transfers between devices, exchange(): arrived[k] = lax.ppermute(parts[k], ('freq',) + across, route)  3.03 us
    pallas_call x1, Pallas kernels, correlate(): pl.pallas_call(functools.partial(correlate_kernel, mesh_shape, in_dev, fr...  1.93 us
  transfers between devices with their start and end apart: 10, of which 7 were waited for; matrix products, arithmetic and copies ran while one was open for 0% of the time, Pallas kernels for 0%

profile of v7, /device:TPU:0, one launch (start us, length us, event | category | flops | bytes accessed | tf_op | source)
XLA Modules:
  0.0 31.4 jit_solution(14120588242770362848)
XLA Ops:
  0.0 11.6 %channelize.1 = (bf16[2,72,128]{2,1,0:T(8,128)(2,1)S(1)}, bf16[2,72,128]{2,1,0:T(8,128)(2,1)S(1)}, bf16[2,72,128]{2,1,0:T(8,128)(2,1)S(1)}, bf16[2,72,128]{2,1,0:T(8,128)(2,1)S(1)}) custom-call(s32[8]{0:T(128)} %chan_hbm.1, s32[64,64,2048]{2,1,0:T(8,128)} %x_ref.1), custom_call_target="tpu_custom_call" | custom-call | tf_op jit(solution)/shard_map/channelize/pallas_call | solution.py:154
  11.6 2.5 %collective-permute-start = (bf16[2,72,128]{2,1,0:T(8,128)(2,1)S(1)}, bf16[2,72,128]{2,1,0:T(8,128)(2,1)S(1)}, u32[]{:S(2)}, u32[]{:S(2)}) collective-permute-start(bf16[2,72,128]{2,1,0:T(8,128)(2,1)S(1)} %get-tuple-element.10), channel_id=1, source_target_pairs={{0,9},{1,8},{2,11},{3,10},{4,13},{5,12},{6,15},{7,14},{8,17},{9,16... | collective-permute-start | bytes 110600 | tf_op jit(solution)/shard_map/ppermute | solution.py:316
  14.1 2.9 %collective-permute-start.1 = (bf16[2,72,128]{2,1,0:T(8,128)(2,1)S(1)}, bf16[2,72,128]{2,1,0:T(8,128)(2,1)S(1)}, u32[]{:S(2)}, u32[]{:S(2)}) collective-permute-start(bf16[2,72,128]{2,1,0:T(8,128)(2,1)S(1)} %get-tuple-element.11), channel_id=1, source_target_pairs={{0,17},{1,16},{2,19},{3,18},{4,21},{5,20},{6,23},{7,22},{8,25},{9,... | collective-permute-start | bytes 110600 | tf_op jit(solution)/shard_map/ppermute | solution.py:316
  17.0 0.8 %collective-permute-start.2 = (bf16[2,72,128]{2,1,0:T(8,128)(2,1)S(1)}, bf16[2,72,128]{2,1,0:T(8,128)(2,1)S(1)}, u32[]{:S(2)}, u32[]{:S(2)}) collective-permute-start(bf16[2,72,128]{2,1,0:T(8,128)(2,1)S(1)} %get-tuple-element.12), channel_id=1, source_target_pairs={{0,25},{1,24},{2,27},{3,26},{4,29},{5,28},{6,31},{7,30},{8,1},{9,0... | collective-permute-start | bytes 110600 | tf_op jit(solution)/shard_map/ppermute | solution.py:316
  17.8 0.0 collective-permute-done
  17.8 1.8 %collective-permute-done.1 = bf16[2,72,128]{2,1,0:T(8,128)(2,1)S(1)} collective-permute-done((bf16[2,72,128]{2,1,0:T(8,128)(2,1)S(1)}, bf16[2,72,128]{2,1,0:T(8,128)(2,1)S(1)}, u32[]{:S(2)}, u32[]{:S(2)}) %collective-permute-start.1) | collective-permute-done | bytes 36896 | tf_op jit(solution)/shard_map/ppermute | solution.py:316
  19.6 1.2 %collective-permute-done.2 = bf16[2,72,128]{2,1,0:T(8,128)(2,1)S(1)} collective-permute-done((bf16[2,72,128]{2,1,0:T(8,128)(2,1)S(1)}, bf16[2,72,128]{2,1,0:T(8,128)(2,1)S(1)}, u32[]{:S(2)}, u32[]{:S(2)}) %collective-permute-start.2) | collective-permute-done | bytes 36896 | tf_op jit(solution)/shard_map/ppermute | solution.py:316
  20.8 1.3 %collective-permute-start.4 = (bf16[4,72,128]{2,1,0:T(8,128)(2,1)S(1)}, bf16[4,72,128]{2,1,0:T(8,128)(2,1)S(1)}, u32[]{:S(2)}, u32[]{:S(2)}) collective-permute-start(bf16[4,72,128]{2,1,0:T(8,128)(2,1)S(1)} %pad_maximum_fusion.refs_0_), channel_id=1, source_target_pairs={{0,3},{1,2},{2,1},{3,0},{4,7},{5,6},{6,5},{7,4},{8,11},{9,10},{10,... | collective-permute-start | bytes 221192 | tf_op jit(solution)/shard_map/ppermute | solution.py:304
  22.2 1.5 %collective-permute-start.8 = (bf16[4,72,128]{2,1,0:T(8,128)(2,1)S(1)}, bf16[4,72,128]{2,1,0:T(8,128)(2,1)S(1)}, u32[]{:S(2)}, u32[]{:S(2)}) collective-permute-start(bf16[4,72,128]{2,1,0:T(8,128)(2,1)S(1)} %pad_maximum_fusion.1), channel_id=1, source_target_pairs={{0,7},{1,6},{2,5},{3,4},{4,3},{5,2},{6,1},{7,0},{8,15},{9,14},{10,... | collective-permute-start | bytes 221192 | tf_op jit(solution)/shard_map/ppermute | solution.py:304
  23.7 0.2 collective-permute-start.6
  23.9 0.4 %collective-permute-start.3 = (bf16[4,72,128]{2,1,0:T(8,128)(2,1)S(1)}, bf16[4,72,128]{2,1,0:T(8,128)(2,1)S(1)}, u32[]{:S(2)}, u32[]{:S(2)}) collective-permute-start(bf16[4,72,128]{2,1,0:T(8,128)(2,1)S(1)} %pad_maximum_fusion.refs_0_), channel_id=1, source_target_pairs={{0,1},{1,0},{2,3},{3,2},{4,5},{5,4},{6,7},{7,6},{8,9},{9,8},{10,11... | collective-permute-start | bytes 221192 | tf_op jit(solution)/shard_map/ppermute | solution.py:304
  24.3 1.8 %collective-permute-done.4.refs_3_ = bf16[4,72,128]{2,1,0:T(8,128)(2,1)S(1)} collective-permute-done((bf16[4,72,128]{2,1,0:T(8,128)(2,1)S(1)}, bf16[4,72,128]{2,1,0:T(8,128)(2,1)S(1)}, u32[]{:S(2)}, u32[]{:S(2)}) %collective-permute-start.4) | collective-permute-done | bytes 73760 | tf_op jit(solution)/shard_map/ppermute | solution.py:304
  26.1 0.0 collective-permute-start.5
  26.1 1.0 %collective-permute-done.8.refs_7_ = bf16[4,72,128]{2,1,0:T(8,128)(2,1)S(1)} collective-permute-done((bf16[4,72,128]{2,1,0:T(8,128)(2,1)S(1)}, bf16[4,72,128]{2,1,0:T(8,128)(2,1)S(1)}, u32[]{:S(2)}, u32[]{:S(2)}) %collective-permute-start.8) | collective-permute-done | bytes 73760 | tf_op jit(solution)/shard_map/ppermute | solution.py:304
  27.1 0.4 %collective-permute-start.9 = (bf16[4,72,128]{2,1,0:T(8,128)(2,1)S(1)}, bf16[4,72,128]{2,1,0:T(8,128)(2,1)S(1)}, u32[]{:S(2)}, u32[]{:S(2)}) collective-permute-start(bf16[4,72,128]{2,1,0:T(8,128)(2,1)S(1)} %collective-permute-done.8.refs_7_), channel_id=1, source_target_pairs={{0,1},{1,0},{2,3},{3,2},{4,5},{5,4},{6,7},{7,6},{8,9},{9,8},{10,11... | collective-permute-start | bytes 221192 | tf_op jit(solution)/shard_map/ppermute | solution.py:304
  27.6 0.6 %collective-permute-done.6.refs_5_ = bf16[4,72,128]{2,1,0:T(8,128)(2,1)S(1)} collective-permute-done((bf16[4,72,128]{2,1,0:T(8,128)(2,1)S(1)}, bf16[4,72,128]{2,1,0:T(8,128)(2,1)S(1)}, u32[]{:S(2)}, u32[]{:S(2)}) %collective-permute-start.6) | collective-permute-done | bytes 73760 | tf_op jit(solution)/shard_map/ppermute | solution.py:304
  28.2 0.1 collective-permute-start.7
  28.3 0.0 collective-permute-done.3.refs_1_
  28.3 0.0 collective-permute-done.5.refs_2_
  28.3 0.2 collective-permute-done.9.refs_6_
  28.5 1.0 %collective-permute-done.7.refs_4_ = bf16[4,72,128]{2,1,0:T(8,128)(2,1)S(1)} collective-permute-done((bf16[4,72,128]{2,1,0:T(8,128)(2,1)S(1)}, bf16[4,72,128]{2,1,0:T(8,128)(2,1)S(1)}, u32[]{:S(2)}, u32[]{:S(2)}) %collective-permute-start.7) | collective-permute-done | bytes 73760 | tf_op jit(solution)/shard_map/ppermute | solution.py:304
  29.5 1.9 %correlate.1 = f32[1,1,2,512,512]{4,3,2,1,0:T(8,128)} custom-call(bf16[4,72,128]{2,1,0:T(8,128)(2,1)S(1)} %pad_maximum_fusion.refs_0_, bf16[4,72,128]{2,1,0:T(8,128)(2,1)S(1)} %collective-permute-done.3.refs_1_, bf16[4,72,128]{2,1,0:T(8,128)(2,1)S(1)} %collective-permute-done.5.refs_2_, bf16[4,72,128]{2,1,0:T(8,128)(2,1)S(1)} %collective-permute-done.4.refs_3_, ...), custom_call_target="tpu_custom_call" | custom-call | tf_op jit(solution)/shard_map/correlate/pallas_call | solution.py:263
  (6 shorter events, 0.0 us)
Async XLA Ops:
  11.6 6.2 %collective-permute-start = (bf16[2,72,128]{2,1,0:T(8,128)(2,1)S(1)}, bf16[2,72,128]{2,1,0:T(8,128)(2,1)S(1)}, u32[]{:S(2)}, u32[]{:S(2)}) collective-permute-start(bf16[2,72,128]{2,1,0:T(8,128)(2,1)S(1)} %get-tuple-element.10), channel_id=1, source_target_pairs={{0,9},{1,8},{2,11},{3,10},{4,13},{5,12},{6,15},{7,14},{8,17},{9,16... | collective-permute-start | bytes 110600 | tf_op jit(solution)/shard_map/ppermute | solution.py:316
  14.1 5.5 %collective-permute-start.1 = (bf16[2,72,128]{2,1,0:T(8,128)(2,1)S(1)}, bf16[2,72,128]{2,1,0:T(8,128)(2,1)S(1)}, u32[]{:S(2)}, u32[]{:S(2)}) collective-permute-start(bf16[2,72,128]{2,1,0:T(8,128)(2,1)S(1)} %get-tuple-element.11), channel_id=1, source_target_pairs={{0,17},{1,16},{2,19},{3,18},{4,21},{5,20},{6,23},{7,22},{8,25},{9,... | collective-permute-start | bytes 110600 | tf_op jit(solution)/shard_map/ppermute | solution.py:316
  17.0 3.8 %collective-permute-start.2 = (bf16[2,72,128]{2,1,0:T(8,128)(2,1)S(1)}, bf16[2,72,128]{2,1,0:T(8,128)(2,1)S(1)}, u32[]{:S(2)}, u32[]{:S(2)}) collective-permute-start(bf16[2,72,128]{2,1,0:T(8,128)(2,1)S(1)} %get-tuple-element.12), channel_id=1, source_target_pairs={{0,25},{1,24},{2,27},{3,26},{4,29},{5,28},{6,31},{7,30},{8,1},{9,0... | collective-permute-start | bytes 110600 | tf_op jit(solution)/shard_map/ppermute | solution.py:316
  20.8 5.3 %collective-permute-start.4 = (bf16[4,72,128]{2,1,0:T(8,128)(2,1)S(1)}, bf16[4,72,128]{2,1,0:T(8,128)(2,1)S(1)}, u32[]{:S(2)}, u32[]{:S(2)}) collective-permute-start(bf16[4,72,128]{2,1,0:T(8,128)(2,1)S(1)} %pad_maximum_fusion.refs_0_), channel_id=1, source_target_pairs={{0,3},{1,2},{2,1},{3,0},{4,7},{5,6},{6,5},{7,4},{8,11},{9,10},{10,... | collective-permute-start | bytes 221192 | tf_op jit(solution)/shard_map/ppermute | solution.py:304
  22.2 5.0 %collective-permute-start.8 = (bf16[4,72,128]{2,1,0:T(8,128)(2,1)S(1)}, bf16[4,72,128]{2,1,0:T(8,128)(2,1)S(1)}, u32[]{:S(2)}, u32[]{:S(2)}) collective-permute-start(bf16[4,72,128]{2,1,0:T(8,128)(2,1)S(1)} %pad_maximum_fusion.1), channel_id=1, source_target_pairs={{0,7},{1,6},{2,5},{3,4},{4,3},{5,2},{6,1},{7,0},{8,15},{9,14},{10,... | collective-permute-start | bytes 221192 | tf_op jit(solution)/shard_map/ppermute | solution.py:304
  23.7 4.5 %collective-permute-start.6 = (bf16[4,72,128]{2,1,0:T(8,128)(2,1)S(1)}, bf16[4,72,128]{2,1,0:T(8,128)(2,1)S(1)}, u32[]{:S(2)}, u32[]{:S(2)}) collective-permute-start(bf16[4,72,128]{2,1,0:T(8,128)(2,1)S(1)} %pad_maximum_fusion.1), channel_id=1, source_target_pairs={{0,5},{1,4},{2,7},{3,6},{4,1},{5,0},{6,3},{7,2},{8,13},{9,12},{10,... | collective-permute-start | bytes 221192 | tf_op jit(solution)/shard_map/ppermute | solution.py:304
  23.9 4.4 %collective-permute-start.3 = (bf16[4,72,128]{2,1,0:T(8,128)(2,1)S(1)}, bf16[4,72,128]{2,1,0:T(8,128)(2,1)S(1)}, u32[]{:S(2)}, u32[]{:S(2)}) collective-permute-start(bf16[4,72,128]{2,1,0:T(8,128)(2,1)S(1)} %pad_maximum_fusion.refs_0_), channel_id=1, source_target_pairs={{0,1},{1,0},{2,3},{3,2},{4,5},{5,4},{6,7},{7,6},{8,9},{9,8},{10,11... | collective-permute-start | bytes 221192 | tf_op jit(solution)/shard_map/ppermute | solution.py:304
  26.1 2.2 %collective-permute-start.5 = (bf16[4,72,128]{2,1,0:T(8,128)(2,1)S(1)}, bf16[4,72,128]{2,1,0:T(8,128)(2,1)S(1)}, u32[]{:S(2)}, u32[]{:S(2)}) collective-permute-start(bf16[4,72,128]{2,1,0:T(8,128)(2,1)S(1)} %collective-permute-done.4.refs_3_), channel_id=1, source_target_pairs={{0,1},{1,0},{2,3},{3,2},{4,5},{5,4},{6,7},{7,6},{8,9},{9,8},{10,11... | collective-permute-start | bytes 221192 | tf_op jit(solution)/shard_map/ppermute | solution.py:304
  27.1 1.3 %collective-permute-start.9 = (bf16[4,72,128]{2,1,0:T(8,128)(2,1)S(1)}, bf16[4,72,128]{2,1,0:T(8,128)(2,1)S(1)}, u32[]{:S(2)}, u32[]{:S(2)}) collective-permute-start(bf16[4,72,128]{2,1,0:T(8,128)(2,1)S(1)} %collective-permute-done.8.refs_7_), channel_id=1, source_target_pairs={{0,1},{1,0},{2,3},{3,2},{4,5},{5,4},{6,7},{7,6},{8,9},{9,8},{10,11... | collective-permute-start | bytes 221192 | tf_op jit(solution)/shard_map/ppermute | solution.py:304
  28.2 1.3 %collective-permute-start.7 = (bf16[4,72,128]{2,1,0:T(8,128)(2,1)S(1)}, bf16[4,72,128]{2,1,0:T(8,128)(2,1)S(1)}, u32[]{:S(2)}, u32[]{:S(2)}) collective-permute-start(bf16[4,72,128]{2,1,0:T(8,128)(2,1)S(1)} %collective-permute-done.6.refs_5_), channel_id=1, source_target_pairs={{0,1},{1,0},{2,3},{3,2},{4,5},{5,4},{6,7},{7,6},{8,9},{9,8},{10,11... | collective-permute-start | bytes 221192 | tf_op jit(solution)/shard_map/ppermute | solution.py:304

commit v8 on v7

--- a/solution.py
+++ b/solution.py
@@ -113,7 +113,7 @@
         if not relative:
             return m
         freq, tm = lax.axis_index("freq"), lax.axis_index("tm")
-        return label((label(freq) + m // n_tm) % n_freq) * n_tm + (tm ^ (m % n_tm))
+        return (freq + m // n_tm) % n_freq * n_tm + (tm ^ (m % n_tm))
 
     def emit(first, count):
         for m in range(chans):
@@ -122,7 +122,11 @@
                 at = pl.multiple_of(at, 8)
             per = chans // len(outs)
             block = spec[pl.ds(at, count), :].astype(jnp.bfloat16)
-            outs[m // per][m % per, first : first + count, :] = block
+            if relative:
+                start = m % per * in_dev + first
+                outs[m // per][start : start + count, :] = block
+            else:
+                outs[0][m, first : first + count, :] = block
 
     count = in_dev // GROUP
     lax.fori_loop(0, count, step, 0)
@@ -133,23 +137,28 @@
         for bank in range(2):
             rows = carry[bank, p * chans : (p + 1) * chans, :]
             edge[pl.ds(2 * p + bank, chans, stride=8), :] = rows
-    for m in range(chans):
-        per = chans // len(outs)
-        at = slot(m) * 8
-        if relative:
-            at = pl.multiple_of(at, 8)
+    if relative:
+        for k, out in enumerate(outs):
+            both = []
+            for m in (2 * k, 2 * k + 1):
+                both.append(edge[pl.ds(pl.multiple_of(slot(m) * 8, 8), 8), :])
+            block = both[0] + pltpu.roll(both[1], 4, 0)
+            out[2 * in_dev :, :] = block.astype(jnp.bfloat16)
+    else:
         count = outs[0].shape[1] - in_dev
-        block = edge[pl.ds(at, count), :].astype(jnp.bfloat16)
-        outs[m // per][m % per, in_dev:, :] = block
-
-
-def channelize(samples, chan_index, me, relative, mesh_shape):
+        for m in range(chans):
+            block = edge[m * 8 : m * 8 + count, :].astype(jnp.bfloat16)
+            outs[0][m, in_dev:, :] = block
+
+
+def channelize(samples, chan_index, relative, mesh_shape):
     in_dev, fr_dev, frame = samples.shape
     chans = chan_index.shape[0]
     rows = (in_dev + 4 + 7) // 8 * 8
     products = TAPS * 2 * chans
     parts = mesh_shape[0] if relative else 1
-    out = jax.ShapeDtypeStruct((chans // parts, rows, LANES), jnp.bfloat16)
+    shape = (2 * in_dev + 8, LANES) if relative else (chans, rows, LANES)
+    out = jax.ShapeDtypeStruct(shape, jnp.bfloat16)
     chan_index = pltpu.with_memory_space_constraint(chan_index, pltpu.HBM)
     return pl.pallas_call(
         functools.partial(channelize_kernel, chans, relative, mesh_shape),
@@ -188,7 +197,7 @@
     for four in carried:
         both = []
         for p in range(2):
-            row = jnp.where(second, four[2 * p + 1][None], four[2 * p][None])
+            row = jnp.where(second, four[2 * p + 1], four[2 * p])
             both.append(jnp.where(mask, row, 0.0).astype(jnp.bfloat16))
         picked.append(jnp.concatenate(both, axis=1))
     return jnp.dot(
@@ -196,10 +205,6 @@
     )
 
 
-def label(z):
-    return z + 0
-
-
 def place_of(turn):
     at = jnp.int32(0)
     for place, k in enumerate(ORDER):
@@ -210,21 +215,23 @@
 def correlate_kernel(mesh_shape, in_dev, fr_dev, *refs):
     n_freq, n_tm, n_bl = mesh_shape
     own_half, other_half = refs[:n_bl], refs[n_bl : 2 * n_bl]
-    o_ref, left, right, result, sems = refs[2 * n_bl :]
+    o_ref, left, right, result, edges, sems = refs[2 * n_bl :]
+    for i in range(2 * n_bl):
+        edges[i] = refs[i][n_freq * in_dev :, :].astype(jnp.float32)
     freq, tm, bl = (lax.axis_index(axis) for axis in ("freq", "tm", "bl"))
     scale = 1.0 / (n_tm * fr_dev)
     order = [(f, k) for f in range(n_freq // 2) for k in range(n_bl)]
     for out, base in ((left, bl // 2 * (n_freq // 2)), (right, bl % 2 * (n_freq // 2))):
         early, late, carried, core = [], [], [], []
         for f, k in order:
-            at = place_of((label(freq) - label(base + f) + n_freq) % n_freq)
+            at = place_of((freq - base - f + n_freq) % n_freq)
             mine, other = own_half[k], other_half[k]
             core.append(jnp.where(at == 0, 0, 1))
-            body, over = slice(0, in_dev), slice(in_dev, in_dev + 4)
-            early.append(jnp.where(tm == 0, mine[at, body, :], other[at, body, :]))
-            late.append(jnp.where(tm == 0, other[at, body, :], mine[at, body, :]))
-            four = jnp.where(tm == 0, mine[at, over, :], other[at, over, :])
-            carried.append(four.astype(jnp.float32))
+            body = pl.ds(pl.multiple_of(at * in_dev, in_dev), in_dev)
+            early.append(jnp.where(tm == 0, mine[body, :], other[body, :]))
+            late.append(jnp.where(tm == 0, other[body, :], mine[body, :]))
+            giver = jnp.where(tm == 0, k, n_bl + k)
+            carried.append([edges[giver, pl.ds(at * 4 + r, 1), :] for r in range(4)])
         late = jnp.concatenate(late, axis=0).astype(jnp.float32)
         late = (late + place_carry(carried, in_dev, fr_dev)).astype(jnp.bfloat16)
         for m, (f, k) in enumerate(order):
@@ -257,7 +264,7 @@
         copy.wait()
 
 
-def correlate(sources, me, mesh_shape, in_dev, fr_dev):
+def correlate(sources, mesh_shape, in_dev, fr_dev):
     n_freq, n_tm, n_bl = mesh_shape
     half = n_freq * n_bl * in_dev // 2
     return pl.pallas_call(
@@ -269,6 +276,7 @@
             pltpu.VMEM((half, n_tm * LANES), jnp.bfloat16),
             pltpu.VMEM((half, n_tm * LANES), jnp.bfloat16),
             pltpu.VMEM((2, half, half), jnp.float32),
+            pltpu.VMEM((len(sources), 4 * n_freq, LANES), jnp.float32),
             pltpu.SemaphoreType.DMA((4,)),
         ],
         compiler_params=pltpu.CompilerParams(vmem_limit_bytes=16 * 2**20),
@@ -311,11 +319,14 @@
         route = []
         for z in range(len(parts)):
             for i in range(plane):
-                to = label((label(z) + k) % len(parts))
+                to = (z + k) % len(parts)
                 route.append((z * plane + i, to * plane + (i ^ 1)))
         arrived[k] = lax.ppermute(parts[k], ("freq",) + across, route)
-    keep = jnp.stack([arrived[k][0] for k in ORDER])
-    send = jnp.stack([arrived[k][1] for k in ORDER])
+    rows = [arrived[k] for k in ORDER]
+    half = (parts[0].shape[0] - 8) // 2
+    keep = [block[:half] for block in rows] + [block[2 * half : 2 * half + 4] for block in rows]
+    send = [block[half : 2 * half] for block in rows] + [block[2 * half + 4 :] for block in rows]
+    keep, send = jnp.concatenate(keep), jnp.concatenate(send)
     corner = swapped(send, across, n_bl + 3)
     beside = swapped(send, across, n_bl + 1)
     far = swapped(keep, across, 3)
@@ -330,12 +341,11 @@
     axes = ("freq", "tm", "bl")
     mesh_shape = tuple(lax.axis_size(axis) for axis in axes)
     n_freq, n_tm, n_bl = mesh_shape
-    me = lax.axis_index(axes).reshape(1)
     relative = in_dev % 16 == 0 and n_freq <= 4 and n_tm == 2 and n_bl == 4
-    spectra = channelize(samples, chan_index, me, relative, mesh_shape)
+    spectra = channelize(samples, chan_index, relative, mesh_shape)
     if relative:
         sources = exchange(spectra, n_tm, n_bl)
-        return correlate(sources, me, mesh_shape, in_dev, fr_dev)
+        return correlate(sources, mesh_shape, in_dev, fr_dev)
     moved = lax.all_to_all(spectra[0], ("freq", "tm"), split_axis=0, concat_axis=0, tiled=True)
     gathered = lax.all_gather(moved, "bl", axis=0, tiled=False)
     tile = lax.axis_index("bl")

time: 31.5 us -> 31.4 us (level)
  waiting for transfers between devices: 7.6 us -> 7.18 us
where the time goes in v8:
time: 31.4 us; the launch traced here: 31.2 us
  Pallas kernels  13.5 us (43%)
  starting transfers between devices  10.2 us (32%)
  waiting for transfers between devices  7.18 us (23%)
    pallas_call x1, Pallas kernels, channelize(): pl.pallas_call(functools.partial(channelize_kernel, chans, relative, mesh...  11.6 us
    ppermute x3, starting transfers between devices, exchange(): arrived[k] = lax.ppermute(parts[k], ('freq',) + across, route)  6.17 us
    ppermute x7, waiting for transfers between devices, swapped(): return lax.ppermute(block, axes, [(i, i ^ distance) for i in range(count)])  4.27 us
    ppermute x7, starting transfers between devices, swapped(): return lax.ppermute(block, axes, [(i, i ^ distance) for i in range(count)])  4.06 us
    ppermute x3, waiting for transfers between devices, exchange(): arrived[k] = lax.ppermute(parts[k], ('freq',) + across, route)  2.9 us
    pallas_call x1, Pallas kernels, correlate(): pl.pallas_call(functools.partial(correlate_kernel, mesh_shape, in_dev, fr...  1.93 us
  transfers between devices with their start and end apart: 10, of which 7 were waited for; matrix products, arithmetic and copies ran while one was open for 0% of the time, Pallas kernels for 0%

profile of v8, /device:TPU:0, one launch (start us, length us, event | category | flops | bytes accessed | tf_op | source)
XLA Modules:
  0.0 31.2 jit_solution(7192502001332030023)
XLA Ops:
  0.0 11.6 %channelize.1 = (bf16[136,128]{1,0:T(8,128)(2,1)S(1)}, bf16[136,128]{1,0:T(8,128)(2,1)S(1)}, bf16[136,128]{1,0:T(8,128)(2,1)S(1)}, bf16[136,128]{1,0:T(8,128)(2,1)S(1)}) custom-call(s32[8]{0:T(128)} %chan_hbm.1, s32[64,64,2048]{2,1,0:T(8,128)} %x_ref.1), custom_call_target="tpu_custom_call" | custom-call | tf_op jit(solution)/shard_map/channelize/pallas_call | solution.py:163
  11.6 2.5 %collective-permute-start = (bf16[136,128]{1,0:T(8,128)(2,1)S(1)}, bf16[136,128]{1,0:T(8,128)(2,1)S(1)}, u32[]{:S(2)}, u32[]{:S(2)}) collective-permute-start(bf16[136,128]{1,0:T(8,128)(2,1)S(1)} %get-tuple-element.10), channel_id=1, source_target_pairs={{0,9},{1,8},{2,11},{3,10},{4,13},{5,12},{6,15},{7,14},{8,17},{9,16... | collective-permute-start | bytes 104456 | tf_op jit(solution)/shard_map/ppermute | solution.py:324
  14.1 2.9 %collective-permute-start.1 = (bf16[136,128]{1,0:T(8,128)(2,1)S(1)}, bf16[136,128]{1,0:T(8,128)(2,1)S(1)}, u32[]{:S(2)}, u32[]{:S(2)}) collective-permute-start(bf16[136,128]{1,0:T(8,128)(2,1)S(1)} %get-tuple-element.11), channel_id=1, source_target_pairs={{0,17},{1,16},{2,19},{3,18},{4,21},{5,20},{6,23},{7,22},{8,25},{9,... | collective-permute-start | bytes 104456 | tf_op jit(solution)/shard_map/ppermute | solution.py:324
  17.0 0.8 %collective-permute-start.2 = (bf16[136,128]{1,0:T(8,128)(2,1)S(1)}, bf16[136,128]{1,0:T(8,128)(2,1)S(1)}, u32[]{:S(2)}, u32[]{:S(2)}) collective-permute-start(bf16[136,128]{1,0:T(8,128)(2,1)S(1)} %get-tuple-element.12), channel_id=1, source_target_pairs={{0,25},{1,24},{2,27},{3,26},{4,29},{5,28},{6,31},{7,30},{8,1},{9,0... | collective-permute-start | bytes 104456 | tf_op jit(solution)/shard_map/ppermute | solution.py:324
  17.8 0.0 collective-permute-done
  17.8 1.6 %collective-permute-done.1 = bf16[136,128]{1,0:T(8,128)(2,1)S(1)} collective-permute-done((bf16[136,128]{1,0:T(8,128)(2,1)S(1)}, bf16[136,128]{1,0:T(8,128)(2,1)S(1)}, u32[]{:S(2)}, u32[]{:S(2)}) %collective-permute-start.1) | collective-permute-done | bytes 34848 | tf_op jit(solution)/shard_map/ppermute | solution.py:324
  19.5 1.3 %collective-permute-done.2 = bf16[136,128]{1,0:T(8,128)(2,1)S(1)} collective-permute-done((bf16[136,128]{1,0:T(8,128)(2,1)S(1)}, bf16[136,128]{1,0:T(8,128)(2,1)S(1)}, u32[]{:S(2)}, u32[]{:S(2)}) %collective-permute-start.2) | collective-permute-done | bytes 34848 | tf_op jit(solution)/shard_map/ppermute | solution.py:324
  20.7 0.1 concatenate.6.refs_0_
  20.9 1.3 %collective-permute-start.4 = (bf16[272,128]{1,0:T(8,128)(2,1)S(1)}, bf16[272,128]{1,0:T(8,128)(2,1)S(1)}, u32[]{:S(2)}, u32[]{:S(2)}) collective-permute-start(bf16[272,128]{1,0:T(8,128)(2,1)S(1)} %concatenate.6.refs_0_), channel_id=1, source_target_pairs={{0,3},{1,2},{2,1},{3,0},{4,7},{5,6},{6,5},{7,4},{8,11},{9,10},{10,... | collective-permute-start | bytes 208904 | tf_op jit(solution)/shard_map/ppermute | solution.py:312
  22.1 0.1 concatenate.7
  22.2 1.5 %collective-permute-start.8 = (bf16[272,128]{1,0:T(8,128)(2,1)S(1)}, bf16[272,128]{1,0:T(8,128)(2,1)S(1)}, u32[]{:S(2)}, u32[]{:S(2)}) collective-permute-start(bf16[272,128]{1,0:T(8,128)(2,1)S(1)} %concatenate.7), channel_id=1, source_target_pairs={{0,7},{1,6},{2,5},{3,4},{4,3},{5,2},{6,1},{7,0},{8,15},{9,14},{10,... | collective-permute-start | bytes 208904 | tf_op jit(solution)/shard_map/ppermute | solution.py:312
  23.7 0.3 collective-permute-start.6
  24.0 0.4 %collective-permute-start.3 = (bf16[272,128]{1,0:T(8,128)(2,1)S(1)}, bf16[272,128]{1,0:T(8,128)(2,1)S(1)}, u32[]{:S(2)}, u32[]{:S(2)}) collective-permute-start(bf16[272,128]{1,0:T(8,128)(2,1)S(1)} %concatenate.6.refs_0_), channel_id=1, source_target_pairs={{0,1},{1,0},{2,3},{3,2},{4,5},{5,4},{6,7},{7,6},{8,9},{9,8},{10,11... | collective-permute-start | bytes 208904 | tf_op jit(solution)/shard_map/ppermute | solution.py:312
  24.4 0.7 %collective-permute-done.4.refs_3_ = bf16[272,128]{1,0:T(8,128)(2,1)S(1)} collective-permute-done((bf16[272,128]{1,0:T(8,128)(2,1)S(1)}, bf16[272,128]{1,0:T(8,128)(2,1)S(1)}, u32[]{:S(2)}, u32[]{:S(2)}) %collective-permute-start.4) | collective-permute-done | bytes 69664 | tf_op jit(solution)/shard_map/ppermute | solution.py:312
  25.1 0.1 collective-permute-start.5
  25.2 1.9 %collective-permute-done.8.refs_7_ = bf16[272,128]{1,0:T(8,128)(2,1)S(1)} collective-permute-done((bf16[272,128]{1,0:T(8,128)(2,1)S(1)}, bf16[272,128]{1,0:T(8,128)(2,1)S(1)}, u32[]{:S(2)}, u32[]{:S(2)}) %collective-permute-start.8) | collective-permute-done | bytes 69664 | tf_op jit(solution)/shard_map/ppermute | solution.py:312
  27.1 0.4 %collective-permute-start.9 = (bf16[272,128]{1,0:T(8,128)(2,1)S(1)}, bf16[272,128]{1,0:T(8,128)(2,1)S(1)}, u32[]{:S(2)}, u32[]{:S(2)}) collective-permute-start(bf16[272,128]{1,0:T(8,128)(2,1)S(1)} %collective-permute-done.8.refs_7_), channel_id=1, source_target_pairs={{0,1},{1,0},{2,3},{3,2},{4,5},{5,4},{6,7},{7,6},{8,9},{9,8},{10,11... | collective-permute-start | bytes 208904 | tf_op jit(solution)/shard_map/ppermute | solution.py:312
  27.5 0.6 %collective-permute-done.6.refs_5_ = bf16[272,128]{1,0:T(8,128)(2,1)S(1)} collective-permute-done((bf16[272,128]{1,0:T(8,128)(2,1)S(1)}, bf16[272,128]{1,0:T(8,128)(2,1)S(1)}, u32[]{:S(2)}, u32[]{:S(2)}) %collective-permute-start.6) | collective-permute-done | bytes 69664 | tf_op jit(solution)/shard_map/ppermute | solution.py:312
  28.1 0.1 collective-permute-start.7
  28.2 0.0 collective-permute-done.3.refs_1_
  28.2 0.0 collective-permute-done.5.refs_2_
  28.2 0.2 collective-permute-done.9.refs_6_
  28.4 0.9 %collective-permute-done.7.refs_4_ = bf16[272,128]{1,0:T(8,128)(2,1)S(1)} collective-permute-done((bf16[272,128]{1,0:T(8,128)(2,1)S(1)}, bf16[272,128]{1,0:T(8,128)(2,1)S(1)}, u32[]{:S(2)}, u32[]{:S(2)}) %collective-permute-start.7) | collective-permute-done | bytes 69664 | tf_op jit(solution)/shard_map/ppermute | solution.py:312
  29.3 1.9 %correlate.1 = f32[1,1,2,512,512]{4,3,2,1,0:T(8,128)} custom-call(bf16[272,128]{1,0:T(8,128)(2,1)S(1)} %concatenate.6.refs_0_, bf16[272,128]{1,0:T(8,128)(2,1)S(1)} %collective-permute-done.3.refs_1_, bf16[272,128]{1,0:T(8,128)(2,1)S(1)} %collective-permute-done.5.refs_2_, bf16[272,128]{1,0:T(8,128)(2,1)S(1)} %collective-permute-done.4.refs_3_, ...), custom_call_target="tpu_custom_call" | custom-call | tf_op jit(solution)/shard_map/correlate/pallas_call | solution.py:270
  (8 shorter events, 0.0 us)
Async XLA Ops:
  11.6 6.2 %collective-permute-start = (bf16[136,128]{1,0:T(8,128)(2,1)S(1)}, bf16[136,128]{1,0:T(8,128)(2,1)S(1)}, u32[]{:S(2)}, u32[]{:S(2)}) collective-permute-start(bf16[136,128]{1,0:T(8,128)(2,1)S(1)} %get-tuple-element.10), channel_id=1, source_target_pairs={{0,9},{1,8},{2,11},{3,10},{4,13},{5,12},{6,15},{7,14},{8,17},{9,16... | collective-permute-start | bytes 104456 | tf_op jit(solution)/shard_map/ppermute | solution.py:324
  14.1 5.4 %collective-permute-start.1 = (bf16[136,128]{1,0:T(8,128)(2,1)S(1)}, bf16[136,128]{1,0:T(8,128)(2,1)S(1)}, u32[]{:S(2)}, u32[]{:S(2)}) collective-permute-start(bf16[136,128]{1,0:T(8,128)(2,1)S(1)} %get-tuple-element.11), channel_id=1, source_target_pairs={{0,17},{1,16},{2,19},{3,18},{4,21},{5,20},{6,23},{7,22},{8,25},{9,... | collective-permute-start | bytes 104456 | tf_op jit(solution)/shard_map/ppermute | solution.py:324
  17.0 3.8 %collective-permute-start.2 = (bf16[136,128]{1,0:T(8,128)(2,1)S(1)}, bf16[136,128]{1,0:T(8,128)(2,1)S(1)}, u32[]{:S(2)}, u32[]{:S(2)}) collective-permute-start(bf16[136,128]{1,0:T(8,128)(2,1)S(1)} %get-tuple-element.12), channel_id=1, source_target_pairs={{0,25},{1,24},{2,27},{3,26},{4,29},{5,28},{6,31},{7,30},{8,1},{9,0... | collective-permute-start | bytes 104456 | tf_op jit(solution)/shard_map/ppermute | solution.py:324
  20.9 4.2 %collective-permute-start.4 = (bf16[272,128]{1,0:T(8,128)(2,1)S(1)}, bf16[272,128]{1,0:T(8,128)(2,1)S(1)}, u32[]{:S(2)}, u32[]{:S(2)}) collective-permute-start(bf16[272,128]{1,0:T(8,128)(2,1)S(1)} %concatenate.6.refs_0_), channel_id=1, source_target_pairs={{0,3},{1,2},{2,1},{3,0},{4,7},{5,6},{6,5},{7,4},{8,11},{9,10},{10,... | collective-permute-start | bytes 208904 | tf_op jit(solution)/shard_map/ppermute | solution.py:312
  22.2 4.9 %collective-permute-start.8 = (bf16[272,128]{1,0:T(8,128)(2,1)S(1)}, bf16[272,128]{1,0:T(8,128)(2,1)S(1)}, u32[]{:S(2)}, u32[]{:S(2)}) collective-permute-start(bf16[272,128]{1,0:T(8,128)(2,1)S(1)} %concatenate.7), channel_id=1, source_target_pairs={{0,7},{1,6},{2,5},{3,4},{4,3},{5,2},{6,1},{7,0},{8,15},{9,14},{10,... | collective-permute-start | bytes 208904 | tf_op jit(solution)/shard_map/ppermute | solution.py:312
  23.7 4.3 %collective-permute-start.6 = (bf16[272,128]{1,0:T(8,128)(2,1)S(1)}, bf16[272,128]{1,0:T(8,128)(2,1)S(1)}, u32[]{:S(2)}, u32[]{:S(2)}) collective-permute-start(bf16[272,128]{1,0:T(8,128)(2,1)S(1)} %concatenate.7), channel_id=1, source_target_pairs={{0,5},{1,4},{2,7},{3,6},{4,1},{5,0},{6,3},{7,2},{8,13},{9,12},{10,... | collective-permute-start | bytes 208904 | tf_op jit(solution)/shard_map/ppermute | solution.py:312
  24.0 4.2 %collective-permute-start.3 = (bf16[272,128]{1,0:T(8,128)(2,1)S(1)}, bf16[272,128]{1,0:T(8,128)(2,1)S(1)}, u32[]{:S(2)}, u32[]{:S(2)}) collective-permute-start(bf16[272,128]{1,0:T(8,128)(2,1)S(1)} %concatenate.6.refs_0_), channel_id=1, source_target_pairs={{0,1},{1,0},{2,3},{3,2},{4,5},{5,4},{6,7},{7,6},{8,9},{9,8},{10,11... | collective-permute-start | bytes 208904 | tf_op jit(solution)/shard_map/ppermute | solution.py:312
  25.1 3.1 %collective-permute-start.5 = (bf16[272,128]{1,0:T(8,128)(2,1)S(1)}, bf16[272,128]{1,0:T(8,128)(2,1)S(1)}, u32[]{:S(2)}, u32[]{:S(2)}) collective-permute-start(bf16[272,128]{1,0:T(8,128)(2,1)S(1)} %collective-permute-done.4.refs_3_), channel_id=1, source_target_pairs={{0,1},{1,0},{2,3},{3,2},{4,5},{5,4},{6,7},{7,6},{8,9},{9,8},{10,11... | collective-permute-start | bytes 208904 | tf_op jit(solution)/shard_map/ppermute | solution.py:312
  27.1 1.3 %collective-permute-start.9 = (bf16[272,128]{1,0:T(8,128)(2,1)S(1)}, bf16[272,128]{1,0:T(8,128)(2,1)S(1)}, u32[]{:S(2)}, u32[]{:S(2)}) collective-permute-start(bf16[272,128]{1,0:T(8,128)(2,1)S(1)} %collective-permute-done.8.refs_7_), channel_id=1, source_target_pairs={{0,1},{1,0},{2,3},{3,2},{4,5},{5,4},{6,7},{7,6},{8,9},{9,8},{10,11... | collective-permute-start | bytes 208904 | tf_op jit(solution)/shard_map/ppermute | solution.py:312
  28.1 1.3 %collective-permute-start.7 = (bf16[272,128]{1,0:T(8,128)(2,1)S(1)}, bf16[272,128]{1,0:T(8,128)(2,1)S(1)}, u32[]{:S(2)}, u32[]{:S(2)}) collective-permute-start(bf16[272,128]{1,0:T(8,128)(2,1)S(1)} %collective-permute-done.6.refs_5_), channel_id=1, source_target_pairs={{0,1},{1,0},{2,3},{3,2},{4,5},{5,4},{6,7},{7,6},{8,9},{9,8},{10,11... | collective-permute-start | bytes 208904 | tf_op jit(solution)/shard_map/ppermute | solution.py:312

commit v9 on v8

--- a/solution.py
+++ b/solution.py
@@ -115,23 +115,9 @@
         freq, tm = lax.axis_index("freq"), lax.axis_index("tm")
         return (freq + m // n_tm) % n_freq * n_tm + (tm ^ (m % n_tm))
 
-    def emit(first, count):
-        for m in range(chans):
-            at = slot(m) * in_dev + first
-            if relative:
-                at = pl.multiple_of(at, 8)
-            per = chans // len(outs)
-            block = spec[pl.ds(at, count), :].astype(jnp.bfloat16)
-            if relative:
-                start = m % per * in_dev + first
-                outs[m // per][start : start + count, :] = block
-            else:
-                outs[0][m, first : first + count, :] = block
-
     count = in_dev // GROUP
     lax.fori_loop(0, count, step, 0)
     finish(count - 1, True)
-    emit(0, in_dev)
     edge[...] = jnp.zeros_like(edge)
     for p in range(2):
         for bank in range(2):
@@ -140,24 +126,30 @@
     if relative:
         for k, out in enumerate(outs):
             both = []
-            for m in (2 * k, 2 * k + 1):
-                both.append(edge[pl.ds(pl.multiple_of(slot(m) * 8, 8), 8), :])
-            block = both[0] + pltpu.roll(both[1], 4, 0)
-            out[2 * in_dev :, :] = block.astype(jnp.bfloat16)
+            for j in range(2):
+                at = slot(2 * k + j)
+                own = spec[pl.ds(pl.multiple_of(at * in_dev, in_dev), in_dev), :]
+                out[j * in_dev : (j + 1) * in_dev, :] = own.astype(jnp.bfloat16)
+                both.append(edge[pl.ds(pl.multiple_of(at * 8, 8), 8), :])
+            last = both[0] + pltpu.roll(both[1], 4, 0)
+            last = jnp.concatenate([last, jnp.zeros_like(last)], axis=0)
+            out[2 * in_dev :, :] = last.astype(jnp.bfloat16)
     else:
-        count = outs[0].shape[1] - in_dev
+        spare = outs[0].shape[1] - in_dev - 4
         for m in range(chans):
-            block = edge[m * 8 : m * 8 + count, :].astype(jnp.bfloat16)
-            outs[0][m, in_dev:, :] = block
+            block = [spec[m * in_dev : (m + 1) * in_dev, :], edge[m * 8 : m * 8 + 4, :]]
+            if spare:
+                block.append(jnp.zeros((spare, LANES), jnp.float32))
+            outs[0][m] = jnp.concatenate(block, axis=0).astype(jnp.bfloat16)
 
 
 def channelize(samples, chan_index, relative, mesh_shape):
     in_dev, fr_dev, frame = samples.shape
     chans = chan_index.shape[0]
-    rows = (in_dev + 4 + 7) // 8 * 8
+    rows = (in_dev + 4 + 15) // 16 * 16
     products = TAPS * 2 * chans
     parts = mesh_shape[0] if relative else 1
-    shape = (2 * in_dev + 8, LANES) if relative else (chans, rows, LANES)
+    shape = (2 * in_dev + 16, LANES) if relative else (chans, rows, LANES)
     out = jax.ShapeDtypeStruct(shape, jnp.bfloat16)
     chan_index = pltpu.with_memory_space_constraint(chan_index, pltpu.HBM)
     return pl.pallas_call(
@@ -323,9 +315,9 @@
                 route.append((z * plane + i, to * plane + (i ^ 1)))
         arrived[k] = lax.ppermute(parts[k], ("freq",) + across, route)
     rows = [arrived[k] for k in ORDER]
-    half = (parts[0].shape[0] - 8) // 2
+    half = (parts[0].shape[0] - 16) // 2
     keep = [block[:half] for block in rows] + [block[2 * half : 2 * half + 4] for block in rows]
-    send = [block[half : 2 * half] for block in rows] + [block[2 * half + 4 :] for block in rows]
+    send = [block[half : 2 * half] for block in rows] + [block[2 * half + 4 : 2 * half + 8] for block in rows]
     keep, send = jnp.concatenate(keep), jnp.concatenate(send)
     corner = swapped(send, across, n_bl + 3)
     beside = swapped(send, across, n_bl + 1)

time: 31.4 us -> 31.4 us (level)
  no operation moved by 1% of the time
where the time goes in v9:
time: 31.4 us; the launch traced here: 31.3 us
  Pallas kernels  13.5 us (43%)
  starting transfers between devices  10.2 us (32%)
  waiting for transfers between devices  7.22 us (23%)
    pallas_call x1, Pallas kernels, channelize(): pl.pallas_call(functools.partial(channelize_kernel, chans, relative, mesh...  11.6 us
    ppermute x3, starting transfers between devices, exchange(): arrived[k] = lax.ppermute(parts[k], ('freq',) + across, route)  6.17 us
    ppermute x7, waiting for transfers between devices, swapped(): return lax.ppermute(block, axes, [(i, i ^ distance) for i in range(count)])  4.24 us
    ppermute x7, starting transfers between devices, swapped(): return lax.ppermute(block, axes, [(i, i ^ distance) for i in range(count)])  4.06 us
    ppermute x3, waiting for transfers between devices, exchange(): arrived[k] = lax.ppermute(parts[k], ('freq',) + across, route)  2.98 us
    pallas_call x1, Pallas kernels, correlate(): pl.pallas_call(functools.partial(correlate_kernel, mesh_shape, in_dev, fr...  1.93 us
  transfers between devices with their start and end apart: 10, of which 7 were waited for; matrix products, arithmetic and copies ran while one was open for 0% of the time, Pallas kernels for 0%

profile of v9, /device:TPU:0, one launch (start us, length us, event | category | flops | bytes accessed | tf_op | source)
XLA Modules:
  0.0 31.3 jit_solution(936698178275920899)
XLA Ops:
  0.0 11.6 %channelize.1 = (bf16[144,128]{1,0:T(8,128)(2,1)S(1)}, bf16[144,128]{1,0:T(8,128)(2,1)S(1)}, bf16[144,128]{1,0:T(8,128)(2,1)S(1)}, bf16[144,128]{1,0:T(8,128)(2,1)S(1)}) custom-call(s32[8]{0:T(128)} %chan_hbm.1, s32[64,64,2048]{2,1,0:T(8,128)} %x_ref.1), custom_call_target="tpu_custom_call" | custom-call | tf_op jit(solution)/shard_map/channelize/pallas_call | solution.py:155
  11.6 2.5 %collective-permute-start = (bf16[144,128]{1,0:T(8,128)(2,1)S(1)}, bf16[144,128]{1,0:T(8,128)(2,1)S(1)}, u32[]{:S(2)}, u32[]{:S(2)}) collective-permute-start(bf16[144,128]{1,0:T(8,128)(2,1)S(1)} %get-tuple-element.10), channel_id=1, source_target_pairs={{0,9},{1,8},{2,11},{3,10},{4,13},{5,12},{6,15},{7,14},{8,17},{9,16... | collective-permute-start | bytes 110600 | tf_op jit(solution)/shard_map/ppermute | solution.py:316
  14.1 2.9 %collective-permute-start.1 = (bf16[144,128]{1,0:T(8,128)(2,1)S(1)}, bf16[144,128]{1,0:T(8,128)(2,1)S(1)}, u32[]{:S(2)}, u32[]{:S(2)}) collective-permute-start(bf16[144,128]{1,0:T(8,128)(2,1)S(1)} %get-tuple-element.11), channel_id=1, source_target_pairs={{0,17},{1,16},{2,19},{3,18},{4,21},{5,20},{6,23},{7,22},{8,25},{9,... | collective-permute-start | bytes 110600 | tf_op jit(solution)/shard_map/ppermute | solution.py:316
  17.0 0.8 %collective-permute-start.2 = (bf16[144,128]{1,0:T(8,128)(2,1)S(1)}, bf16[144,128]{1,0:T(8,128)(2,1)S(1)}, u32[]{:S(2)}, u32[]{:S(2)}) collective-permute-start(bf16[144,128]{1,0:T(8,128)(2,1)S(1)} %get-tuple-element.12), channel_id=1, source_target_pairs={{0,25},{1,24},{2,27},{3,26},{4,29},{5,28},{6,31},{7,30},{8,1},{9,0... | collective-permute-start | bytes 110600 | tf_op jit(solution)/shard_map/ppermute | solution.py:316
  17.8 0.0 collective-permute-done
  17.8 1.8 %collective-permute-done.1 = bf16[144,128]{1,0:T(8,128)(2,1)S(1)} collective-permute-done((bf16[144,128]{1,0:T(8,128)(2,1)S(1)}, bf16[144,128]{1,0:T(8,128)(2,1)S(1)}, u32[]{:S(2)}, u32[]{:S(2)}) %collective-permute-start.1) | collective-permute-done | bytes 36896 | tf_op jit(solution)/shard_map/ppermute | solution.py:316
  19.6 1.2 %collective-permute-done.2 = bf16[144,128]{1,0:T(8,128)(2,1)S(1)} collective-permute-done((bf16[144,128]{1,0:T(8,128)(2,1)S(1)}, bf16[144,128]{1,0:T(8,128)(2,1)S(1)}, u32[]{:S(2)}, u32[]{:S(2)}) %collective-permute-start.2) | collective-permute-done | bytes 36896 | tf_op jit(solution)/shard_map/ppermute | solution.py:316
  20.8 0.1 concatenate.6.refs_0_
  20.9 1.3 %collective-permute-start.4 = (bf16[272,128]{1,0:T(8,128)(2,1)S(1)}, bf16[272,128]{1,0:T(8,128)(2,1)S(1)}, u32[]{:S(2)}, u32[]{:S(2)}) collective-permute-start(bf16[272,128]{1,0:T(8,128)(2,1)S(1)} %concatenate.6.refs_0_), channel_id=1, source_target_pairs={{0,3},{1,2},{2,1},{3,0},{4,7},{5,6},{6,5},{7,4},{8,11},{9,10},{10,... | collective-permute-start | bytes 208904 | tf_op jit(solution)/shard_map/ppermute | solution.py:304
  22.2 0.1 concatenate.7
  22.3 1.5 %collective-permute-start.8 = (bf16[272,128]{1,0:T(8,128)(2,1)S(1)}, bf16[272,128]{1,0:T(8,128)(2,1)S(1)}, u32[]{:S(2)}, u32[]{:S(2)}) collective-permute-start(bf16[272,128]{1,0:T(8,128)(2,1)S(1)} %concatenate.7), channel_id=1, source_target_pairs={{0,7},{1,6},{2,5},{3,4},{4,3},{5,2},{6,1},{7,0},{8,15},{9,14},{10,... | collective-permute-start | bytes 208904 | tf_op jit(solution)/shard_map/ppermute | solution.py:304
  23.9 0.2 collective-permute-start.6
  24.1 0.4 %collective-permute-start.3 = (bf16[272,128]{1,0:T(8,128)(2,1)S(1)}, bf16[272,128]{1,0:T(8,128)(2,1)S(1)}, u32[]{:S(2)}, u32[]{:S(2)}) collective-permute-start(bf16[272,128]{1,0:T(8,128)(2,1)S(1)} %concatenate.6.refs_0_), channel_id=1, source_target_pairs={{0,1},{1,0},{2,3},{3,2},{4,5},{5,4},{6,7},{7,6},{8,9},{9,8},{10,11... | collective-permute-start | bytes 208904 | tf_op jit(solution)/shard_map/ppermute | solution.py:304
  24.5 0.7 %collective-permute-done.4.refs_3_ = bf16[272,128]{1,0:T(8,128)(2,1)S(1)} collective-permute-done((bf16[272,128]{1,0:T(8,128)(2,1)S(1)}, bf16[272,128]{1,0:T(8,128)(2,1)S(1)}, u32[]{:S(2)}, u32[]{:S(2)}) %collective-permute-start.4) | collective-permute-done | bytes 69664 | tf_op jit(solution)/shard_map/ppermute | solution.py:304
  25.2 0.1 collective-permute-start.5
  25.3 1.9 %collective-permute-done.8.refs_7_ = bf16[272,128]{1,0:T(8,128)(2,1)S(1)} collective-permute-done((bf16[272,128]{1,0:T(8,128)(2,1)S(1)}, bf16[272,128]{1,0:T(8,128)(2,1)S(1)}, u32[]{:S(2)}, u32[]{:S(2)}) %collective-permute-start.8) | collective-permute-done | bytes 69664 | tf_op jit(solution)/shard_map/ppermute | solution.py:304
  27.2 0.4 %collective-permute-start.9 = (bf16[272,128]{1,0:T(8,128)(2,1)S(1)}, bf16[272,128]{1,0:T(8,128)(2,1)S(1)}, u32[]{:S(2)}, u32[]{:S(2)}) collective-permute-start(bf16[272,128]{1,0:T(8,128)(2,1)S(1)} %collective-permute-done.8.refs_7_), channel_id=1, source_target_pairs={{0,1},{1,0},{2,3},{3,2},{4,5},{5,4},{6,7},{7,6},{8,9},{9,8},{10,11... | collective-permute-start | bytes 208904 | tf_op jit(solution)/shard_map/ppermute | solution.py:304
  27.6 0.5 %collective-permute-done.6.refs_5_ = bf16[272,128]{1,0:T(8,128)(2,1)S(1)} collective-permute-done((bf16[272,128]{1,0:T(8,128)(2,1)S(1)}, bf16[272,128]{1,0:T(8,128)(2,1)S(1)}, u32[]{:S(2)}, u32[]{:S(2)}) %collective-permute-start.6) | collective-permute-done | bytes 69664 | tf_op jit(solution)/shard_map/ppermute | solution.py:304
  28.1 0.1 collective-permute-start.7
  28.2 0.0 collective-permute-done.3.refs_1_
  28.2 0.0 collective-permute-done.5.refs_2_
  28.2 0.3 collective-permute-done.9.refs_6_
  28.5 0.9 %collective-permute-done.7.refs_4_ = bf16[272,128]{1,0:T(8,128)(2,1)S(1)} collective-permute-done((bf16[272,128]{1,0:T(8,128)(2,1)S(1)}, bf16[272,128]{1,0:T(8,128)(2,1)S(1)}, u32[]{:S(2)}, u32[]{:S(2)}) %collective-permute-start.7) | collective-permute-done | bytes 69664 | tf_op jit(solution)/shard_map/ppermute | solution.py:304
  29.4 1.9 %correlate.1 = f32[1,1,2,512,512]{4,3,2,1,0:T(8,128)} custom-call(bf16[272,128]{1,0:T(8,128)(2,1)S(1)} %concatenate.6.refs_0_, bf16[272,128]{1,0:T(8,128)(2,1)S(1)} %collective-permute-done.3.refs_1_, bf16[272,128]{1,0:T(8,128)(2,1)S(1)} %collective-permute-done.5.refs_2_, bf16[272,128]{1,0:T(8,128)(2,1)S(1)} %collective-permute-done.4.refs_3_, ...), custom_call_target="tpu_custom_call" | custom-call | tf_op jit(solution)/shard_map/correlate/pallas_call | solution.py:262
  (8 shorter events, 0.0 us)
Async XLA Ops:
  11.6 6.2 %collective-permute-start = (bf16[144,128]{1,0:T(8,128)(2,1)S(1)}, bf16[144,128]{1,0:T(8,128)(2,1)S(1)}, u32[]{:S(2)}, u32[]{:S(2)}) collective-permute-start(bf16[144,128]{1,0:T(8,128)(2,1)S(1)} %get-tuple-element.10), channel_id=1, source_target_pairs={{0,9},{1,8},{2,11},{3,10},{4,13},{5,12},{6,15},{7,14},{8,17},{9,16... | collective-permute-start | bytes 110600 | tf_op jit(solution)/shard_map/ppermute | solution.py:316
  14.1 5.5 %collective-permute-start.1 = (bf16[144,128]{1,0:T(8,128)(2,1)S(1)}, bf16[144,128]{1,0:T(8,128)(2,1)S(1)}, u32[]{:S(2)}, u32[]{:S(2)}) collective-permute-start(bf16[144,128]{1,0:T(8,128)(2,1)S(1)} %get-tuple-element.11), channel_id=1, source_target_pairs={{0,17},{1,16},{2,19},{3,18},{4,21},{5,20},{6,23},{7,22},{8,25},{9,... | collective-permute-start | bytes 110600 | tf_op jit(solution)/shard_map/ppermute | solution.py:316
  17.0 3.8 %collective-permute-start.2 = (bf16[144,128]{1,0:T(8,128)(2,1)S(1)}, bf16[144,128]{1,0:T(8,128)(2,1)S(1)}, u32[]{:S(2)}, u32[]{:S(2)}) collective-permute-start(bf16[144,128]{1,0:T(8,128)(2,1)S(1)} %get-tuple-element.12), channel_id=1, source_target_pairs={{0,25},{1,24},{2,27},{3,26},{4,29},{5,28},{6,31},{7,30},{8,1},{9,0... | collective-permute-start | bytes 110600 | tf_op jit(solution)/shard_map/ppermute | solution.py:316
  20.9 4.2 %collective-permute-start.4 = (bf16[272,128]{1,0:T(8,128)(2,1)S(1)}, bf16[272,128]{1,0:T(8,128)(2,1)S(1)}, u32[]{:S(2)}, u32[]{:S(2)}) collective-permute-start(bf16[272,128]{1,0:T(8,128)(2,1)S(1)} %concatenate.6.refs_0_), channel_id=1, source_target_pairs={{0,3},{1,2},{2,1},{3,0},{4,7},{5,6},{6,5},{7,4},{8,11},{9,10},{10,... | collective-permute-start | bytes 208904 | tf_op jit(solution)/shard_map/ppermute | solution.py:304
  22.3 4.9 %collective-permute-start.8 = (bf16[272,128]{1,0:T(8,128)(2,1)S(1)}, bf16[272,128]{1,0:T(8,128)(2,1)S(1)}, u32[]{:S(2)}, u32[]{:S(2)}) collective-permute-start(bf16[272,128]{1,0:T(8,128)(2,1)S(1)} %concatenate.7), channel_id=1, source_target_pairs={{0,7},{1,6},{2,5},{3,4},{4,3},{5,2},{6,1},{7,0},{8,15},{9,14},{10,... | collective-permute-start | bytes 208904 | tf_op jit(solution)/shard_map/ppermute | solution.py:304
  23.9 4.2 %collective-permute-start.6 = (bf16[272,128]{1,0:T(8,128)(2,1)S(1)}, bf16[272,128]{1,0:T(8,128)(2,1)S(1)}, u32[]{:S(2)}, u32[]{:S(2)}) collective-permute-start(bf16[272,128]{1,0:T(8,128)(2,1)S(1)} %concatenate.7), channel_id=1, source_target_pairs={{0,5},{1,4},{2,7},{3,6},{4,1},{5,0},{6,3},{7,2},{8,13},{9,12},{10,... | collective-permute-start | bytes 208904 | tf_op jit(solution)/shard_map/ppermute | solution.py:304
  24.1 4.1 %collective-permute-start.3 = (bf16[272,128]{1,0:T(8,128)(2,1)S(1)}, bf16[272,128]{1,0:T(8,128)(2,1)S(1)}, u32[]{:S(2)}, u32[]{:S(2)}) collective-permute-start(bf16[272,128]{1,0:T(8,128)(2,1)S(1)} %concatenate.6.refs_0_), channel_id=1, source_target_pairs={{0,1},{1,0},{2,3},{3,2},{4,5},{5,4},{6,7},{7,6},{8,9},{9,8},{10,11... | collective-permute-start | bytes 208904 | tf_op jit(solution)/shard_map/ppermute | solution.py:304
  25.2 3.0 %collective-permute-start.5 = (bf16[272,128]{1,0:T(8,128)(2,1)S(1)}, bf16[272,128]{1,0:T(8,128)(2,1)S(1)}, u32[]{:S(2)}, u32[]{:S(2)}) collective-permute-start(bf16[272,128]{1,0:T(8,128)(2,1)S(1)} %collective-permute-done.4.refs_3_), channel_id=1, source_target_pairs={{0,1},{1,0},{2,3},{3,2},{4,5},{5,4},{6,7},{7,6},{8,9},{9,8},{10,11... | collective-permute-start | bytes 208904 | tf_op jit(solution)/shard_map/ppermute | solution.py:304
  27.2 1.3 %collective-permute-start.9 = (bf16[272,128]{1,0:T(8,128)(2,1)S(1)}, bf16[272,128]{1,0:T(8,128)(2,1)S(1)}, u32[]{:S(2)}, u32[]{:S(2)}) collective-permute-start(bf16[272,128]{1,0:T(8,128)(2,1)S(1)} %collective-permute-done.8.refs_7_), channel_id=1, source_target_pairs={{0,1},{1,0},{2,3},{3,2},{4,5},{5,4},{6,7},{7,6},{8,9},{9,8},{10,11... | collective-permute-start | bytes 208904 | tf_op jit(solution)/shard_map/ppermute | solution.py:304
  28.1 1.3 %collective-permute-start.7 = (bf16[272,128]{1,0:T(8,128)(2,1)S(1)}, bf16[272,128]{1,0:T(8,128)(2,1)S(1)}, u32[]{:S(2)}, u32[]{:S(2)}) collective-permute-start(bf16[272,128]{1,0:T(8,128)(2,1)S(1)} %collective-permute-done.6.refs_5_), channel_id=1, source_target_pairs={{0,1},{1,0},{2,3},{3,2},{4,5},{5,4},{6,7},{7,6},{8,9},{9,8},{10,11... | collective-permute-start | bytes 208904 | tf_op jit(solution)/shard_map/ppermute | solution.py:304

commit v10 on v9

--- a/solution.py
+++ b/solution.py
@@ -314,11 +314,16 @@
                 to = (z + k) % len(parts)
                 route.append((z * plane + i, to * plane + (i ^ 1)))
         arrived[k] = lax.ppermute(parts[k], ("freq",) + across, route)
-    rows = [arrived[k] for k in ORDER]
     half = (parts[0].shape[0] - 16) // 2
-    keep = [block[:half] for block in rows] + [block[2 * half : 2 * half + 4] for block in rows]
-    send = [block[half : 2 * half] for block in rows] + [block[2 * half + 4 : 2 * half + 8] for block in rows]
-    keep, send = jnp.concatenate(keep), jnp.concatenate(send)
+    count = len(parts)
+    keep = jnp.zeros((count * (half + 4), LANES), jnp.bfloat16)
+    send = jnp.zeros((count * (half + 4), LANES), jnp.bfloat16)
+    for place, k in enumerate(ORDER):
+        block, last = arrived[k], count * half + 4 * place
+        keep = lax.dynamic_update_slice(keep, block[:half], (place * half, 0))
+        keep = lax.dynamic_update_slice(keep, block[2 * half : 2 * half + 4], (last, 0))
+        send = lax.dynamic_update_slice(send, block[half : 2 * half], (place * half, 0))
+        send = lax.dynamic_update_slice(send, block[2 * half + 4 : 2 * half + 8], (last, 0))
     corner = swapped(send, across, n_bl + 3)
     beside = swapped(send, across, n_bl + 1)
     far = swapped(keep, across, 3)

time: 31.4 us -> 31.3 us (level)
  transfers between devices with their start and end apart: 10 -> 10, of which waited for: 7 -> 6; matrix products, arithmetic and copies ran while one was open for 0% -> 0% of each run, Pallas kernels for 0% -> 0%
where the time goes in v10:
time: 31.3 us; the launch traced here: 31.1 us
  Pallas kernels  13.5 us (43%)
  starting transfers between devices  10.5 us (34%)
  waiting for transfers between devices  6.95 us (22%)
    pallas_call x1, Pallas kernels, channelize(): pl.pallas_call(functools.partial(channelize_kernel, chans, relative, mesh...  11.6 us
    ppermute x3, starting transfers between devices, exchange(): arrived[k] = lax.ppermute(parts[k], ('freq',) + across, route)  6.17 us
    ppermute x7, starting transfers between devices, swapped(): return lax.ppermute(block, axes, [(i, i ^ distance) for i in range(count)])  4.34 us
    ppermute x7, waiting for transfers between devices, swapped(): return lax.ppermute(block, axes, [(i, i ^ distance) for i in range(count)])  4.02 us
    ppermute x3, waiting for transfers between devices, exchange(): arrived[k] = lax.ppermute(parts[k], ('freq',) + across, route)  2.93 us
    pallas_call x1, Pallas kernels, correlate(): pl.pallas_call(functools.partial(correlate_kernel, mesh_shape, in_dev, fr...  1.93 us
  transfers between devices with their start and end apart: 10, of which 6 were waited for; matrix products, arithmetic and copies ran while one was open for 0% of the time, Pallas kernels for 0%

profile of v10, /device:TPU:0, one launch (start us, length us, event | category | flops | bytes accessed | tf_op | source)
XLA Modules:
  0.0 31.1 jit_solution(15634166194400297961)
XLA Ops:
  0.0 11.6 %channelize.1 = (bf16[144,128]{1,0:T(8,128)(2,1)S(1)}, bf16[144,128]{1,0:T(8,128)(2,1)S(1)}, bf16[144,128]{1,0:T(8,128)(2,1)S(1)}, bf16[144,128]{1,0:T(8,128)(2,1)S(1)}) custom-call(s32[8]{0:T(128)} %chan_hbm.1, s32[64,64,2048]{2,1,0:T(8,128)} %x_ref.1), custom_call_target="tpu_custom_call" | custom-call | tf_op jit(solution)/shard_map/channelize/pallas_call | solution.py:155
  11.6 2.5 %collective-permute-start = (bf16[144,128]{1,0:T(8,128)(2,1)S(1)}, bf16[144,128]{1,0:T(8,128)(2,1)S(1)}, u32[]{:S(2)}, u32[]{:S(2)}) collective-permute-start(bf16[144,128]{1,0:T(8,128)(2,1)S(1)} %get-tuple-element.10), channel_id=1, source_target_pairs={{0,9},{1,8},{2,11},{3,10},{4,13},{5,12},{6,15},{7,14},{8,17},{9,16... | collective-permute-start | bytes 110600 | tf_op jit(solution)/shard_map/ppermute | solution.py:316
  14.1 2.9 %collective-permute-start.1 = (bf16[144,128]{1,0:T(8,128)(2,1)S(1)}, bf16[144,128]{1,0:T(8,128)(2,1)S(1)}, u32[]{:S(2)}, u32[]{:S(2)}) collective-permute-start(bf16[144,128]{1,0:T(8,128)(2,1)S(1)} %get-tuple-element.11), channel_id=1, source_target_pairs={{0,17},{1,16},{2,19},{3,18},{4,21},{5,20},{6,23},{7,22},{8,25},{9,... | collective-permute-start | bytes 110600 | tf_op jit(solution)/shard_map/ppermute | solution.py:316
  17.0 0.8 %collective-permute-start.2 = (bf16[144,128]{1,0:T(8,128)(2,1)S(1)}, bf16[144,128]{1,0:T(8,128)(2,1)S(1)}, u32[]{:S(2)}, u32[]{:S(2)}) collective-permute-start(bf16[144,128]{1,0:T(8,128)(2,1)S(1)} %get-tuple-element.12), channel_id=1, source_target_pairs={{0,25},{1,24},{2,27},{3,26},{4,29},{5,28},{6,31},{7,30},{8,1},{9,0... | collective-permute-start | bytes 110600 | tf_op jit(solution)/shard_map/ppermute | solution.py:316
  17.8 0.0 collective-permute-done
  17.9 1.7 %collective-permute-done.1 = bf16[144,128]{1,0:T(8,128)(2,1)S(1)} collective-permute-done((bf16[144,128]{1,0:T(8,128)(2,1)S(1)}, bf16[144,128]{1,0:T(8,128)(2,1)S(1)}, u32[]{:S(2)}, u32[]{:S(2)}) %collective-permute-start.1) | collective-permute-done | bytes 36896 | tf_op jit(solution)/shard_map/ppermute | solution.py:316
  19.6 1.2 %collective-permute-done.2 = bf16[144,128]{1,0:T(8,128)(2,1)S(1)} collective-permute-done((bf16[144,128]{1,0:T(8,128)(2,1)S(1)}, bf16[144,128]{1,0:T(8,128)(2,1)S(1)}, u32[]{:S(2)}, u32[]{:S(2)}) %collective-permute-start.2) | collective-permute-done | bytes 36896 | tf_op jit(solution)/shard_map/ppermute | solution.py:316
  20.8 2.2 %collective-permute-start.8 = (bf16[272,128]{1,0:T(8,128)(2,1)S(1)}, bf16[272,128]{1,0:T(8,128)(2,1)S(1)}, u32[]{:S(2)}, u32[]{:S(2)}) collective-permute-start(bf16[272,128]{1,0:T(8,128)(2,1)S(1)} %get-tuple-element.13), channel_id=1, source_target_pairs={{0,7},{1,6},{2,5},{3,4},{4,3},{5,2},{6,1},{7,0},{8,15},{9,14},{10,... | collective-permute-start | bytes 208904 | tf_op jit(solution)/shard_map/ppermute | solution.py:304
  23.1 0.6 %collective-permute-start.6 = (bf16[272,128]{1,0:T(8,128)(2,1)S(1)}, bf16[272,128]{1,0:T(8,128)(2,1)S(1)}, u32[]{:S(2)}, u32[]{:S(2)}) collective-permute-start(bf16[272,128]{1,0:T(8,128)(2,1)S(1)} %get-tuple-element.13), channel_id=1, source_target_pairs={{0,5},{1,4},{2,7},{3,6},{4,1},{5,0},{6,3},{7,2},{8,13},{9,12},{10,... | collective-permute-start | bytes 208904 | tf_op jit(solution)/shard_map/ppermute | solution.py:304
  23.6 0.2 collective-permute-start.4
  23.8 0.4 %collective-permute-start.3 = (bf16[272,128]{1,0:T(8,128)(2,1)S(1)}, bf16[272,128]{1,0:T(8,128)(2,1)S(1)}, u32[]{:S(2)}, u32[]{:S(2)}) collective-permute-start(bf16[272,128]{1,0:T(8,128)(2,1)S(1)} %get-tuple-element.14.refs_0_), channel_id=1, source_target_pairs={{0,1},{1,0},{2,3},{3,2},{4,5},{5,4},{6,7},{7,6},{8,9},{9,8},{10,11... | collective-permute-start | bytes 208904 | tf_op jit(solution)/shard_map/ppermute | solution.py:304
  24.3 1.7 %collective-permute-done.8.refs_7_ = bf16[272,128]{1,0:T(8,128)(2,1)S(1)} collective-permute-done((bf16[272,128]{1,0:T(8,128)(2,1)S(1)}, bf16[272,128]{1,0:T(8,128)(2,1)S(1)}, u32[]{:S(2)}, u32[]{:S(2)}) %collective-permute-start.8) | collective-permute-done | bytes 69664 | tf_op jit(solution)/shard_map/ppermute | solution.py:304
  26.0 0.4 %collective-permute-start.9 = (bf16[272,128]{1,0:T(8,128)(2,1)S(1)}, bf16[272,128]{1,0:T(8,128)(2,1)S(1)}, u32[]{:S(2)}, u32[]{:S(2)}) collective-permute-start(bf16[272,128]{1,0:T(8,128)(2,1)S(1)} %collective-permute-done.8.refs_7_), channel_id=1, source_target_pairs={{0,1},{1,0},{2,3},{3,2},{4,5},{5,4},{6,7},{7,6},{8,9},{9,8},{10,11... | collective-permute-start | bytes 208904 | tf_op jit(solution)/shard_map/ppermute | solution.py:304
  26.4 1.1 %collective-permute-done.6.refs_5_ = bf16[272,128]{1,0:T(8,128)(2,1)S(1)} collective-permute-done((bf16[272,128]{1,0:T(8,128)(2,1)S(1)}, bf16[272,128]{1,0:T(8,128)(2,1)S(1)}, u32[]{:S(2)}, u32[]{:S(2)}) %collective-permute-start.6) | collective-permute-done | bytes 69664 | tf_op jit(solution)/shard_map/ppermute | solution.py:304
  27.5 0.5 %collective-permute-start.7 = (bf16[272,128]{1,0:T(8,128)(2,1)S(1)}, bf16[272,128]{1,0:T(8,128)(2,1)S(1)}, u32[]{:S(2)}, u32[]{:S(2)}) collective-permute-start(bf16[272,128]{1,0:T(8,128)(2,1)S(1)} %collective-permute-done.6.refs_5_), channel_id=1, source_target_pairs={{0,1},{1,0},{2,3},{3,2},{4,5},{5,4},{6,7},{7,6},{8,9},{9,8},{10,11... | collective-permute-start | bytes 208904 | tf_op jit(solution)/shard_map/ppermute | solution.py:304
  27.9 0.0 collective-permute-done.4.refs_3_
  27.9 0.1 collective-permute-start.5
  28.0 0.0 collective-permute-done.3.refs_1_
  28.0 0.0 collective-permute-done.9.refs_6_
  28.0 0.8 %collective-permute-done.7.refs_4_ = bf16[272,128]{1,0:T(8,128)(2,1)S(1)} collective-permute-done((bf16[272,128]{1,0:T(8,128)(2,1)S(1)}, bf16[272,128]{1,0:T(8,128)(2,1)S(1)}, u32[]{:S(2)}, u32[]{:S(2)}) %collective-permute-start.7) | collective-permute-done | bytes 69664 | tf_op jit(solution)/shard_map/ppermute | solution.py:304
  28.9 0.4 %collective-permute-done.5.refs_2_ = bf16[272,128]{1,0:T(8,128)(2,1)S(1)} collective-permute-done((bf16[272,128]{1,0:T(8,128)(2,1)S(1)}, bf16[272,128]{1,0:T(8,128)(2,1)S(1)}, u32[]{:S(2)}, u32[]{:S(2)}) %collective-permute-start.5) | collective-permute-done | bytes 69664 | tf_op jit(solution)/shard_map/ppermute | solution.py:304
  29.2 1.9 %correlate.1 = f32[1,1,2,512,512]{4,3,2,1,0:T(8,128)} custom-call(bf16[272,128]{1,0:T(8,128)(2,1)S(1)} %get-tuple-element.14.refs_0_, bf16[272,128]{1,0:T(8,128)(2,1)S(1)} %collective-permute-done.3.refs_1_, bf16[272,128]{1,0:T(8,128)(2,1)S(1)} %collective-permute-done.5.refs_2_, bf16[272,128]{1,0:T(8,128)(2,1)S(1)} %collective-permute-done.4.refs_3_, ...), custom_call_target="tpu_custom_call" | custom-call | tf_op jit(solution)/shard_map/correlate/pallas_call | solution.py:262
  (10 shorter events, 0.1 us)
Async XLA Ops:
  11.6 6.2 %collective-permute-start = (bf16[144,128]{1,0:T(8,128)(2,1)S(1)}, bf16[144,128]{1,0:T(8,128)(2,1)S(1)}, u32[]{:S(2)}, u32[]{:S(2)}) collective-permute-start(bf16[144,128]{1,0:T(8,128)(2,1)S(1)} %get-tuple-element.10), channel_id=1, source_target_pairs={{0,9},{1,8},{2,11},{3,10},{4,13},{5,12},{6,15},{7,14},{8,17},{9,16... | collective-permute-start | bytes 110600 | tf_op jit(solution)/shard_map/ppermute | solution.py:316
  14.1 5.5 %collective-permute-start.1 = (bf16[144,128]{1,0:T(8,128)(2,1)S(1)}, bf16[144,128]{1,0:T(8,128)(2,1)S(1)}, u32[]{:S(2)}, u32[]{:S(2)}) collective-permute-start(bf16[144,128]{1,0:T(8,128)(2,1)S(1)} %get-tuple-element.11), channel_id=1, source_target_pairs={{0,17},{1,16},{2,19},{3,18},{4,21},{5,20},{6,23},{7,22},{8,25},{9,... | collective-permute-start | bytes 110600 | tf_op jit(solution)/shard_map/ppermute | solution.py:316
  17.0 3.8 %collective-permute-start.2 = (bf16[144,128]{1,0:T(8,128)(2,1)S(1)}, bf16[144,128]{1,0:T(8,128)(2,1)S(1)}, u32[]{:S(2)}, u32[]{:S(2)}) collective-permute-start(bf16[144,128]{1,0:T(8,128)(2,1)S(1)} %get-tuple-element.12), channel_id=1, source_target_pairs={{0,25},{1,24},{2,27},{3,26},{4,29},{5,28},{6,31},{7,30},{8,1},{9,0... | collective-permute-start | bytes 110600 | tf_op jit(solution)/shard_map/ppermute | solution.py:316
  20.8 5.1 %collective-permute-start.8 = (bf16[272,128]{1,0:T(8,128)(2,1)S(1)}, bf16[272,128]{1,0:T(8,128)(2,1)S(1)}, u32[]{:S(2)}, u32[]{:S(2)}) collective-permute-start(bf16[272,128]{1,0:T(8,128)(2,1)S(1)} %get-tuple-element.13), channel_id=1, source_target_pairs={{0,7},{1,6},{2,5},{3,4},{4,3},{5,2},{6,1},{7,0},{8,15},{9,14},{10,... | collective-permute-start | bytes 208904 | tf_op jit(solution)/shard_map/ppermute | solution.py:304
  23.1 4.4 %collective-permute-start.6 = (bf16[272,128]{1,0:T(8,128)(2,1)S(1)}, bf16[272,128]{1,0:T(8,128)(2,1)S(1)}, u32[]{:S(2)}, u32[]{:S(2)}) collective-permute-start(bf16[272,128]{1,0:T(8,128)(2,1)S(1)} %get-tuple-element.13), channel_id=1, source_target_pairs={{0,5},{1,4},{2,7},{3,6},{4,1},{5,0},{6,3},{7,2},{8,13},{9,12},{10,... | collective-permute-start | bytes 208904 | tf_op jit(solution)/shard_map/ppermute | solution.py:304
  23.6 4.3 %collective-permute-start.4 = (bf16[272,128]{1,0:T(8,128)(2,1)S(1)}, bf16[272,128]{1,0:T(8,128)(2,1)S(1)}, u32[]{:S(2)}, u32[]{:S(2)}) collective-permute-start(bf16[272,128]{1,0:T(8,128)(2,1)S(1)} %get-tuple-element.14.refs_0_), channel_id=1, source_target_pairs={{0,3},{1,2},{2,1},{3,0},{4,7},{5,6},{6,5},{7,4},{8,11},{9,10},{10,... | collective-permute-start | bytes 208904 | tf_op jit(solution)/shard_map/ppermute | solution.py:304
  23.8 4.2 %collective-permute-start.3 = (bf16[272,128]{1,0:T(8,128)(2,1)S(1)}, bf16[272,128]{1,0:T(8,128)(2,1)S(1)}, u32[]{:S(2)}, u32[]{:S(2)}) collective-permute-start(bf16[272,128]{1,0:T(8,128)(2,1)S(1)} %get-tuple-element.14.refs_0_), channel_id=1, source_target_pairs={{0,1},{1,0},{2,3},{3,2},{4,5},{5,4},{6,7},{7,6},{8,9},{9,8},{10,11... | collective-permute-start | bytes 208904 | tf_op jit(solution)/shard_map/ppermute | solution.py:304
  26.0 2.0 %collective-permute-start.9 = (bf16[272,128]{1,0:T(8,128)(2,1)S(1)}, bf16[272,128]{1,0:T(8,128)(2,1)S(1)}, u32[]{:S(2)}, u32[]{:S(2)}) collective-permute-start(bf16[272,128]{1,0:T(8,128)(2,1)S(1)} %collective-permute-done.8.refs_7_), channel_id=1, source_target_pairs={{0,1},{1,0},{2,3},{3,2},{4,5},{5,4},{6,7},{7,6},{8,9},{9,8},{10,11... | collective-permute-start | bytes 208904 | tf_op jit(solution)/shard_map/ppermute | solution.py:304
  27.5 1.4 %collective-permute-start.7 = (bf16[272,128]{1,0:T(8,128)(2,1)S(1)}, bf16[272,128]{1,0:T(8,128)(2,1)S(1)}, u32[]{:S(2)}, u32[]{:S(2)}) collective-permute-start(bf16[272,128]{1,0:T(8,128)(2,1)S(1)} %collective-permute-done.6.refs_5_), channel_id=1, source_target_pairs={{0,1},{1,0},{2,3},{3,2},{4,5},{5,4},{6,7},{7,6},{8,9},{9,8},{10,11... | collective-permute-start | bytes 208904 | tf_op jit(solution)/shard_map/ppermute | solution.py:304
  27.9 1.3 %collective-permute-start.5 = (bf16[272,128]{1,0:T(8,128)(2,1)S(1)}, bf16[272,128]{1,0:T(8,128)(2,1)S(1)}, u32[]{:S(2)}, u32[]{:S(2)}) collective-permute-start(bf16[272,128]{1,0:T(8,128)(2,1)S(1)} %collective-permute-done.4.refs_3_), channel_id=1, source_target_pairs={{0,1},{1,0},{2,3},{3,2},{4,5},{5,4},{6,7},{7,6},{8,9},{9,8},{10,11... | collective-permute-start | bytes 208904 | tf_op jit(solution)/shard_map/ppermute | solution.py:304

commit v11 on v10

--- a/solution.py
+++ b/solution.py
@@ -15,6 +15,7 @@
 PIECES = 2
 NARROW = jnp.bfloat16
 ORDER = (0, 1, 2, 3)
+SEATS = (5, 4, 7, 6, 3, 2, 0, 1)
 
 
 def bin_column(chan_ref, chans):
@@ -206,50 +207,56 @@
 
 def correlate_kernel(mesh_shape, in_dev, fr_dev, *refs):
     n_freq, n_tm, n_bl = mesh_shape
-    own_half, other_half = refs[:n_bl], refs[n_bl : 2 * n_bl]
-    o_ref, left, right, result, edges, sems = refs[2 * n_bl :]
+    seated = [refs[SEATS.index(i)] for i in range(2 * n_bl)]
+    own_half, other_half = seated[:n_bl], seated[n_bl:]
+    o_ref, right, result, edges, sems = refs[2 * n_bl :]
     for i in range(2 * n_bl):
-        edges[i] = refs[i][n_freq * in_dev :, :].astype(jnp.float32)
+        edges[i] = seated[i][n_freq * in_dev :, :].astype(jnp.float32)
     freq, tm, bl = (lax.axis_index(axis) for axis in ("freq", "tm", "bl"))
     scale = 1.0 / (n_tm * fr_dev)
-    order = [(f, k) for f in range(n_freq // 2) for k in range(n_bl)]
-    for out, base in ((left, bl // 2 * (n_freq // 2)), (right, bl % 2 * (n_freq // 2))):
-        early, late, carried, core = [], [], [], []
-        for f, k in order:
-            at = place_of((freq - base - f + n_freq) % n_freq)
+    half, per = right.shape[0], right.shape[0] // (n_freq // 2)
+
+    def gather(f, base):
+        at = place_of((freq - base - f + n_freq) % n_freq)
+        core = jnp.where(at == 0, 0, 1)
+        body = pl.ds(pl.multiple_of(at * in_dev, in_dev), in_dev)
+        early, late, carried, places = [], [], [], []
+        for k in range(n_bl):
             mine, other = own_half[k], other_half[k]
-            core.append(jnp.where(at == 0, 0, 1))
-            body = pl.ds(pl.multiple_of(at * in_dev, in_dev), in_dev)
             early.append(jnp.where(tm == 0, mine[body, :], other[body, :]))
             late.append(jnp.where(tm == 0, other[body, :], mine[body, :]))
             giver = jnp.where(tm == 0, k, n_bl + k)
             carried.append([edges[giver, pl.ds(at * 4 + r, 1), :] for r in range(4)])
+            places.append(pl.multiple_of(f * per + (bl ^ k ^ core) * in_dev, in_dev))
         late = jnp.concatenate(late, axis=0).astype(jnp.float32)
         late = (late + place_carry(carried, in_dev, fr_dev)).astype(jnp.bfloat16)
-        for m, (f, k) in enumerate(order):
-            at = pl.multiple_of((f * n_bl + (bl ^ k ^ core[m])) * in_dev, in_dev)
-            out[pl.ds(at, in_dev), :LANES] = early[m]
-            out[pl.ds(at, in_dev), LANES:] = late[m * in_dev : (m + 1) * in_dev]
-    half = left.shape[0]
-    count = sems.shape[0] // 2
-    rows = half // count
-    lane = lax.broadcasted_iota(jnp.int32, (rows, LANES), 1)
+        return jnp.concatenate(early, axis=0), late, places
+
+    for f in range(n_freq // 2):
+        early, late, places = gather(f, bl % 2 * (n_freq // 2))
+        for k, at in enumerate(places):
+            right[pl.ds(at, in_dev), :LANES] = early[k * in_dev : (k + 1) * in_dev]
+            right[pl.ds(at, in_dev), LANES:] = late[k * in_dev : (k + 1) * in_dev]
+    lane = lax.broadcasted_iota(jnp.int32, (per, LANES), 1)
     dims = (((1,), (1,)), ((), ()))
     copies = []
-    for m in range(count):
-        span = pl.ds(m * rows, rows)
-        mine = left[m * rows : (m + 1) * rows, :]
+    for f in range(n_freq // 2):
+        early, late, places = gather(f, bl // 2 * (n_freq // 2))
         turned = []
-        for t in range(n_tm):
-            part = mine[:, t * LANES : (t + 1) * LANES].astype(jnp.float32)
-            part = pltpu.roll(part, fr_dev, 1)
+        for part in (early, late):
+            part = pltpu.roll(part.astype(jnp.float32), fr_dev, 1)
             turned.append(jnp.where(lane < fr_dev, part, -part).astype(jnp.bfloat16))
-        for p, a in enumerate((mine, jnp.concatenate(turned, axis=1))):
-            result[p, m * rows : (m + 1) * rows, :] = scale * lax.dot_general(
-                a, right[...], dims, preferred_element_type=jnp.float32
+        for p, a in enumerate(((early, late), turned)):
+            product = scale * lax.dot_general(
+                jnp.concatenate(a, axis=1), right[...], dims, preferred_element_type=jnp.float32
             )
+            for k, at in enumerate(places):
+                result[p, pl.ds(at, in_dev), :] = product[k * in_dev : (k + 1) * in_dev]
+            span = pl.ds(f * per, per)
             copies.append(
-                pltpu.make_async_copy(result.at[p, span], o_ref.at[0, 0, p, span], sems.at[2 * m + p])
+                pltpu.make_async_copy(
+                    result.at[p, span], o_ref.at[0, 0, p, span], sems.at[2 * f + p]
+                )
             )
             copies[-1].start()
     for copy in copies:
@@ -266,10 +273,9 @@
         out_shape=jax.ShapeDtypeStruct((1, 1, 2, half, half), jnp.float32),
         scratch_shapes=[
             pltpu.VMEM((half, n_tm * LANES), jnp.bfloat16),
-            pltpu.VMEM((half, n_tm * LANES), jnp.bfloat16),
             pltpu.VMEM((2, half, half), jnp.float32),
             pltpu.VMEM((len(sources), 4 * n_freq, LANES), jnp.float32),
-            pltpu.SemaphoreType.DMA((4,)),
+            pltpu.SemaphoreType.DMA((n_freq,)),
         ],
         compiler_params=pltpu.CompilerParams(vmem_limit_bytes=16 * 2**20),
         name="correlate",
@@ -330,7 +336,8 @@
     turn = lambda block: swapped(block, ("bl",), 1)
     own_half = [keep, turn(keep), turn(far), far]
     other_half = [turn(beside), beside, turn(corner), corner]
-    return own_half + other_half
+    both = own_half + other_half
+    return [both[i] for i in SEATS]
 
 
 def on_device(samples, chan_index):

time: 31.3 us -> 31.2 us (level)
  no operation moved by 1% of the time
where the time goes in v11:
time: 31.2 us; the launch traced here: 31.1 us
  Pallas kernels  13.5 us (43%)
  starting transfers between devices  10.5 us (34%)
  waiting for transfers between devices  6.95 us (22%)
    pallas_call x1, Pallas kernels, channelize(): pl.pallas_call(functools.partial(channelize_kernel, chans, relative, mesh...  11.6 us
    ppermute x3, starting transfers between devices, exchange(): arrived[k] = lax.ppermute(parts[k], ('freq',) + across, route)  6.17 us
    ppermute x7, starting transfers between devices, swapped(): return lax.ppermute(block, axes, [(i, i ^ distance) for i in range(count)])  4.34 us
    ppermute x7, waiting for transfers between devices, swapped(): return lax.ppermute(block, axes, [(i, i ^ distance) for i in range(count)])  4.02 us
    ppermute x3, waiting for transfers between devices, exchange(): arrived[k] = lax.ppermute(parts[k], ('freq',) + across, route)  2.93 us
    pallas_call x1, Pallas kernels, correlate(): pl.pallas_call(functools.partial(correlate_kernel, mesh_shape, in_dev, fr...  1.9 us
  transfers between devices with their start and end apart: 10, of which 6 were waited for; matrix products, arithmetic and copies ran while one was open for 0% of the time, Pallas kernels for 0%

profile of v11, /device:TPU:0, one launch (start us, length us, event | category | flops | bytes accessed | tf_op | source)
XLA Modules:
  0.0 31.1 jit_solution(15966165191546900593)
XLA Ops:
  0.0 11.6 %channelize.1 = (bf16[144,128]{1,0:T(8,128)(2,1)S(1)}, bf16[144,128]{1,0:T(8,128)(2,1)S(1)}, bf16[144,128]{1,0:T(8,128)(2,1)S(1)}, bf16[144,128]{1,0:T(8,128)(2,1)S(1)}) custom-call(s32[8]{0:T(128)} %chan_hbm.1, s32[64,64,2048]{2,1,0:T(8,128)} %x_ref.1), custom_call_target="tpu_custom_call" | custom-call | tf_op jit(solution)/shard_map/channelize/pallas_call | solution.py:156
  11.6 2.5 %collective-permute-start = (bf16[144,128]{1,0:T(8,128)(2,1)S(1)}, bf16[144,128]{1,0:T(8,128)(2,1)S(1)}, u32[]{:S(2)}, u32[]{:S(2)}) collective-permute-start(bf16[144,128]{1,0:T(8,128)(2,1)S(1)} %get-tuple-element.10), channel_id=1, source_target_pairs={{0,9},{1,8},{2,11},{3,10},{4,13},{5,12},{6,15},{7,14},{8,17},{9,16... | collective-permute-start | bytes 110600 | tf_op jit(solution)/shard_map/ppermute | solution.py:322
  14.1 2.9 %collective-permute-start.1 = (bf16[144,128]{1,0:T(8,128)(2,1)S(1)}, bf16[144,128]{1,0:T(8,128)(2,1)S(1)}, u32[]{:S(2)}, u32[]{:S(2)}) collective-permute-start(bf16[144,128]{1,0:T(8,128)(2,1)S(1)} %get-tuple-element.11), channel_id=1, source_target_pairs={{0,17},{1,16},{2,19},{3,18},{4,21},{5,20},{6,23},{7,22},{8,25},{9,... | collective-permute-start | bytes 110600 | tf_op jit(solution)/shard_map/ppermute | solution.py:322
  17.0 0.8 %collective-permute-start.2 = (bf16[144,128]{1,0:T(8,128)(2,1)S(1)}, bf16[144,128]{1,0:T(8,128)(2,1)S(1)}, u32[]{:S(2)}, u32[]{:S(2)}) collective-permute-start(bf16[144,128]{1,0:T(8,128)(2,1)S(1)} %get-tuple-element.12), channel_id=1, source_target_pairs={{0,25},{1,24},{2,27},{3,26},{4,29},{5,28},{6,31},{7,30},{8,1},{9,0... | collective-permute-start | bytes 110600 | tf_op jit(solution)/shard_map/ppermute | solution.py:322
  17.8 0.0 collective-permute-done
  17.9 1.7 %collective-permute-done.1 = bf16[144,128]{1,0:T(8,128)(2,1)S(1)} collective-permute-done((bf16[144,128]{1,0:T(8,128)(2,1)S(1)}, bf16[144,128]{1,0:T(8,128)(2,1)S(1)}, u32[]{:S(2)}, u32[]{:S(2)}) %collective-permute-start.1) | collective-permute-done | bytes 36896 | tf_op jit(solution)/shard_map/ppermute | solution.py:322
  19.6 1.2 %collective-permute-done.2 = bf16[144,128]{1,0:T(8,128)(2,1)S(1)} collective-permute-done((bf16[144,128]{1,0:T(8,128)(2,1)S(1)}, bf16[144,128]{1,0:T(8,128)(2,1)S(1)}, u32[]{:S(2)}, u32[]{:S(2)}) %collective-permute-start.2) | collective-permute-done | bytes 36896 | tf_op jit(solution)/shard_map/ppermute | solution.py:322
  20.8 2.2 %collective-permute-start.5 = (bf16[272,128]{1,0:T(8,128)(2,1)S(1)}, bf16[272,128]{1,0:T(8,128)(2,1)S(1)}, u32[]{:S(2)}, u32[]{:S(2)}) collective-permute-start(bf16[272,128]{1,0:T(8,128)(2,1)S(1)} %get-tuple-element.14), channel_id=1, source_target_pairs={{0,7},{1,6},{2,5},{3,4},{4,3},{5,2},{6,1},{7,0},{8,15},{9,14},{10,... | collective-permute-start | bytes 208904 | tf_op jit(solution)/shard_map/ppermute | solution.py:310
  23.1 0.6 %collective-permute-start.3 = (bf16[272,128]{1,0:T(8,128)(2,1)S(1)}, bf16[272,128]{1,0:T(8,128)(2,1)S(1)}, u32[]{:S(2)}, u32[]{:S(2)}) collective-permute-start(bf16[272,128]{1,0:T(8,128)(2,1)S(1)} %get-tuple-element.14), channel_id=1, source_target_pairs={{0,5},{1,4},{2,7},{3,6},{4,1},{5,0},{6,3},{7,2},{8,13},{9,12},{10,... | collective-permute-start | bytes 208904 | tf_op jit(solution)/shard_map/ppermute | solution.py:310
  23.6 0.2 collective-permute-start.7
  23.8 0.4 %collective-permute-start.9 = (bf16[272,128]{1,0:T(8,128)(2,1)S(1)}, bf16[272,128]{1,0:T(8,128)(2,1)S(1)}, u32[]{:S(2)}, u32[]{:S(2)}) collective-permute-start(bf16[272,128]{1,0:T(8,128)(2,1)S(1)} %get-tuple-element.13.refs_6_), channel_id=1, source_target_pairs={{0,1},{1,0},{2,3},{3,2},{4,5},{5,4},{6,7},{7,6},{8,9},{9,8},{10,11... | collective-permute-start | bytes 208904 | tf_op jit(solution)/shard_map/ppermute | solution.py:310
  24.3 1.7 %collective-permute-done.5.refs_2_ = bf16[272,128]{1,0:T(8,128)(2,1)S(1)} collective-permute-done((bf16[272,128]{1,0:T(8,128)(2,1)S(1)}, bf16[272,128]{1,0:T(8,128)(2,1)S(1)}, u32[]{:S(2)}, u32[]{:S(2)}) %collective-permute-start.5) | collective-permute-done | bytes 69664 | tf_op jit(solution)/shard_map/ppermute | solution.py:310
  26.0 0.4 %collective-permute-start.6 = (bf16[272,128]{1,0:T(8,128)(2,1)S(1)}, bf16[272,128]{1,0:T(8,128)(2,1)S(1)}, u32[]{:S(2)}, u32[]{:S(2)}) collective-permute-start(bf16[272,128]{1,0:T(8,128)(2,1)S(1)} %collective-permute-done.5.refs_2_), channel_id=1, source_target_pairs={{0,1},{1,0},{2,3},{3,2},{4,5},{5,4},{6,7},{7,6},{8,9},{9,8},{10,11... | collective-permute-start | bytes 208904 | tf_op jit(solution)/shard_map/ppermute | solution.py:310
  26.4 1.1 %collective-permute-done.3.refs_0_ = bf16[272,128]{1,0:T(8,128)(2,1)S(1)} collective-permute-done((bf16[272,128]{1,0:T(8,128)(2,1)S(1)}, bf16[272,128]{1,0:T(8,128)(2,1)S(1)}, u32[]{:S(2)}, u32[]{:S(2)}) %collective-permute-start.3) | collective-permute-done | bytes 69664 | tf_op jit(solution)/shard_map/ppermute | solution.py:310
  27.5 0.5 %collective-permute-start.4 = (bf16[272,128]{1,0:T(8,128)(2,1)S(1)}, bf16[272,128]{1,0:T(8,128)(2,1)S(1)}, u32[]{:S(2)}, u32[]{:S(2)}) collective-permute-start(bf16[272,128]{1,0:T(8,128)(2,1)S(1)} %collective-permute-done.3.refs_0_), channel_id=1, source_target_pairs={{0,1},{1,0},{2,3},{3,2},{4,5},{5,4},{6,7},{7,6},{8,9},{9,8},{10,11... | collective-permute-start | bytes 208904 | tf_op jit(solution)/shard_map/ppermute | solution.py:310
  27.9 0.0 collective-permute-done.7.refs_4_
  27.9 0.1 collective-permute-start.8
  28.0 0.0 collective-permute-done.9.refs_7_
  28.0 0.0 collective-permute-done.6.refs_3_
  28.0 0.8 %collective-permute-done.4.refs_1_ = bf16[272,128]{1,0:T(8,128)(2,1)S(1)} collective-permute-done((bf16[272,128]{1,0:T(8,128)(2,1)S(1)}, bf16[272,128]{1,0:T(8,128)(2,1)S(1)}, u32[]{:S(2)}, u32[]{:S(2)}) %collective-permute-start.4) | collective-permute-done | bytes 69664 | tf_op jit(solution)/shard_map/ppermute | solution.py:310
  28.9 0.4 %collective-permute-done.8.refs_5_ = bf16[272,128]{1,0:T(8,128)(2,1)S(1)} collective-permute-done((bf16[272,128]{1,0:T(8,128)(2,1)S(1)}, bf16[272,128]{1,0:T(8,128)(2,1)S(1)}, u32[]{:S(2)}, u32[]{:S(2)}) %collective-permute-start.8) | collective-permute-done | bytes 69664 | tf_op jit(solution)/shard_map/ppermute | solution.py:310
  29.2 1.9 %correlate.1 = f32[1,1,2,512,512]{4,3,2,1,0:T(8,128)} custom-call(bf16[272,128]{1,0:T(8,128)(2,1)S(1)} %collective-permute-done.3.refs_0_, bf16[272,128]{1,0:T(8,128)(2,1)S(1)} %collective-permute-done.4.refs_1_, bf16[272,128]{1,0:T(8,128)(2,1)S(1)} %collective-permute-done.5.refs_2_, bf16[272,128]{1,0:T(8,128)(2,1)S(1)} %collective-permute-done.6.refs_3_, ...), custom_call_target="tpu_custom_call" | custom-call | tf_op jit(solution)/shard_map/correlate/pallas_call | solution.py:269
  (10 shorter events, 0.1 us)
Async XLA Ops:
  11.6 6.2 %collective-permute-start = (bf16[144,128]{1,0:T(8,128)(2,1)S(1)}, bf16[144,128]{1,0:T(8,128)(2,1)S(1)}, u32[]{:S(2)}, u32[]{:S(2)}) collective-permute-start(bf16[144,128]{1,0:T(8,128)(2,1)S(1)} %get-tuple-element.10), channel_id=1, source_target_pairs={{0,9},{1,8},{2,11},{3,10},{4,13},{5,12},{6,15},{7,14},{8,17},{9,16... | collective-permute-start | bytes 110600 | tf_op jit(solution)/shard_map/ppermute | solution.py:322
  14.1 5.5 %collective-permute-start.1 = (bf16[144,128]{1,0:T(8,128)(2,1)S(1)}, bf16[144,128]{1,0:T(8,128)(2,1)S(1)}, u32[]{:S(2)}, u32[]{:S(2)}) collective-permute-start(bf16[144,128]{1,0:T(8,128)(2,1)S(1)} %get-tuple-element.11), channel_id=1, source_target_pairs={{0,17},{1,16},{2,19},{3,18},{4,21},{5,20},{6,23},{7,22},{8,25},{9,... | collective-permute-start | bytes 110600 | tf_op jit(solution)/shard_map/ppermute | solution.py:322
  17.0 3.8 %collective-permute-start.2 = (bf16[144,128]{1,0:T(8,128)(2,1)S(1)}, bf16[144,128]{1,0:T(8,128)(2,1)S(1)}, u32[]{:S(2)}, u32[]{:S(2)}) collective-permute-start(bf16[144,128]{1,0:T(8,128)(2,1)S(1)} %get-tuple-element.12), channel_id=1, source_target_pairs={{0,25},{1,24},{2,27},{3,26},{4,29},{5,28},{6,31},{7,30},{8,1},{9,0... | collective-permute-start | bytes 110600 | tf_op jit(solution)/shard_map/ppermute | solution.py:322
  20.8 5.1 %collective-permute-start.5 = (bf16[272,128]{1,0:T(8,128)(2,1)S(1)}, bf16[272,128]{1,0:T(8,128)(2,1)S(1)}, u32[]{:S(2)}, u32[]{:S(2)}) collective-permute-start(bf16[272,128]{1,0:T(8,128)(2,1)S(1)} %get-tuple-element.14), channel_id=1, source_target_pairs={{0,7},{1,6},{2,5},{3,4},{4,3},{5,2},{6,1},{7,0},{8,15},{9,14},{10,... | collective-permute-start | bytes 208904 | tf_op jit(solution)/shard_map/ppermute | solution.py:310
  23.1 4.4 %collective-permute-start.3 = (bf16[272,128]{1,0:T(8,128)(2,1)S(1)}, bf16[272,128]{1,0:T(8,128)(2,1)S(1)}, u32[]{:S(2)}, u32[]{:S(2)}) collective-permute-start(bf16[272,128]{1,0:T(8,128)(2,1)S(1)} %get-tuple-element.14), channel_id=1, source_target_pairs={{0,5},{1,4},{2,7},{3,6},{4,1},{5,0},{6,3},{7,2},{8,13},{9,12},{10,... | collective-permute-start | bytes 208904 | tf_op jit(solution)/shard_map/ppermute | solution.py:310
  23.6 4.3 %collective-permute-start.7 = (bf16[272,128]{1,0:T(8,128)(2,1)S(1)}, bf16[272,128]{1,0:T(8,128)(2,1)S(1)}, u32[]{:S(2)}, u32[]{:S(2)}) collective-permute-start(bf16[272,128]{1,0:T(8,128)(2,1)S(1)} %get-tuple-element.13.refs_6_), channel_id=1, source_target_pairs={{0,3},{1,2},{2,1},{3,0},{4,7},{5,6},{6,5},{7,4},{8,11},{9,10},{10,... | collective-permute-start | bytes 208904 | tf_op jit(solution)/shard_map/ppermute | solution.py:310
  23.8 4.2 %collective-permute-start.9 = (bf16[272,128]{1,0:T(8,128)(2,1)S(1)}, bf16[272,128]{1,0:T(8,128)(2,1)S(1)}, u32[]{:S(2)}, u32[]{:S(2)}) collective-permute-start(bf16[272,128]{1,0:T(8,128)(2,1)S(1)} %get-tuple-element.13.refs_6_), channel_id=1, source_target_pairs={{0,1},{1,0},{2,3},{3,2},{4,5},{5,4},{6,7},{7,6},{8,9},{9,8},{10,11... | collective-permute-start | bytes 208904 | tf_op jit(solution)/shard_map/ppermute | solution.py:310
  26.0 2.0 %collective-permute-start.6 = (bf16[272,128]{1,0:T(8,128)(2,1)S(1)}, bf16[272,128]{1,0:T(8,128)(2,1)S(1)}, u32[]{:S(2)}, u32[]{:S(2)}) collective-permute-start(bf16[272,128]{1,0:T(8,128)(2,1)S(1)} %collective-permute-done.5.refs_2_), channel_id=1, source_target_pairs={{0,1},{1,0},{2,3},{3,2},{4,5},{5,4},{6,7},{7,6},{8,9},{9,8},{10,11... | collective-permute-start | bytes 208904 | tf_op jit(solution)/shard_map/ppermute | solution.py:310
  27.5 1.4 %collective-permute-start.4 = (bf16[272,128]{1,0:T(8,128)(2,1)S(1)}, bf16[272,128]{1,0:T(8,128)(2,1)S(1)}, u32[]{:S(2)}, u32[]{:S(2)}) collective-permute-start(bf16[272,128]{1,0:T(8,128)(2,1)S(1)} %collective-permute-done.3.refs_0_), channel_id=1, source_target_pairs={{0,1},{1,0},{2,3},{3,2},{4,5},{5,4},{6,7},{7,6},{8,9},{9,8},{10,11... | collective-permute-start | bytes 208904 | tf_op jit(solution)/shard_map/ppermute | solution.py:310
  27.9 1.3 %collective-permute-start.8 = (bf16[272,128]{1,0:T(8,128)(2,1)S(1)}, bf16[272,128]{1,0:T(8,128)(2,1)S(1)}, u32[]{:S(2)}, u32[]{:S(2)}) collective-permute-start(bf16[272,128]{1,0:T(8,128)(2,1)S(1)} %collective-permute-done.7.refs_4_), channel_id=1, source_target_pairs={{0,1},{1,0},{2,3},{3,2},{4,5},{5,4},{6,7},{7,6},{8,9},{9,8},{10,11... | collective-permute-start | bytes 208904 | tf_op jit(solution)/shard_map/ppermute | solution.py:310
